TPU v7x, 32 devices: a whole 2x2x4 slice. The times are simulated.
32 devices in a mesh: dp: 4 (over z), row: 4 (over y, x), col: 2 (over core).
Axes of the slice: x: 2, y: 2, z: 4, core: 2. Of those that a mesh axis runs over, the one named last changes fastest.
Arguments:
- hidden: bfloat16 [16, 1024, 2048], P('dp', 'row', 'col'), may hold values from -6 to 6
- targets: bfloat16 [16, 1024, 2048], P('dp', 'row', 'col'), may hold values from -6 to 6
- lengths: int32 [16], replicated, may hold values from 256 to 1024, as said below
- dest_group: int32 [16], P('dp'), may hold values from 0 to 3, as said below
- norm_gain: float32 [2048], P('col'), may hold values from 0.1 to 1.9
- gate_input_weight: bfloat16 [2048, 64, 128], P('col', 'row'), may hold values from -0.125 to 0.125
- auxiliary_weight: bfloat16 [2048, 320], P('col'), may hold values from -0.125 to 0.125
- conv_x: float32 [4, 64, 64], P(None, 'row'), may hold values from -0.5 to 0.5
- conv_x_bias: float32 [64, 64], P('row'), may hold values from -0.5 to 0.5
- conv_bc: float32 [4, 256], replicated, may hold values from -0.5 to 0.5
- conv_bc_bias: float32 [256], replicated, may hold values from -0.5 to 0.5
- dt_bias: float32 [64], P('row'), may hold values from -6 to -2.5
- a_log: float32 [64], P('row'), may hold values from 0 to 2.77
- d_skip: float32 [64], P('row'), may hold values from 0.5 to 1.5
- out_gain: float32 [64, 64], P('row'), may hold values from 0.1 to 1.9
- output_weight: bfloat16 [64, 64, 2048], P('row', None, 'col'), may hold values from -0.09375 to 0.09375
Outputs:
- loss: float32 [], replicated
- output: bfloat16 [16, 1024, 2048], P('dp', 'row', 'col')
- hidden_grad: bfloat16 [16, 1024, 2048], P('dp', 'row', 'col')
- norm_gain_grad: float32 [2048], P('col')
- w_zx_grad: float32 [2048, 64, 128], P('col', 'row')
- w_aux_grad: float32 [2048, 320], P('col')
- conv_x_grad: float32 [4, 64, 64], P(None, 'row')
- conv_x_bias_grad: float32 [64, 64], P('row')
- conv_bc_grad: float32 [4, 256], replicated
- conv_bc_bias_grad: float32 [256], replicated
- dt_bias_grad: float32 [64], P('row')
- a_log_grad: float32 [64], P('row')
- d_skip_grad: float32 [64], P('row')
- out_gain_grad: float32 [64, 64], P('row')
- w_out_grad: float32 [64, 64, 2048], P('row', None, 'col')
Inputs may be any that keep to these rules, and one draw needn't show every extreme that they name: `lengths`: in every block of 4 dealt sequences (one data group) one sequence has length 1024 and one has length 256. `dest_group`: in every block of 4 consecutive sequences of the given order every group number occurs exactly once.
All inputs are finite; a program needn't handle non-finite values.
Results may differ from a plain program's by a relative error of at most 0.0091.
Values may be sent and summed in bfloat16 or wider, within the bound.
No kernel may reach another device: no remote copies, remote signals or barrier semaphores. Data moves between devices by JAX's collectives and lax.ppermute only.
A program may use at most 320 MiB of HBM per device.

v0:
```python
import jax
import jax.numpy as jnp
from jax import lax
from jax.sharding import PartitionSpec as P

CH = 256


EPSILON = 1e-05
HIGHEST = lax.Precision.HIGHEST


def silu_fn(values):
    return values * jax.nn.sigmoid(values)


def causal_conv(values, kernel, offset):
    tap_count = kernel.shape[0]
    seq_length = values.shape[0]
    padded = jnp.pad(values, ((tap_count - 1, 0), (0, 0)))
    summed = jnp.zeros_like(values) + offset[None, :]
    for tap_index in range(tap_count):
        summed = summed + kernel[tap_index][None, :] * padded[tap_index : tap_index + seq_length]
    return summed


def ssd_sequence(x_conv, b_conv, c_conv, step_size, a_negative, skip_gain, span_len):
    seq_length, head_count, head_dim = x_conv.shape
    state_dim = b_conv.shape[1]
    block_count = seq_length // span_len
    x_blocks = x_conv.reshape(block_count, span_len, head_count, head_dim)
    b_blocks = b_conv.reshape(block_count, span_len, state_dim)
    c_blocks = c_conv.reshape(block_count, span_len, state_dim)
    step_blocks = step_size.reshape(block_count, span_len, head_count)
    causal = (jnp.arange(span_len)[:, None] >= jnp.arange(span_len)[None, :])[:, :, None]

    def block_step(carried, pieces):
        x_blk, b_blk, c_blk, step_blk = pieces
        log_decay = jnp.cumsum(step_blk * a_negative[None, :], axis=0)
        log_gaps = jnp.where(causal, log_decay[:, None, :] - log_decay[None, :, :], 0.0)
        decays = jnp.where(causal, jnp.exp(log_gaps), 0.0)
        scores = jnp.dot(c_blk, b_blk.T, precision=HIGHEST)
        mixing = decays * scores[:, :, None] * step_blk[None, :, :]
        y_inner = jnp.einsum("tsh,shp->thp", mixing, x_blk, precision=HIGHEST)
        y_carry = (
            jnp.einsum("tn,hpn->thp", c_blk, carried, precision=HIGHEST)
            * jnp.exp(log_decay)[:, :, None]
        )
        tail_scale = jnp.exp(log_decay[-1][None, :] - log_decay) * step_blk
        new_state = carried * jnp.exp(log_decay[-1])[:, None, None] + jnp.einsum(
            "sh,shp,sn->hpn", tail_scale, x_blk, b_blk, precision=HIGHEST
        )
        return (new_state, y_inner + y_carry)

    initial = jnp.zeros((head_count, head_dim, state_dim), jnp.float32)
    last_state, y_blocks = lax.scan(
        jax.checkpoint(block_step), initial, (x_blocks, b_blocks, c_blocks, step_blocks)
    )
    return y_blocks.reshape(seq_length, head_count, head_dim) + skip_gain[None, :, None] * x_conv


def mixer_sequence(
    zx_seq,
    aux_seq,
    kernel_x,
    bias_x,
    kernel_bc,
    bias_bc,
    step_bias,
    decay_log,
    skip_gain,
    head_start,
    span_len,
):
    seq_length, head_count, pair_dim = zx_seq.shape
    head_dim = pair_dim // 2
    tap_count = kernel_x.shape[0]
    state_dim = kernel_bc.shape[1] // 2
    gate_vals = zx_seq[:, :, :head_dim]
    x_vals = zx_seq[:, :, head_dim:].reshape(seq_length, head_count * head_dim)
    x_conv = silu_fn(
        causal_conv(
            x_vals,
            kernel_x.reshape(tap_count, head_count * head_dim),
            bias_x.reshape(head_count * head_dim),
        )
    )
    bc_conv = silu_fn(causal_conv(aux_seq[:, : 2 * state_dim], kernel_bc, bias_bc))
    step_raw = lax.dynamic_slice_in_dim(aux_seq, 2 * state_dim + head_start, head_count, 1)
    step_size = jax.nn.softplus(step_raw + step_bias[None, :])
    y_vals = ssd_sequence(
        x_conv.reshape(seq_length, head_count, head_dim),
        bc_conv[:, :state_dim],
        bc_conv[:, state_dim:],
        step_size,
        -jnp.exp(decay_log),
        skip_gain,
        span_len,
    )
    return y_vals * silu_fn(gate_vals)


def place_at(values, index, total):
    holder = jnp.zeros((total,) + values.shape, jnp.float32)
    return lax.dynamic_update_index_in_dim(holder, values, index, 0)


def take_at(values, index):
    return lax.dynamic_index_in_dim(values, index, 0, keepdims=False)


def per_device(
    hidden,
    targets,
    lengths,
    dest_group,
    norm_gain,
    gate_input_weight,
    auxiliary_weight,
    conv_x,
    conv_x_bias,
    conv_bc,
    conv_bc_bias,
    dt_bias,
    a_log,
    d_skip,
    out_gain,
    output_weight,
):
    row_count = lax.axis_size("row")
    col_count = lax.axis_size("col")
    row_index = lax.axis_index("row")
    col_index = lax.axis_index("col")
    group_index = lax.axis_index("dp")
    seq_group, local_len, width_col = hidden.shape
    heads_row = gate_input_weight.shape[1]
    pair_dim = gate_input_weight.shape[2]
    head_dim = pair_dim // 2
    seq_len = local_len * row_count
    seq_col = seq_group // col_count
    model_width = width_col * col_count
    inner_width = heads_row * row_count * head_dim
    all_tokens = lengths.shape[0] * seq_len
    zx_width = heads_row * pair_dim
    head_start = row_index * heads_row
    group_lengths = lax.dynamic_slice_in_dim(lengths, group_index * seq_group, seq_group, 0)
    valid_count = jnp.sum(lengths).astype(jnp.float32)
    hidden_rows = lax.all_gather(hidden, "row", axis=1, tiled=True)
    square_part = jnp.sum(jnp.square(hidden_rows.astype(jnp.float32)), axis=2)
    mean_square = lax.psum(square_part, "col") / model_width
    inv_rms = lax.rsqrt(mean_square + EPSILON)
    rescaled = (
        hidden_rows.astype(jnp.float32) * inv_rms[:, :, None] * norm_gain[None, None, :]
    ).astype(jnp.bfloat16)
    segment = rescaled
    gate_input_addend = jnp.einsum(
        "tfb,bgn->tfgn", segment, gate_input_weight, preferred_element_type=jnp.float32
    )
    auxiliary_addend = jnp.einsum(
        "cgu,un->cgn", segment, auxiliary_weight, preferred_element_type=jnp.float32
    )
    projected = lax.psum_scatter(
        jnp.concatenate(
            [
                gate_input_addend.reshape(seq_col * lax.axis_size("col"), seq_len, zx_width),
                auxiliary_addend,
            ],
            axis=2,
        ),
        "col",
        scatter_dimension=0,
        tiled=True,
    )
    zx_own = projected[:, :, :zx_width].reshape(seq_col, seq_len, heads_row, pair_dim)
    aux_own = projected[:, :, zx_width:]

    def mixer_all(
        zx_vals, aux_vals, kernel_x, bias_x, kernel_bc, bias_bc, step_bias, decay_log, skip_gain
    ):

        def one_sequence(zx_seq, aux_seq):
            return mixer_sequence(
                zx_seq,
                aux_seq,
                kernel_x,
                bias_x,
                kernel_bc,
                bias_bc,
                step_bias,
                decay_log,
                skip_gain,
                head_start,
                CH,
            )

        return jax.vmap(one_sequence)(zx_vals, aux_vals)

    gated, mixer_pullback = jax.vjp(
        mixer_all,
        zx_own,
        aux_own,
        conv_x,
        conv_x_bias,
        conv_bc,
        conv_bc_bias,
        dt_bias,
        a_log,
        d_skip,
    )
    gate_part = jnp.sum(gated * gated, axis=(2, 3))
    gate_mean = lax.psum(gate_part, "row") / inner_width
    gate_inv = lax.rsqrt(gate_mean + EPSILON)
    normed = (gated * gate_inv[:, :, None, None] * out_gain[None, None, :, :]).astype(jnp.bfloat16)
    normalized_tokens = lax.all_gather(normed, "col", axis=0, tiled=True)
    output_segment = jnp.einsum(
        "girc,rce->gie", normalized_tokens, output_weight, preferred_element_type=jnp.float32
    )
    branch = lax.psum_scatter(output_segment, "row", scatter_dimension=1, tiled=True)
    hidden_local = hidden.astype(jnp.float32)
    result = hidden_local + branch
    positions = row_index * local_len + jnp.arange(local_len, dtype=jnp.int32)
    valid_mask = (positions[None, :] < group_lengths[:, None]).astype(jnp.float32)
    difference = (result - targets.astype(jnp.float32)) * valid_mask[:, :, None]
    loss_part = jnp.sum(difference * difference)
    grad_result = difference * (all_tokens / valid_count)
    grad_low = grad_result.astype(jnp.bfloat16)
    gradient_row_block = lax.all_gather(grad_low, "row", axis=1, tiled=True)
    segment = gradient_row_block
    grad_normed = lax.psum_scatter(
        jnp.einsum("qej,oyj->qeoy", segment, output_weight, preferred_element_type=jnp.float32),
        "col",
        scatter_dimension=0,
        tiled=True,
    )
    w_out_part = jnp.einsum(
        "wtkv,wtx->kvx", normalized_tokens, gradient_row_block, preferred_element_type=jnp.float32
    )
    weighted_grad = grad_normed * out_gain[None, None, :, :]
    out_gain_part = jnp.sum(grad_normed * gated * gate_inv[:, :, None, None], axis=(0, 1))
    inner_part = jnp.sum(weighted_grad * gated, axis=(2, 3))
    inner_sum = lax.psum(inner_part, "row")
    gate_cube = gate_inv * gate_inv * gate_inv
    grad_gated = (
        gate_inv[:, :, None, None] * weighted_grad
        - gated * (gate_cube * inner_sum / inner_width)[:, :, None, None]
    )
    (
        grad_zx,
        grad_aux,
        g_conv_x,
        g_conv_x_bias,
        g_conv_bc,
        g_conv_bc_bias,
        g_dt_bias,
        g_a_log,
        g_d_skip,
    ) = mixer_pullback(grad_gated)
    gate_input_segment = lax.all_gather(grad_zx.astype(jnp.bfloat16), "col", axis=0, tiled=True)
    auxiliary_segment = lax.all_gather(grad_aux.astype(jnp.bfloat16), "col", axis=0, tiled=True)
    gradient_segment = jnp.einsum(
        "rqza,kza->rqk", gate_input_segment, gate_input_weight, preferred_element_type=jnp.float32
    )
    gradient_segment = gradient_segment + jnp.einsum(
        "ham,nm->han", auxiliary_segment, auxiliary_weight, preferred_element_type=jnp.float32
    )
    gate_input_accum = jnp.einsum(
        "pgm,pgbq->mbq", rescaled, gate_input_segment, preferred_element_type=jnp.float32
    )
    auxiliary_accum = jnp.einsum(
        "azu,azt->ut", rescaled, auxiliary_segment, preferred_element_type=jnp.float32
    )
    hidden_wide = hidden_rows.astype(jnp.float32)
    gain_grad_part = jnp.sum(gradient_segment * hidden_wide * inv_rms[:, :, None], axis=(0, 1))
    stat_part = jnp.sum(gradient_segment * hidden_wide * norm_gain[None, None, :], axis=2)
    grad_local = lax.psum_scatter(gradient_segment, "row", scatter_dimension=1, tiled=True)
    shared = lax.psum(
        (
            stat_part,
            place_at(gain_grad_part, col_index, col_count),
            place_at(auxiliary_accum, col_index, col_count),
            g_conv_bc,
            g_conv_bc_bias,
            place_at(g_conv_x, row_index, row_count),
            place_at(g_conv_x_bias, row_index, row_count),
            place_at(g_dt_bias, row_index, row_count),
            place_at(g_a_log, row_index, row_count),
            place_at(g_d_skip, row_index, row_count),
            place_at(out_gain_part, row_index, row_count),
            loss_part,
        ),
        ("row", "col"),
    )
    (
        stat_full,
        gain_all,
        aux_all,
        conv_bc_sum,
        conv_bc_bias_sum,
        conv_x_all,
        conv_x_bias_all,
        dt_bias_all,
        a_log_all,
        d_skip_all,
        out_gain_all,
        loss_group,
    ) = shared
    stat_local = lax.dynamic_slice_in_dim(stat_full, row_index * local_len, local_len, 1)
    inv_local = lax.dynamic_slice_in_dim(inv_rms, row_index * local_len, local_len, 1)
    inv_cube = inv_local * inv_local * inv_local
    grad_hidden = (
        inv_local[:, :, None] * norm_gain[None, None, :] * grad_local
        - hidden_local * (inv_cube * stat_local / model_width)[:, :, None]
        + grad_result
    )
    summed = lax.psum(
        (
            gate_input_accum,
            w_out_part,
            take_at(gain_all, col_index),
            take_at(aux_all, col_index),
            conv_bc_sum,
            conv_bc_bias_sum,
            take_at(conv_x_all, row_index),
            take_at(conv_x_bias_all, row_index),
            take_at(dt_bias_all, row_index),
            take_at(a_log_all, row_index),
            take_at(d_skip_all, row_index),
            take_at(out_gain_all, row_index),
            loss_group,
        ),
        "dp",
    )
    (
        w_zx_grad,
        w_out_grad,
        norm_gain_grad,
        w_aux_grad,
        conv_bc_grad,
        conv_bc_bias_grad,
        conv_x_grad,
        conv_x_bias_grad,
        dt_bias_grad,
        a_log_grad,
        d_skip_grad,
        out_gain_grad,
        loss_total,
    ) = summed
    loss_value = loss_total * 0.5 / valid_count
    returned = (
        lax.all_to_all(result.astype(jnp.bfloat16), "dp", split_axis=0, concat_axis=0, tiled=True),
        lax.all_to_all(
            grad_hidden.astype(jnp.bfloat16), "dp", split_axis=0, concat_axis=0, tiled=True
        ),
    )
    output = jnp.take(returned[0], dest_group, axis=0)
    hidden_grad = jnp.take(returned[1], dest_group, axis=0)
    return (
        loss_value,
        output,
        hidden_grad,
        norm_gain_grad,
        w_zx_grad,
        w_aux_grad,
        conv_x_grad,
        conv_x_bias_grad,
        conv_bc_grad,
        conv_bc_bias_grad,
        dt_bias_grad,
        a_log_grad,
        d_skip_grad,
        out_gain_grad,
        w_out_grad,
    )


def solution(mesh):
    placed = (
        P("dp", "row", "col"),
        P("dp", "row", "col"),
        P(),
        P("dp"),
        P("col"),
        P("col", "row", None),
        P("col", None),
        P(None, "row", None),
        P("row", None),
        P(),
        P(),
        P("row"),
        P("row"),
        P("row"),
        P("row", None),
        P("row", None, "col"),
    )
    return jax.shard_map(
        per_device,
        mesh=mesh,
        in_specs=placed,
        out_specs=(
            P(),
            P("dp", "row", "col"),
            P("dp", "row", "col"),
            P("col"),
            P("col", "row", None),
            P("col", None),
            P(None, "row", None),
            P("row", None),
            P(),
            P(),
            P("row"),
            P("row"),
            P("row"),
            P("row", None),
            P("row", None, "col"),
        ),
        check_vma=False,
    )
```

profile of v0, /device:TPU:0, one launch (start us, length us, event | category | flops | bytes accessed | tf_op | source)
XLA Modules:
  0.0 2138.0 jit_solution(12645598484695174601)
XLA Ops:
  14.6 85.6 %all-gather.6.cloned.1.call-done = bf16[4,1024,1024]{2,1,0:T(8,128)(2,1)} async-done(((bf16[4,256,1024]{2,1,0:T(8,128)(2,1)}), bf16[4,1024,1024]{2,1,0:T(8,128)(2,1)}) %all-gather.6.cloned.1.call-update) | async-done | bytes 8388624 | tf_op jit(solution)/shard_map/all_gather | solution.py:148
  108.7 25.7 %fusion.109 = f32[4,1024,16,128]{1,3,2,0:T(8,128)} fusion(bf16[1024,16,128]{0,2,1:T(8,128)(2,1)} %copy.201, bf16[4,1024,1024]{2,1,0:T(8,128)(2,1)} %all-gather.6.cloned.1.call-done, f32[1024]{0:T(1024)S(1)} %copy-done.68, f32[4,1024]{1,0:T(4,128)S(1)} %add_rsqrt_fusion), kind=kOutput, calls=%fused_computation.161 | convolution fusion | flops 17196646400 | bytes 46157824 | tf_op jit(solution)/shard_map/tfb,bgn->tfgn/dot_general | solution.py:156
  137.5 24.3 %pad_maximum_fusion = f32[4,1024,2368]{1,2,0:T(8,128)} fusion(f32[4,1024,320]{1,2,0:T(8,128)S(1)} %fusion.133, f32[4,1024,2048]{1,2,0:T(8,128)} %bitcast.457), kind=kLoop, calls=%fused_computation.132 | loop fusion | flops 9699328 | bytes 77594624 | tf_op jit(solution)/shard_map/concatenate | solution.py:163
  163.8 48.7 %reduce-scatter.5.cloned.1.call-done = f32[2,1024,2368]{1,2,0:T(8,128)} async-done(((f32[4,1024,2368]{1,2,0:T(8,128)}), f32[2,1024,2368]{1,2,0:T(8,128)}) %reduce-scatter.5.cloned.1.call-update) | async-done | bytes 19398672 | tf_op jit(solution)/shard_map/reduce_scatter | solution.py:162
  288.4 104.4 %while.46 = (s32[]{:T(128)}, f32[2,16,64,128]{3,2,1,0:T(8,128)S(1)}, f32[4,2,256,16,64]{2,4,3,1,0:T(8,128)}, f32[4,2,16,64,128]{4,3,2,1,0:T(8,128)}, f32[4,2,256...) while((s32[]{:T(128)}, ...), condition=%wide.region_6.7_spmd.clone.clone, body=%wide.region_3.6_spmd.clone.clone.sunk | while | flops 3437002752 | bytes 18521172 | solution.py:56
  397.3 13.2 multiply_reduce_fusion.13
  427.3 19.1 all-gather.8.cloned.1.call-done
  446.4 14.5 convolution_bitcast_fusion
  463.1 153.1 %reduce-scatter.7.cloned.1.call-done = f32[4,256,1024]{2,1,0:T(8,128)} async-done(((f32[4,1024,1024]{2,1,0:T(8,128)}), f32[4,256,1024]{2,1,0:T(8,128)}) %reduce-scatter.7.cloned.1.call-update) | async-done | bytes 4194320 | tf_op jit(solution)/shard_map/reduce_scatter | solution.py:218
  622.6 87.7 %all-gather.10.cloned.1.call-done = bf16[4,1024,1024]{2,1,0:T(8,128)(2,1)} async-done(((bf16[4,256,1024]{2,1,0:T(8,128)(2,1)}), bf16[4,1024,1024]{2,1,0:T(8,128)(2,1)}) %all-gather.10.cloned.1.call-update) | async-done | bytes 8388624 | tf_op jit(solution)/shard_map/all_gather | solution.py:227
  710.4 14.6 fusion.113
  726.7 24.7 %reduce-scatter.9.cloned.1.call-done = f32[2,1024,16,64]{1,3,2,0:T(8,128)} async-done(((f32[4,1024,16,64]{1,3,2,0:T(8,128)}), f32[2,1024,16,64]{1,3,2,0:T(8,128)}) %reduce-scatter.9.cloned.1.call-update) | async-done | bytes 8388624 | tf_op jit(solution)/shard_map/reduce_scatter | solution.py:229
  769.4 21.6 %multiply_reduce_fusion.7 = (f32[16]{0:T(128)}, f32[2,1024,16,64]{1,3,2,0:T(8,128)S(1)}, f32[2,1024,16,64]{1,3,2,0:T(8,128)}) fusion(f32[2,1024,16,64]{1,3,2,0:T(8,128)} %bitcast.451, f32[2,1024,16,128]{1,3,2,0:T(8,128)} %bitcast.450, f32[2,1024,16,64]{1,3,2,0:T(8,128)} %get-tuple-element.900, f32[2,1024]{1,0:T(2,128)S(1)} %fusion.165, ...), kind=kLoop, calls=%fused_computation.171 | loop fusion | flops 50331632 | bytes 67129472 | tf_op jit(solution)/shard_map/transpose(jvp(vmap()))/reduce_sum | solution.py:59
  804.0 360.0 %while.45 = (s32[]{:T(128)}, f32[16]{0:T(128)S(1)}, f32[2,16,64,128]{3,2,1,0:T(8,128)}, f32[4,2,256,16,64]{2,4,3,1,0:T(8,128)}, f32[4,2,256,128]{3,2,1,0:T(8,128...) while((s32[]{:T(128)}, f32[16]{0:T(128)S(1)}, ...), condition=%wide.region_30.32_spmd.clone, body=%wide.region_17.31_spmd.clone.sunk | while | flops 7901995008 | bytes 64428108 | solution.py:56
  839.0 15.2 fusion.258
  927.6 15.2 fusion.258
  1016.2 15.2 fusion.258
  1104.8 15.2 fusion.258
  1172.0 12.4 multiply_add_fusion
  1213.6 19.9 multiply_reduce_fusion.10
  1245.6 13.9 pad_add_fusion
  1267.0 12.5 copy.211
  1291.0 13.1 fusion.152
  1308.8 27.9 %multiply_reduce_fusion.4 = (f32[1024]{0:T(1024)S(1)}, f32[4,1024]{1,0:T(4,128)S(1)}, f32[4,1024,1024]{2,1,0:T(8,128)}) fusion(bf16[4,1024,1024]{2,1,0:T(8,128)(2,1)} %all-gather.6.cloned.1.call-done, f32[4,1024]{1,0:T(4,128)S(1)} %copy-done.44, f32[1024]{0:T(1024)S(1)} %copy-done.69, f32[4,1024,1024]{2,1,0:T(8,128)} %fusion.152, ...), kind=kOutput, calls=%fused_computation.144 | convolution fusion | flops 17209225216 | bytes 62955520 | tf_op jit(solution)/shard_map/rqza,kza->rqk/dot_general | solution.py:260
  1336.9 15.4 fusion.137
  1352.2 28.0 %all-reduce.32.cloned.1.call-done = (f32[2,1024,320]{1,2,0:T(8,128)}, f32[4,4,16,64]{3,2,1,0:T(8,128)}) async-done(((f32[2,1024,320]{1,2,0:T(8,128)}, f32[4,4,16,64]{3,2,1,0:T(8,128)}), (f32[2,1024,320]{1,2,0:T(8,128)}, f32[4,4,16,64]{3,2,1,0:T(8,128)})) %all-reduce.32.cloned.1.call-update) | async-done | bytes 2686992 | tf_op jit(solution)/shard_map/psum | solution.py:276
  1382.7 26.4 %fusion.124 = f32[1024,16,128]{2,0,1:T(8,128)} fusion(bf16[4,1024,16,128]{3,2,1,0:T(8,128)(2,1)} %all-gather.12.cloned.1.call-done, bf16[4,1024,1024]{2,1,0:T(8,128)(2,1)} %all-gather.6.cloned.1.call-done, f32[1024]{0:T(1024)S(1)} %copy-done.69, f32[4,1024]{1,0:T(4,128)S(1)} %copy-done.44), kind=kOutput, calls=%fused_computation.202 | convolution fusion | flops 17196646400 | bytes 33574912 | tf_op jit(solution)/shard_map/pgm,pgbq->mbq/dot_general | solution.py:266
  1411.1 28.0 %all-reduce.25 = (f32[]{:T(128)}, f32[4,1024]{1,0:T(4,128)S(1)}, f32[2,1024]{1,0:T(2,128)S(1)}, f32[4,16,64]{2,1,0:T(8,128)S(1)}, f32[4,256]{1,0:T(4,128)S(1)}, ...) all-reduce(f32[]{:T(128)} %get-tuple-element.922, ...), channel_id=1, replica_groups=mesh['dp'=4,'row'=4,'col'=2] {'row','col'}, use_global_device_ids=true, to_apply=%region_11.12 | all-reduce | flops 15809 | bytes 126472 | tf_op jit(solution)/shard_map/psum | solution.py:276
  1439.1 100.4 %reduce-scatter.11.cloned.1.call-done = f32[4,256,1024]{2,1,0:T(8,128)} async-done(((f32[4,1024,1024]{2,1,0:T(8,128)}), f32[4,256,1024]{2,1,0:T(8,128)}) %reduce-scatter.11.cloned.1.call-update) | async-done | bytes 4194320 | tf_op jit(solution)/shard_map/reduce_scatter | solution.py:275
  1545.4 112.1 %all_to_all.10 = bf16[4,256,1024]{2,1,0:T(8,128)(2,1)S(1)} all-to-all(bf16[4,256,1024]{2,1,0:T(8,128)(2,1)S(1)} %get-tuple-element.928), channel_id=1, replica_groups=mesh['dp'=4,'row'=4,'col'=2] {'dp'}, dimensions={0} | all-to-all | bytes 4194304 | tf_op jit(solution)/shard_map/all_to_all | solution.py:350
  1662.8 110.9 %all-reduce.27 = (f32[]{:T(128)}, f32[1024]{0:T(1024)}, f32[4,16,64]{2,1,0:T(8,128)}, f32[16,64]{1,0:T(8,128)}, f32[4,256]{1,0:T(4,128)}, /*index=5*/f32[256]{0:...) all-reduce(f32[]{:T(128)} %get-tuple-element.868, ...), channel_id=1, replica_groups=mesh['dp'=4,'row'=4,'col'=2] {'dp'}, use_global_device_ids=true, to_apply=%region_12.13 | all-reduce | flops 8497 | bytes 67976 | tf_op jit(solution)/shard_map/psum | solution.py:315
  1774.5 330.3 %all-reduce.34.cloned.1.call-done = (f32[1024,16,128]{2,0,1:T(8,128)}, f32[1024,320]{0,1:T(8,128)}, f32[16,64,1024]{2,1,0:T(8,128)}) async-done(((f32[1024,16,128]{2,0,1:T(8,128)}, f32[1024,320]{0,1:T(8,128)}, f32[16,64,1024]{2,1,0:T(8,128)}), (f32[1024,16,128]{2,0,1:T(8,128)}, f32[1024,320]{0,1:T(8,128)}, f32[16,64,1024]{2,1,0:T(8,128)})) %all-reduce.34.cloned.1.call-update) | async-done | bytes 13893648 | tf_op jit(solution)/shard_map/psum | solution.py:315
  (614 shorter events, 667.8 us)
Async XLA Ops:
  7.2 439.2 %copy-start = (bf16[16,64,1024]{2,1,0:T(8,128)(2,1)S(1)}, bf16[16,64,1024]{2,1,0:T(8,128)(2,1)}, u32[]{:S(2)}) copy-start(bf16[16,64,1024]{2,1,0:T(8,128)(2,1)} %param.39) | copy-start | bytes 6291460
  7.2 93.0 %all-gather.6.cloned.1.call-start = ((), (), s32[]{:S(2)}) async-start(), calls=%async_computation.6 | async-start | bytes 10485760 | tf_op jit(solution)/shard_map/all_gather | solution.py:148
  7.9 100.8 %copy-start.68 = (f32[1024]{0:T(1024)S(1)}, f32[1024]{0:T(1024)}, u32[]{:S(2)}) copy-start(f32[1024]{0:T(1024)} %param.28) | copy-start | bytes 12292
  7.9 204.6 %reduce-scatter.5.cloned.1.call-start = ((), (), s32[]{:S(2)}) async-start(), calls=%async_computation.7 | async-start | bytes 58195968 | tf_op jit(solution)/shard_map/reduce_scatter | solution.py:162
  108.7 25.7 %copy-start.43 = (f32[4,1024]{1,0:T(4,128)}, f32[4,1024]{1,0:T(4,128)S(1)}, u32[]{:S(2)}) copy-start(f32[4,1024]{1,0:T(4,128)S(1)} %add_rsqrt_fusion) | copy-start | bytes 49156
  108.7 25.7 %copy-start.13 = (bf16[4,1024,1024]{2,1,0:T(8,128)(2,1)S(1)}, bf16[4,1024,1024]{2,1,0:T(8,128)(2,1)}, u32[]{:S(2)}) copy-start(bf16[4,1024,1024]{2,1,0:T(8,128)(2,1)} %all-gather.6.cloned.1.call-done) | copy-start | bytes 25165828
  108.7 25.7 %copy-start.26 = (bf16[1024,320]{0,1:T(8,128)(2,1)S(1)}, bf16[1024,320]{0,1:T(8,128)(2,1)}, u32[]{:S(2)}) copy-start(bf16[1024,320]{0,1:T(8,128)(2,1)} %param.30) | copy-start | bytes 1966084
  161.9 284.5 %all-gather.8.cloned.1.call-start = ((), (), s32[]{:S(2)}) async-start(), calls=%async_computation.8 | async-start | bytes 12582912 | tf_op jit(solution)/shard_map/all_gather | solution.py:214
  162.9 69.8 %copy-start.31 = (f32[1024]{0:T(1024)}, f32[1024]{0:T(1024)S(1)}, u32[]{:S(2)}) copy-start(f32[1024]{0:T(1024)S(1)} %mul.734) | copy-start | bytes 12292
  163.0 69.8 %copy-start.33 = (f32[1024]{0:T(1024)}, f32[1024]{0:T(1024)S(1)}, u32[]{:S(2)}) copy-start(f32[1024]{0:T(1024)S(1)} %mul.737) | copy-start | bytes 12292
  163.0 69.7 %copy-start.35 = (f32[1024]{0:T(1024)}, f32[1024]{0:T(1024)S(1)}, u32[]{:S(2)}) copy-start(f32[1024]{0:T(1024)S(1)} %mul.740) | copy-start | bytes 12292
  163.1 69.6 %copy-start.37 = (f32[1024]{0:T(1024)}, f32[1024]{0:T(1024)S(1)}, u32[]{:S(2)}) copy-start(f32[1024]{0:T(1024)S(1)} %mul.743) | copy-start | bytes 12292
  163.7 103.1 %copy-start.48 = (f32[1,256]{1,0:T(1,128)}, f32[1,256]{1,0:T(1,128)S(1)}, u32[]{:S(2)}) copy-start(f32[1,256]{1,0:T(1,128)S(1)} %get-tuple-element.941) | copy-start | bytes 3076
  163.7 103.1 %copy-start.50 = (f32[1,256]{1,0:T(1,128)}, f32[1,256]{1,0:T(1,128)S(1)}, u32[]{:S(2)}) copy-start(f32[1,256]{1,0:T(1,128)S(1)} %get-tuple-element.942) | copy-start | bytes 3076
  163.8 103.1 %copy-start.52 = (f32[1,256]{1,0:T(1,128)}, f32[1,256]{1,0:T(1,128)S(1)}, u32[]{:S(2)}) copy-start(f32[1,256]{1,0:T(1,128)S(1)} %get-tuple-element.943) | copy-start | bytes 3076
  163.8 103.1 %copy-start.54 = (f32[1,256]{1,0:T(1,128)}, f32[1,256]{1,0:T(1,128)S(1)}, u32[]{:S(2)}) copy-start(f32[1,256]{1,0:T(1,128)S(1)} %get-tuple-element.944) | copy-start | bytes 3076
  216.6 66.4 %copy-start.19 = (f32[2,4,256,16]{2,1,3,0:T(4,128)}, f32[2,4,256,16]{2,1,3,0:T(4,128)S(1)}, u32[]{:S(2)}) copy-start(f32[2,4,256,16]{2,1,3,0:T(4,128)S(1)} %gather.9) | copy-start | bytes 393220
  397.2 23.9 %copy-start.29 = (f32[16,64]{1,0:T(8,128)S(1)}, f32[16,64]{1,0:T(8,128)}, u32[]{:S(2)}) copy-start(f32[16,64]{1,0:T(8,128)} %param.38) | copy-start | bytes 12292
  427.3 188.8 %reduce-scatter.7.cloned.1.call-start = ((), (), s32[]{:S(2)}) async-start(), calls=%async_computation.9 | async-start | bytes 20971520 | tf_op jit(solution)/shard_map/reduce_scatter | solution.py:218
  461.0 249.4 %all-gather.10.cloned.1.call-start = ((), (), s32[]{:S(2)}) async-start(), calls=%async_computation.10 | async-start | bytes 10485760 | tf_op jit(solution)/shard_map/all_gather | solution.py:227
  463.1 261.8 %copy-start.39 = (f32[4,256]{1,0:T(4,128)}, f32[4,256]{1,0:T(4,128)S(1)}, u32[]{:S(2)}) copy-start(f32[4,256]{1,0:T(4,128)S(1)} %compare_convert_fusion) | copy-start | bytes 12292
  622.6 128.8 %reduce-scatter.9.cloned.1.call-start = ((), (), s32[]{:S(2)}) async-start(), calls=%async_computation.11 | async-start | bytes 25165824 | tf_op jit(solution)/shard_map/reduce_scatter | solution.py:229
  724.9 554.8 %all-gather.14.cloned.1.call-start = ((), (), s32[]{:S(2)}) async-start(), calls=%async_computation.13 | async-start | bytes 3932160 | tf_op jit(solution)/shard_map/all_gather | solution.py:259
  1213.5 20.0 copy-start.32
  1213.5 95.3 %all-gather.12.cloned.1.call-start = ((), (), s32[]{:S(2)}) async-start(), calls=%async_computation.12 | async-start | bytes 25165824 | tf_op jit(solution)/shard_map/all_gather | solution.py:258
  1279.5 100.7 %all-reduce.32.cloned.1.call-start = ((), (), s32[]{:S(2)}) async-start(), calls=%async_computation.15 | async-start | bytes 5505024 | tf_op jit(solution)/shard_map/psum | solution.py:276
  1291.0 248.5 %reduce-scatter.11.cloned.1.call-start = ((), (), s32[]{:S(2)}) async-start(), calls=%async_computation.14 | async-start | bytes 20971520 | tf_op jit(solution)/shard_map/reduce_scatter | solution.py:275
  1336.8 768.0 %all-reduce.34.cloned.1.call-start = ((), (), s32[]{:S(2)}) async-start(), calls=%async_computation.16 | async-start | bytes 27787264 | tf_op jit(solution)/shard_map/psum | solution.py:315
  1409.2 130.2 %copy-start.12 = (bf16[4,256,1024]{2,1,0:T(8,128)(2,1)S(1)}, bf16[4,256,1024]{2,1,0:T(8,128)(2,1)}, u32[]{:S(2)}) copy-start(bf16[4,256,1024]{2,1,0:T(8,128)(2,1)} %param.24) | copy-start | bytes 6291460
  1409.2 130.2 %copy-start.40 = (f32[4,256]{1,0:T(4,128)S(1)}, f32[4,256]{1,0:T(4,128)}, u32[]{:S(2)}) copy-start(f32[4,256]{1,0:T(4,128)} %copy-done.39) | copy-start | bytes 12292
  1545.4 116.6 %copy-start.76 = (s32[4]{0:T(128)S(1)}, s32[4]{0:T(128)}, u32[]{:S(2)}) copy-start(s32[4]{0:T(128)} %param.27) | copy-start | bytes 52
  1657.5 461.0 %all-to-all-start.1 = ((bf16[4,256,1024]{2,1,0:T(8,128)(2,1)}), bf16[4,256,1024]{2,1,0:T(8,128)(2,1)}, u32[]{:S(2)}, u32[]{:S(2)}) async-start(bf16[4,256,1024]{2,1,0:T(8,128)(2,1)} %get-tuple-element.927), calls=%async_computation.5 | async-start | bytes 4194304 | tf_op jit(solution)/shard_map/all_to_all | solution.py:351
  (81 other events, 681.3 us)
Sparse Core Ops, SparseCore 0:
  9.9 90.2 all-gather.5
  162.0 50.4 reduce-scatter.4
  427.4 18.9 all-gather.7
  461.1 155.0 reduce-scatter.6
  622.7 87.5 all-gather.9
  725.1 26.2 reduce-scatter.8
  1213.6 10.4 all-gather.13
  1279.6 29.1 all-gather.11
  1313.1 67.0 all-reduce.31
  1383.4 155.9 reduce-scatter.10
  1543.7 561.0 all-reduce.33
where the time goes:
time: 2150 us; the launch traced here: 2140 us
  waiting for transfers between devices  883 us (41%)
  matrix products  448 us (21%)
  blocking collectives  275 us (13%)
  other arithmetic  263 us (12%)
  local copies, waits for them, and re-layouts  238 us (11%)
    psum x1, waiting for transfers between devices, per_device(): lax.psum((gate_input_accum, w_out_part, take_at(gain_all, col_index), tak...  330 us
    reduce_scatter x1, waiting for transfers between devices, per_device(): lax.psum_scatter(output_segment, 'row', scatter_dimension=1, tiled=True)  153 us
    dot_general x12, matrix products, block_step(): y_inner = jnp.einsum('tsh,shp->thp', mixing, x_blk, precision=HIGHEST)  149 us
    all_to_all x1, blocking collectives, per_device(): lax.all_to_all(result.astype(jnp.bfloat16), 'dp', split_axis=0, concat_ax...  112 us
    psum x1, blocking collectives, per_device(): lax.psum((gate_input_accum, w_out_part, take_at(gain_all, col_index), tak...  111 us
    reduce_scatter x1, waiting for transfers between devices, per_device(): lax.psum_scatter(gradient_segment, 'row', scatter_dimension=1, tiled=True)  100 us
    all_gather x1, waiting for transfers between devices, per_device(): gradient_row_block = lax.all_gather(grad_low, 'row', axis=1, tiled=True)  87.7 us
    all_gather x1, waiting for transfers between devices, per_device(): hidden_rows = lax.all_gather(hidden, 'row', axis=1, tiled=True)  85.6 us
  transfers between devices with their start and end apart: 12, of which 10 were waited for; matrix products, arithmetic and copies ran while one was open for 9% of the time, Pallas kernels for 0%

commit v1 on v0

v1 whole, which is shorter than its diff:
```python
import functools
import jax
import jax.numpy as jnp
from jax import lax
from jax.experimental import pallas as pl
from jax.experimental.pallas import tpu as pltpu
from jax.sharding import PartitionSpec as P

BF = jnp.bfloat16
F32 = jnp.float32
SPAN = 512
EDGE = 128
EPSILON = 1e-05


def nn(a, b):
    return lax.dot_general(a, b, (((1,), (0,)), ((), ())), preferred_element_type=F32)


def nt(a, b):
    return lax.dot_general(a, b, (((1,), (1,)), ((), ())), preferred_element_type=F32)


def tn(a, b):
    return lax.dot_general(a, b, (((0,), (0,)), ((), ())), preferred_element_type=F32)


def exact(a, b):
    return lax.dot_general(
        a, b, (((1,), (0,)), ((), ())), precision=lax.Precision.HIGHEST, preferred_element_type=F32
    )


def sigmoid(v):
    return 0.5 * jnp.tanh(0.5 * v) + 0.5


def softplus(v):
    return jnp.maximum(v, 0.0) + jnp.log1p(jnp.exp(-jnp.abs(v)))


def shifted(before, now):
    joined = jnp.concatenate([before, now], axis=1)
    return [now] + [pltpu.roll(joined, k, 1)[:, EDGE:] for k in (1, 2, 3)]


def ahead(now, after):
    joined = jnp.concatenate([now, after], axis=1)
    size = joined.shape[1]
    return [now] + [pltpu.roll(joined, size - k, 1)[:, : now.shape[1]] for k in (1, 2, 3)]


def conv_of(shifts, taps):
    total = taps[:, 4:5] + taps[:, 3:4] * shifts[0]
    for k in (1, 2, 3):
        total = total + taps[:, 3 - k : 4 - k] * shifts[k]
    return total


def span_common(bc_before, bc_now, dt_raw, bc_taps, dt_par):
    shifts = shifted(bc_before, bc_now)
    pre = conv_of(shifts, bc_taps)
    sig = sigmoid(pre)
    act = pre * sig
    half = act.shape[0] // 2
    b_t = act[:half].astype(BF)
    c_t = act[half:].astype(BF)
    span = bc_now.shape[1]
    rows = lax.broadcasted_iota(jnp.int32, (span, span), 0)
    cols = lax.broadcasted_iota(jnp.int32, (span, span), 1)
    causal = rows <= cols
    steps = softplus(dt_raw + dt_par[:, 0:1])
    rate = -jnp.exp(dt_par[:, 1:2])
    decay = exact(steps * rate, causal.astype(F32))
    return shifts, pre, sig, b_t, c_t, causal, steps, rate, decay


def forward_kernel(
    heads, zx_ref, bc_ref, dt_ref, taps_ref, bc_taps_ref, dt_par_ref,
    gated_ref, square_ref, enter_ref,
    state, x_tail, bc_tail, carry, tailed,
):
    span = zx_ref.shape[1]
    size = zx_ref.shape[0] // heads // 2

    @pl.when(pl.program_id(0) == 0)
    def _():
        state[...] = jnp.zeros_like(state)
        x_tail[...] = jnp.zeros_like(x_tail)
        bc_tail[...] = jnp.zeros_like(bc_tail)

    bc_now = bc_ref[...]
    _, _, _, b_t, c_t, causal, steps, rate, decay = span_common(
        bc_tail[...], bc_now, dt_ref[...], bc_taps_ref[...], dt_par_ref[...]
    )
    bc_tail[...] = bc_now[:, span - EDGE :]
    b_n = b_t.astype(F32).T.astype(BF)
    scores = jnp.where(causal, nn(b_n, c_t), 0.0)
    decay_n = decay.T
    grown = jnp.exp(decay)
    last = decay[:, span - 1 : span]
    left = jnp.exp(last - decay)
    kept = jnp.exp(last)
    entering = state[...].astype(BF)
    enter_ref[...] = entering
    carry[...] = nn(entering, c_t)
    square = jnp.zeros((size, span), F32)
    for h in range(heads):
        at = slice(h * size, (h + 1) * size)
        z = zx_ref[2 * h * size : (2 * h + 1) * size, :]
        x_raw = zx_ref[(2 * h + 1) * size : (2 * h + 2) * size, :]
        taps = taps_ref[at, :]
        pre = conv_of(shifted(x_tail[at, :], x_raw), taps)
        x_tail[at, :] = x_raw[:, span - EDGE :]
        x = pre * sigmoid(pre)
        xd = x * steps[h : h + 1, :]
        mixing = scores * jnp.exp(jnp.minimum(decay[h : h + 1, :] - decay_n[:, h : h + 1], 0.0))
        y = nn(xd.astype(BF), mixing.astype(BF)) + carry[at, :] * grown[h : h + 1, :] + taps[:, 5:6] * x
        tailed[at, :] = (xd * left[h : h + 1, :]).astype(BF)
        gated = y * (z * sigmoid(z))
        square = square + gated * gated
        gated_ref[at, :] = (gated * taps[:, 6:7]).astype(BF)
        state[at, :] = state[at, :] * kept[h : h + 1, :]
    square_ref[...] = jnp.sum(square, axis=0, keepdims=True)
    state[...] = state[...] + nn(tailed[...], b_n)


def backward_kernel(
    heads, zx_ref, zx_before_ref, bc_ref, bc_before_ref, dt_ref, enter_ref, gn_ref, coef_ref,
    taps_ref, bc_taps_ref, dt_par_ref,
    gzx_ref, gx_sum_ref, gbc_sum_ref, gdt_sum_ref,
    dstate, x_head, bc_head, carry, from_state, grown_g, tailed, x_acc, bc_acc, dt_acc, rsum, dsum,
):
    span = zx_ref.shape[1]
    size = zx_ref.shape[0] // heads // 2
    half = bc_ref.shape[0] // 2
    wide = zx_ref.shape[0]
    step = pl.program_id(0)
    count = pl.num_programs(0)
    first = step == count - 1

    @pl.when(step == 0)
    def _():
        dstate[...] = jnp.zeros_like(dstate)
        x_head[...] = jnp.zeros_like(x_head)
        bc_head[...] = jnp.zeros_like(bc_head)
        x_acc[...] = jnp.zeros_like(x_acc)
        bc_acc[...] = jnp.zeros_like(bc_acc)
        dt_acc[...] = jnp.zeros_like(dt_acc)
        rsum[...] = jnp.zeros_like(rsum)
        dsum[...] = jnp.zeros_like(dsum)

    live = jnp.where(first, 0.0, 1.0)
    bc_taps = bc_taps_ref[...]
    dt_raw = dt_ref[...]
    bc_shifts, bc_pre, bc_sig, b_t, c_t, causal, steps, rate, decay = span_common(
        bc_before_ref[...] * live, bc_ref[...], dt_raw, bc_taps, dt_par_ref[...]
    )
    b_n = b_t.astype(F32).T.astype(BF)
    scores = jnp.where(causal, nn(b_n, c_t), 0.0)
    decay_n = decay.T
    grown = jnp.exp(decay)
    last = decay[:, span - 1 : span]
    left = jnp.exp(last - decay)
    kept = jnp.exp(last)
    entering = enter_ref[...]
    leaving = dstate[...].astype(BF)
    carry[...] = nn(entering, c_t)
    from_state[...] = nn(leaving, b_t)
    coef = coef_ref[...]
    dscores = jnp.zeros((span, span), F32)
    def fold(v):
        total = v[:, :EDGE]
        for k in range(1, span // EDGE):
            total = total + v[:, k * EDGE : (k + 1) * EDGE]
        return total
    for h in range(heads):
        at = slice(h * size, (h + 1) * size)
        z = zx_ref[2 * h * size : (2 * h + 1) * size, :]
        x_raw = zx_ref[(2 * h + 1) * size : (2 * h + 2) * size, :]
        x_before = zx_before_ref[(2 * h + 1) * size : (2 * h + 2) * size, :] * live
        taps = taps_ref[at, :]
        shifts = shifted(x_before, x_raw)
        pre = conv_of(shifts, taps)
        sig = sigmoid(pre)
        x = pre * sig
        steps_h = steps[h : h + 1, :]
        grown_h = grown[h : h + 1, :]
        left_h = left[h : h + 1, :]
        xd = x * steps_h
        xd_low = xd.astype(BF)
        ratio = jnp.exp(jnp.minimum(decay[h : h + 1, :] - decay_n[:, h : h + 1], 0.0))
        mixing = (scores * ratio).astype(BF)
        skip = taps[:, 5:6]
        y_scan = nn(xd_low, mixing) + carry[at, :] * grown_h
        y = y_scan + skip * x
        zsig = sigmoid(z)
        silu_z = z * zsig
        gated = y * silu_z
        gn = gn_ref[at, :].astype(F32)
        g_gated = taps[:, 6:7] * gn - gated * coef
        gy = g_gated * silu_z
        gzx_ref[2 * h * size : (2 * h + 1) * size, :] = (
            g_gated * y * (zsig + silu_z * (1.0 - zsig))
        ).astype(BF)
        gy_low = gy.astype(BF)
        gy_wide = gy_low.astype(F32)
        grown_g[at, :] = (gy * grown_h).astype(BF)
        tailed[at, :] = (xd * left_h).astype(BF)
        dx_state = from_state[at, :] * left_h
        dxd = nt(gy_low, mixing) + dx_state
        xd_wide = xd_low.astype(F32)
        rsum[h : h + 1, :] = jnp.sum(gy_wide * y_scan - xd_wide * dxd, axis=0, keepdims=True)
        dsum[h : h + 1, :] = jnp.sum(x * dxd, axis=0, keepdims=True)
        held = jnp.sum(xd_wide * dx_state, axis=0, keepdims=True)
        held = jnp.sum(held, axis=1, keepdims=True)
        flow = jnp.sum(dstate[at, :] * entering[at, :].astype(F32), axis=0, keepdims=True)
        flow = jnp.sum(flow, axis=1, keepdims=True) * kept[h : h + 1, :]
        dt_acc[h : h + 1, 0:1] = held + flow
        dscores = dscores + tn(xd_low, gy_low) * ratio
        dx = dxd * steps_h + skip * gy
        gpre = dx * (sig + x * (1.0 - sig))
        later = ahead(gpre, x_head[at, :])
        x_head[at, :] = gpre[:, :EDGE]
        g_raw = taps[:, 3:4] * later[0]
        for k in (1, 2, 3):
            g_raw = g_raw + taps[:, 3 - k : 4 - k] * later[k]
        gzx_ref[(2 * h + 1) * size : (2 * h + 2) * size, :] = g_raw.astype(BF)
        for k in range(4):
            x_acc[3 - k, at, :] = x_acc[3 - k, at, :] + fold(gpre * shifts[k])
        x_acc[4, at, :] = x_acc[4, at, :] + fold(gpre)
        x_acc[5, at, :] = x_acc[5, at, :] + fold(gy * x)
        x_acc[6, at, :] = x_acc[6, at, :] + fold(gn * gated)
    dscores = jnp.where(causal, dscores, 0.0).astype(BF)
    dc = nn(b_t, dscores) + tn(entering, grown_g[...])
    db = nt(c_t, dscores) + tn(leaving, tailed[...])
    dstate[...] = nt(grown_g[...], c_t)  + dstate[...] * jnp.concatenate(
        [jnp.broadcast_to(kept[h : h + 1, :], (size, dstate.shape[1])) for h in range(heads)], axis=0
    )
    gbc = jnp.concatenate([db, dc], axis=0) * (bc_sig + bc_pre * bc_sig * (1.0 - bc_sig))
    later = ahead(gbc, bc_head[...])
    bc_head[...] = gbc[:, :EDGE]
    g_raw = bc_taps[:, 3:4] * later[0]
    for k in (1, 2, 3):
        g_raw = g_raw + bc_taps[:, 3 - k : 4 - k] * later[k]
    gzx_ref[wide : wide + 2 * half, :] = g_raw.astype(BF)
    for k in range(4):
        bc_acc[3 - k] = bc_acc[3 - k] + fold(gbc * bc_shifts[k])
    bc_acc[4] = bc_acc[4] + fold(gbc)
    rows = lax.broadcasted_iota(jnp.int32, (span, span), 0)
    cols = lax.broadcasted_iota(jnp.int32, (span, span), 1)
    da = exact(rsum[...], (rows >= cols).astype(F32)) + dt_acc[:, 0:1]
    g_steps = dsum[...] + rate * da
    g_dt = g_steps * sigmoid(dt_raw + dt_par_ref[:, 0:1])
    gzx_ref[wide + 2 * half :, :] = g_dt.astype(BF)
    dt_acc[:, 1:2] = dt_acc[:, 1:2] + jnp.sum(g_dt, axis=1, keepdims=True)
    dt_acc[:, 2:3] = dt_acc[:, 2:3] + jnp.sum(da * steps * rate, axis=1, keepdims=True)

    @pl.when(first)
    def _():
        for k in range(7):
            gx_sum_ref[:, k : k + 1] = jnp.sum(x_acc[k], axis=1, keepdims=True)
        for k in range(5):
            gbc_sum_ref[:, k : k + 1] = jnp.sum(bc_acc[k], axis=1, keepdims=True)
        gdt_sum_ref[...] = dt_acc[...]


def scan_forward(zx, taps, bc_taps, dt_par, heads, span=SPAN):
    inner = taps.shape[0]
    length = zx.shape[1]
    aux = bc_taps.shape[0]
    steps = dt_par.shape[0]
    states = aux // 2
    body = functools.partial(forward_kernel, heads)
    whole = lambda r, c: pl.BlockSpec((r, c), lambda i: (0, 0))
    return pl.pallas_call(
        body,
        grid=(length // span,),
        in_specs=[
            pl.BlockSpec((2 * inner, span), lambda i: (0, i)),
            pl.BlockSpec((aux, span), lambda i: (2 * inner // aux, i)),
            pl.BlockSpec((steps, span), lambda i: ((2 * inner + aux) // steps, i)),
            whole(inner, 8), whole(aux, 8), whole(steps, 8),
        ],
        out_specs=[
            pl.BlockSpec((inner, span), lambda i: (0, i)),
            pl.BlockSpec((1, span), lambda i: (0, i)),
            pl.BlockSpec((inner, states), lambda i: (i, 0)),
        ],
        out_shape=[
            jax.ShapeDtypeStruct((inner, length), BF),
            jax.ShapeDtypeStruct((1, length), F32),
            jax.ShapeDtypeStruct((length // span * inner, states), BF),
        ],
        scratch_shapes=[
            pltpu.VMEM((inner, states), F32),
            pltpu.VMEM((inner, EDGE), F32),
            pltpu.VMEM((aux, EDGE), F32),
            pltpu.VMEM((inner, span), F32),
            pltpu.VMEM((inner, span), BF),
        ],
        compiler_params=pltpu.CompilerParams(vmem_limit_bytes=48 * 2**20),
        name="scan_forward",
    )(zx, zx, zx, taps, bc_taps, dt_par)


def scan_backward(zx, entering, gn, coef, taps, bc_taps, dt_par, heads, span=SPAN):
    inner = taps.shape[0]
    length = zx.shape[1]
    aux = bc_taps.shape[0]
    steps = dt_par.shape[0]
    states = aux // 2
    count = length // span
    ratio = span // EDGE
    body = functools.partial(backward_kernel, heads)
    whole = lambda r, c: pl.BlockSpec((r, c), lambda i: (0, 0))
    rev = lambda i: count - 1 - i
    before = lambda i: jnp.maximum((count - 1 - i) * ratio - 1, 0)
    return pl.pallas_call(
        body,
        grid=(count,),
        in_specs=[
            pl.BlockSpec((2 * inner, span), lambda i: (0, rev(i))),
            pl.BlockSpec((2 * inner, EDGE), lambda i: (0, before(i))),
            pl.BlockSpec((aux, span), lambda i: (2 * inner // aux, rev(i))),
            pl.BlockSpec((aux, EDGE), lambda i: (2 * inner // aux, before(i))),
            pl.BlockSpec((steps, span), lambda i: ((2 * inner + aux) // steps, rev(i))),
            pl.BlockSpec((inner, states), lambda i: (rev(i), 0)),
            pl.BlockSpec((inner, span), lambda i: (0, rev(i))),
            pl.BlockSpec((1, span), lambda i: (0, rev(i))),
            whole(inner, 8), whole(aux, 8), whole(steps, 8),
        ],
        out_specs=[
            pl.BlockSpec((2 * inner + aux + steps, span), lambda i: (0, rev(i))),
            whole(inner, 8), whole(aux, 8), whole(steps, EDGE),
        ],
        out_shape=[
            jax.ShapeDtypeStruct((2 * inner + aux + steps, length), BF),
            jax.ShapeDtypeStruct((inner, 8), F32),
            jax.ShapeDtypeStruct((aux, 8), F32),
            jax.ShapeDtypeStruct((steps, EDGE), F32),
        ],
        scratch_shapes=[
            pltpu.VMEM((inner, states), F32),
            pltpu.VMEM((inner, EDGE), F32),
            pltpu.VMEM((aux, EDGE), F32),
            pltpu.VMEM((inner, span), F32),
            pltpu.VMEM((inner, span), F32),
            pltpu.VMEM((inner, span), BF),
            pltpu.VMEM((inner, span), BF),
            pltpu.VMEM((7, inner, EDGE), F32),
            pltpu.VMEM((5, aux, EDGE), F32),
            pltpu.VMEM((steps, EDGE), F32),
            pltpu.VMEM((steps, span), F32),
            pltpu.VMEM((steps, span), F32),
        ],
        compiler_params=pltpu.CompilerParams(vmem_limit_bytes=56 * 2**20),
        name="scan_backward",
    )(zx, zx, zx, zx, zx, entering, gn, coef, taps, bc_taps, dt_par)


def gather_row(x):
    count = lax.axis_size("row")
    if count != 4:
        return lax.all_gather(x, "row", axis=0, tiled=True)
    me = lax.axis_index("row")
    size = x.shape[0]
    flip = lambda v, bit: lax.ppermute(v, "row", [(i, i ^ bit) for i in range(4)])
    from_x = flip(x, 1)
    from_y = flip(x, 2)
    cross_a = flip(from_y[: size // 2], 1)
    cross_b = flip(from_x[size // 2 :], 2)
    out = jnp.zeros((4 * size, x.shape[1]), x.dtype)
    put = lambda o, v, bit, off: lax.dynamic_update_slice(o, v, ((me ^ bit) * size + off, 0))
    out = put(out, x, 0, 0)
    out = put(out, from_x, 1, 0)
    out = put(out, from_y, 2, 0)
    out = put(out, cross_a, 3, 0)
    return put(out, cross_b, 3, size // 2)


def scatter_row(x):
    count = lax.axis_size("row")
    if count != 4:
        return lax.psum_scatter(x, "row", scatter_dimension=0, tiled=True).astype(F32)
    me = lax.axis_index("row")
    size, width = x.shape[0] // 4, x.shape[1]
    half = width // 2
    my_y, my_x = me // 2, me % 2
    blocks = x.reshape(2, 2, size, width)
    flip = lambda v, bit: lax.ppermute(v, "row", [(i, i ^ bit) for i in range(4)])
    at_x = lambda i: lax.dynamic_slice(blocks, (0, i, 0, 0), (2, 1, size, half))[:, 0]
    at_y = lambda i: lax.dynamic_slice(blocks, (i, 0, 0, half), (1, 2, size, half))[0]
    got_x = flip(at_x(1 - my_x), 1)
    got_y = flip(at_y(1 - my_y), 2)
    pick = lambda v, i: lax.dynamic_index_in_dim(v, i, 0, keepdims=False).astype(F32)
    keep_x, keep_y = at_x(my_x), at_y(my_y)
    pass_x = (pick(keep_x, 1 - my_y) + pick(got_x, 1 - my_y)).astype(BF)
    pass_y = (pick(keep_y, 1 - my_x) + pick(got_y, 1 - my_x)).astype(BF)
    end_x = flip(pass_x, 2)
    end_y = flip(pass_y, 1)
    left = pick(keep_x, my_y) + pick(got_x, my_y) + end_x.astype(F32)
    right = pick(keep_y, my_x) + pick(got_y, my_x) + end_y.astype(F32)
    return jnp.concatenate([left, right], axis=1)


def butterfly(v, axis):
    count = lax.axis_size(axis)
    bit = 1
    while bit < count:
        v = v + lax.ppermute(v, axis, [(i, i ^ bit) for i in range(count)])
        bit *= 2
    return v


def other_col(v):
    return lax.ppermute(v, "col", [(0, 1), (1, 0)])


def deal_back(rows, dest_group):
    groups = lax.axis_size("dp")
    me = lax.axis_index("dp")
    col = lax.axis_index("col")
    half = rows[0].shape[1] // 2
    own = jnp.stack([r[:, :half] for r in rows])
    got = other_col(jnp.stack([r[:, half:] for r in rows]))
    first = jnp.where(col == 0, own, got)
    second = jnp.where(col == 0, got, own)
    dealt = jnp.concatenate([first, second], axis=0)
    parts = []
    for hop in range(groups):
        piece = lax.dynamic_index_in_dim(dealt, (me + hop) % groups, 0, keepdims=False)
        if hop:
            piece = lax.ppermute(piece, "dp", [(i, (i + hop) % groups) for i in range(groups)])
        parts.append(piece)
    hops = ((me - dest_group) % groups)[:, None, None]
    out = jnp.where(hops == 0, parts[0][None], jnp.zeros((), BF))
    for hop in range(1, groups):
        out = jnp.where(hops == hop, parts[hop][None], out)
    return out


def per_device(
    hidden, targets, lengths, dest_group, norm_gain, gate_input_weight, auxiliary_weight,
    conv_x, conv_x_bias, conv_bc, conv_bc_bias, dt_bias, a_log, d_skip, out_gain, output_weight,
):
    row_count = lax.axis_size("row")
    col_count = lax.axis_size("col")
    row_index = lax.axis_index("row")
    col_index = lax.axis_index("col")
    group_index = lax.axis_index("dp")
    seq_group, local_len, width_col = hidden.shape
    heads = gate_input_weight.shape[1]
    pair = gate_input_weight.shape[2]
    head_dim = pair // 2
    inner = heads * head_dim
    wide = heads * pair
    aux = conv_bc.shape[1]
    head_total = auxiliary_weight.shape[1] - aux
    steps = -(-heads // 16) * 16
    seq_col = seq_group // col_count
    model_width = width_col * col_count
    inner_width = inner * row_count
    all_tokens = lengths.shape[0] * local_len * row_count
    valid_count = jnp.sum(lengths).astype(F32)
    group_lengths = lax.dynamic_slice_in_dim(lengths, group_index * seq_group, seq_group, 0)
    own_lengths = lax.dynamic_slice_in_dim(group_lengths, col_index * seq_col, seq_col, 0)

    def widened(v):
        mine = lax.dynamic_slice_in_dim(v, col_index * seq_col, seq_col, 0)
        theirs = lax.dynamic_slice_in_dim(v, (1 - col_index) * seq_col, seq_col, 0)
        return jnp.concatenate([mine, other_col(theirs)], axis=2)

    u_low = widened(hidden)
    gain = jnp.concatenate([norm_gain, other_col(norm_gain)])
    in_own = jnp.concatenate(
        [
            gate_input_weight.reshape(width_col, wide),
            auxiliary_weight[:, :aux],
            lax.dynamic_slice_in_dim(auxiliary_weight, aux + row_index * heads, heads, 1),
            jnp.zeros((width_col, steps - heads), BF),
        ],
        axis=1,
    )
    in_weight = jnp.concatenate([in_own, other_col(in_own)], axis=0)
    out_own = output_weight.reshape(inner, width_col)
    out_weight = jnp.concatenate([out_own, other_col(out_own)], axis=1)

    u = [u_low[k].astype(F32) for k in range(seq_col)]
    inv_rms = [lax.rsqrt(jnp.mean(v * v, axis=1, keepdims=True) + EPSILON) for v in u]
    scaled = [
        gather_row((v * r * gain[None, :]).astype(BF)) for v, r in zip(u, inv_rms, strict=True)
    ]

    column = lambda v: v.reshape(-1, 1)
    taps = jnp.concatenate(
        [
            conv_x.reshape(-1, inner).T,
            column(conv_x_bias),
            column(jnp.repeat(d_skip, head_dim)),
            column(out_gain),
            jnp.zeros((inner, 1), F32),
        ],
        axis=1,
    )
    bc_taps = jnp.concatenate([conv_bc.T, column(conv_bc_bias), jnp.zeros((aux, 3), F32)], axis=1)
    dt_par = jnp.pad(jnp.stack([dt_bias, a_log], axis=1), ((0, steps - heads), (0, 6)))

    zx, gated, square, entering = [], [], [], []
    for k in range(seq_col):
        projected = lax.dot_general(
            in_weight, scaled[k], (((0,), (1,)), ((), ())), preferred_element_type=F32
        )
        zx.append(projected)
        g, s, e = scan_forward(projected, taps, bc_taps, dt_par, heads)
        gated.append(g)
        square.append(s)
        entering.append(e)

    targets_own = widened(targets)
    positions = row_index * local_len + jnp.arange(local_len, dtype=jnp.int32)
    result, g_result, g_rows, coef = [], [], [], []
    loss_part = jnp.zeros((), F32)
    for k in range(seq_col):
        part = lax.dot_general(
            gated[k], out_weight, (((0,), (0,)), ((), ())), preferred_element_type=F32
        ).astype(BF)
        total_square = butterfly(square[k], "row")[0]
        mine = lax.dynamic_slice_in_dim(total_square, row_index * local_len, local_len, 0)
        gate_inv = lax.rsqrt(mine / inner_width + EPSILON)[:, None]
        branch = scatter_row(part) * gate_inv
        full = u[k] + branch
        valid = (positions < own_lengths[k]).astype(F32)[:, None]
        difference = (full - targets_own[k].astype(F32)) * valid
        loss_part = loss_part + jnp.sum(difference * difference)
        grad = difference * (all_tokens / valid_count)
        result.append(full.astype(BF))
        g_result.append(grad)
        share = gate_inv[:, 0] * gate_inv[:, 0] * jnp.sum(grad * branch, axis=1) / inner_width
        placed = lax.dynamic_update_slice_in_dim(
            jnp.zeros((local_len * row_count,), F32), share, row_index * local_len, 0
        )
        coef.append(butterfly(placed[None, :], "row"))
        g_rows.append(gather_row((grad * gate_inv).astype(BF)))

    output = deal_back(result, dest_group)

    w_out_part = 0.0
    g_in = []
    sums = [0.0, 0.0, 0.0]
    for k in range(seq_col):
        gn = lax.dot_general(
            out_weight, g_rows[k], (((1,), (1,)), ((), ())), preferred_element_type=F32
        )
        g, gx, gbc, gdt = scan_backward(
            zx[k], entering[k], gn, coef[k], taps, bc_taps, dt_par, heads
        )
        g_in.append(g)
        sums = [a + b for a, b in zip(sums, (gx, gbc, gdt), strict=True)]
        w_out_part = w_out_part + lax.dot_general(
            gated[k], g_rows[k], (((1,), (0,)), ((), ())), preferred_element_type=F32
        )
    w_out_half = w_out_part[:, :width_col] + other_col(
        w_out_part[:, width_col:].astype(BF)
    ).astype(F32)
    w_out_sum = lax.psum(w_out_half.astype(BF), "dp")

    in_part = 0.0
    gain_part = jnp.zeros((model_width,), F32)
    g_u = []
    for k in range(seq_col):
        part = lax.dot_general(
            g_in[k], in_weight, (((0,), (1,)), ((), ())), preferred_element_type=F32
        ).astype(BF)
        g_scaled = scatter_row(part)
        gain_part = gain_part + jnp.sum(g_scaled * u[k] * inv_rms[k], axis=0)
        weighted = g_scaled * gain[None, :]
        dot = jnp.sum(weighted * u[k], axis=1, keepdims=True) / model_width
        cube = inv_rms[k] * inv_rms[k] * inv_rms[k]
        g_u.append((g_result[k] + inv_rms[k] * weighted - u[k] * (cube * dot)).astype(BF))
        in_part = in_part + lax.dot_general(
            scaled[k], g_in[k], (((0,), (1,)), ((), ())), preferred_element_type=F32
        )
    in_half = in_part[:width_col] + other_col(in_part[width_col:].astype(BF)).astype(F32)
    aux_half = jnp.concatenate(
        [
            in_half[:, wide : wide + aux],
            lax.dynamic_update_slice_in_dim(
                jnp.zeros((width_col, head_total), F32),
                in_half[:, wide + aux : wide + aux + heads],
                row_index * heads,
                1,
            ),
        ],
        axis=1,
    )
    w_aux = lax.psum(butterfly(aux_half.astype(BF), "row"), "dp")
    w_zx = lax.psum(in_half[:, :wide].astype(BF), "dp")
    hidden_grad = deal_back(g_u, dest_group)

    gx, gbc, gdt = sums
    own = butterfly(
        butterfly(jnp.concatenate([gx.reshape(-1), gdt[:, 1:3].reshape(-1)]), "col"), "dp"
    )
    shared = jnp.concatenate([gbc.reshape(-1), loss_part[None]])
    shared = butterfly(butterfly(butterfly(shared, "col"), "row"), "dp")
    gain_half = gain_part[:width_col] + other_col(gain_part[width_col:])
    gain_sum = butterfly(butterfly(gain_half, "row"), "dp")

    gx = own[: inner * 8].reshape(inner, 8)
    gdt = own[inner * 8 :].reshape(steps, 2)
    gbc = shared[: aux * 8].reshape(aux, 8)
    loss = shared[aux * 8] * 0.5 / valid_count
    return (
        loss,
        output,
        hidden_grad,
        gain_sum,
        w_zx.astype(F32).reshape(width_col, heads, pair),
        w_aux.astype(F32),
        gx[:, :4].T.reshape(4, heads, head_dim),
        gx[:, 4].reshape(heads, head_dim),
        gbc[:, :4].T,
        gbc[:, 4],
        gdt[:heads, 0],
        gdt[:heads, 1],
        gx[:, 5].reshape(heads, head_dim).sum(axis=1),
        gx[:, 6].reshape(heads, head_dim),
        w_out_sum.astype(F32).reshape(heads, head_dim, width_col),
    )


def solution(mesh):
    placed = (
        P("dp", "row", "col"),
        P("dp", "row", "col"),
        P(),
        P("dp"),
        P("col"),
        P("col", "row", None),
        P("col", None),
        P(None, "row", None),
        P("row", None),
        P(),
        P(),
        P("row"),
        P("row"),
        P("row"),
        P("row", None),
        P("row", None, "col"),
    )
    return jax.shard_map(
        per_device,
        mesh=mesh,
        in_specs=placed,
        out_specs=(
            P(),
            P("dp", "row", "col"),
            P("dp", "row", "col"),
            P("col"),
            P("col", "row", None),
            P("col", None),
            P(None, "row", None),
            P("row", None),
            P(),
            P(),
            P("row"),
            P("row"),
            P("row"),
            P("row", None),
            P("row", None, "col"),
        ),
        check_vma=False,
    )
```

time: 2150 us -> 1020 us (0.47)
  waiting for transfers between devices: 883 us -> 357 us
  blocking collectives: 275 us -> 0 us
  matrix products: 448 us -> 195 us
  other arithmetic: 263 us -> 91.8 us
  local copies, waits for them, and re-layouts: 238 us -> 91.8 us
  Pallas kernels: 0 us -> 141 us
  starting transfers between devices: 5.29 us -> 121 us
    reduce_scatter x4 -> x0, waiting for transfers between devices: 327 us -> none  [the longest x1 153 us: per_device(): lax.psum_scatter(output_segment, 'row', scatter_dimension=1, tiled=True)]
    psum x2 -> x1, waiting for transfers between devices: 358 us -> 57.4 us  [per_device(): w_zx = lax.psum(in_half[:, :wide].astype(BF), 'dp')]
    ppermute x0 -> x70, waiting for transfers between devices: none -> 300 us  [the longest x22 145 us: butterfly(): v = v + lax.ppermute(v, axis, [(i, i ^ bit) for i in range(count)])]
    dot_general x65 -> x12, matrix products: 448 us -> 195 us  [the longest x2 63.3 us: per_device(): lax.dot_general(in_weight, scaled[k], (((0,), (1,)), ((), ())), preferred...]
    all_gather x5 -> x0, waiting for transfers between devices: 197 us -> none  [the longest x1 87.7 us: per_device(): gradient_row_block = lax.all_gather(grad_low, 'row', axis=1, tiled=True)]
    psum x5 -> x0, blocking collectives: 163 us -> none  [the longest x1 111 us: per_device(): lax.psum((gate_input_accum, w_out_part, take_at(gain_all, col_index), tak...]
    pallas_call x0 -> x4, Pallas kernels: none -> 141 us  [the longest x2 98.6 us: scan_backward(): pl.pallas_call(body, grid=(count,), in_specs=[pl.BlockSpec((2 * inner, sp...]
    ppermute x0 -> x70, starting transfers between devices: none -> 121 us  [the longest x6 57.8 us: deal_back(): lax.ppermute(piece, 'dp', [(i, (i + hop) % groups) for i in range(groups)])]
  transfers between devices with their start and end apart: 12 -> 71, of which waited for: 10 -> 29; matrix products, arithmetic and copies ran while one was open for 9% -> 31% of each run, Pallas kernels for 0% -> 9%
where the time goes in v1:
time: 1020 us
  waiting for transfers between devices  357 us (35%)
  matrix products  195 us (19%)
  Pallas kernels  141 us (14%)
  starting transfers between devices  121 us (12%)
  local copies, waits for them, and re-layouts  91.8 us (9%)
  other arithmetic  91.8 us (9%)
  between operations  19.6 us (2%)
    ppermute x22, waiting for transfers between devices, butterfly(): v = v + lax.ppermute(v, axis, [(i, i ^ bit) for i in range(count)])  145 us
    pallas_call x2, Pallas kernels, scan_backward(): pl.pallas_call(body, grid=(count,), in_specs=[pl.BlockSpec((2 * inner, sp...  98.6 us
    dot_general x2, matrix products, per_device(): lax.dot_general(in_weight, scaled[k], (((0,), (1,)), ((), ())), preferred...  63.3 us
    ppermute x16, waiting for transfers between devices, scatter_row(): lax.ppermute(v, 'row', [(i, i ^ bit) for i in range(4)])  59.5 us
    ppermute x6, starting transfers between devices, deal_back(): lax.ppermute(piece, 'dp', [(i, (i + hop) % groups) for i in range(groups)])  57.8 us
    psum x1, waiting for transfers between devices, per_device(): w_zx = lax.psum(in_half[:, :wide].astype(BF), 'dp')  57.4 us
    ppermute x16, waiting for transfers between devices, gather_row(): lax.ppermute(v, 'row', [(i, i ^ bit) for i in range(4)])  52.2 us
    dot_general x2, matrix products, per_device(): lax.dot_general(g_in[k], in_weight, (((0,), (1,)), ((), ())), preferred_e...  51.4 us
  transfers between devices with their start and end apart: 71, of which 29 were waited for; matrix products, arithmetic and copies ran while one was open for 31% of the time, Pallas kernels for 9%

profile of v1, /device:TPU:0, one launch (start us, length us, event | category | flops | bytes accessed | tf_op | source)
XLA Modules:
  0.0 1018.0 jit_solution(9023169651021335851)
XLA Ops:
  44.5 19.0 %collective-permute-done.22 = bf16[256,2048]{1,0:T(8,128)(2,1)} collective-permute-done((bf16[256,2048]{1,0:T(8,128)(2,1)}, bf16[256,2048]{1,0:T(8,128)(2,1)}, u32[]{:S(2)}, u32[]{:S(2)}) %collective-permute-start.22) | collective-permute-done | bytes 1048608 | tf_op jit(solution)/shard_map/ppermute | solution.py:368
  70.4 14.4 %collective-permute-done.4 = bf16[256,2048]{1,0:T(8,128)(2,1)} collective-permute-done((bf16[256,2048]{1,0:T(8,128)(2,1)}, bf16[256,2048]{1,0:T(8,128)(2,1)}, u32[]{:S(2)}, u32[]{:S(2)}) %collective-permute-start.4) | collective-permute-done | bytes 1048608 | tf_op jit(solution)/shard_map/ppermute | solution.py:368
  97.9 7.8 collective-permute-done.5
  109.7 31.7 %fusion.72.zx_ref.bc_ref.dt_ref.zx_before_ref.bc_before_ref = f32[2320,1024]{1,0:T(8,128)} fusion(bf16[1024,2048]{1,0:T(8,128)(2,1)} %constant_dynamic-update-slice_fusion.7, bf16[1024,2320]{0,1:T(8,128)(2,1)} %collective-permute-done, bf16[1024,16]{0,1:T(8,128)(2,1)S(1)} %constant_dynamic-slice_fusion.10, bf16[1024,256]{0,1:T(8,128)(2,1)S(1)} %copy-done.30, ...), kind=kOutput, calls=%fused_computation.243 | convolution fusion | flops 9768796160 | bytes 23199744 | tf_op jit(solution)/shard_map/dot_general | solution.py:511
  141.5 21.4 %scan_forward.3 = (bf16[1024,1024]{1,0:T(8,128)(2,1)S(1)}, f32[1,1024]{1,0:T(1,128)S(1)}, bf16[2048,128]{1,0:T(8,128)(2,1)S(1)}) custom-call(f32[2320,1024]{1,0:T(8,128)} %fusion.72.zx_ref.bc_ref.dt_ref.zx_before_ref.bc_before_ref, f32[2320,1024]{1,0:T(8,128)} %fusion.72.zx_ref.bc_ref.dt_ref.zx_before_ref.bc_before_ref, ...), custom_call_target="tpu_custom_call" | custom-call | tf_op jit(solution)/shard_map/scan_forward/pallas_call | solution.py:276
  162.9 7.3 convolution_convert_fusion.2
  174.1 31.6 %fusion.73.zx_ref.bc_ref.dt_ref.zx_before_ref.bc_before_ref = f32[2320,1024]{1,0:T(8,128)} fusion(bf16[1024,2048]{1,0:T(8,128)(2,1)} %constant_dynamic-update-slice_fusion.19, bf16[1024,2320]{0,1:T(8,128)(2,1)} %collective-permute-done, bf16[1024,16]{0,1:T(8,128)(2,1)S(1)} %constant_dynamic-slice_fusion.10, bf16[1024,256]{0,1:T(8,128)(2,1)S(1)} %copy-done.30, ...), kind=kOutput, calls=%fused_computation.244 | convolution fusion | flops 9768796160 | bytes 23199744 | tf_op jit(solution)/shard_map/dot_general | solution.py:511
  205.7 21.0 %scan_forward.2 = (bf16[1024,1024]{1,0:T(8,128)(2,1)S(1)}, f32[1,1024]{1,0:T(1,128)S(1)}, bf16[2048,128]{1,0:T(8,128)(2,1)S(1)}) custom-call(f32[2320,1024]{1,0:T(8,128)} %fusion.73.zx_ref.bc_ref.dt_ref.zx_before_ref.bc_before_ref, f32[2320,1024]{1,0:T(8,128)} %fusion.73.zx_ref.bc_ref.dt_ref.zx_before_ref.bc_before_ref, ...), custom_call_target="tpu_custom_call" | custom-call | tf_op jit(solution)/shard_map/scan_forward/pallas_call | solution.py:276
  226.8 7.8 convolution_convert_fusion.3
  252.1 9.6 collective-permute-done.29
  269.4 9.5 collective-permute-done.26
  286.7 14.8 %collective-permute-done.30 = f32[1,1024]{1,0:T(1,128)S(1)} collective-permute-done((f32[1,1024]{1,0:T(1,128)S(1)}, f32[1,1024]{1,0:T(1,128)S(1)}, u32[]{:S(2)}, u32[]{:S(2)}) %collective-permute-start.30) | collective-permute-done | bytes 4128 | tf_op jit(solution)/shard_map/ppermute | solution.py:411
  303.1 7.3 collective-permute-done.13
  319.7 7.7 collective-permute-done.11
  339.4 29.7 %collective-permute-done.35 = f32[1,1024]{1,0:T(1,128)S(1)} collective-permute-done((f32[1,1024]{1,0:T(1,128)S(1)}, f32[1,1024]{1,0:T(1,128)S(1)}, u32[]{:S(2)}, u32[]{:S(2)}) %collective-permute-start.35) | collective-permute-done | bytes 4128 | tf_op jit(solution)/shard_map/ppermute | solution.py:411
  385.7 8.1 collective-permute-done.33
  394.0 9.2 fusion.70.gn_ref
  403.2 49.3 %scan_backward.3 = (bf16[2320,1024]{1,0:T(8,128)(2,1)}, f32[1024,8]{1,0:T(8,128)}, f32[256,8]{1,0:T(8,128)}, f32[16,128]{1,0:T(8,128)}) custom-call(f32[2320,1024]{1,0:T(8,128)} %fusion.72.zx_ref.bc_ref.dt_ref.zx_before_ref.bc_before_ref, f32[2320,1024]{1,0:T(8,128)} %fusion.72.zx_ref.bc_ref.dt_ref.zx_before_ref.bc_before_ref, ...), custom_call_target="tpu_custom_call" | custom-call | tf_op jit(solution)/shard_map/scan_backward/pallas_call | solution.py:319
  452.6 16.8 %fusion.82 = f32[2048,2320]{0,1:T(8,128)} fusion(bf16[2320,1024]{1,0:T(8,128)(2,1)} %get-tuple-element.38, bf16[1024,2048]{1,0:T(8,128)(2,1)} %constant_dynamic-update-slice_fusion.7), kind=kOutput, calls=%fused_computation.247 | convolution fusion | flops 9730785280 | bytes 27951104 | tf_op jit(solution)/shard_map/dot_general | solution.py:581
  469.6 9.2 fusion.71.gn_ref
  478.7 49.3 %scan_backward.2 = (bf16[2320,1024]{1,0:T(8,128)(2,1)}, f32[1024,8]{1,0:T(8,128)}, f32[256,8]{1,0:T(8,128)}, f32[16,128]{1,0:T(8,128)}) custom-call(f32[2320,1024]{1,0:T(8,128)} %fusion.73.zx_ref.bc_ref.dt_ref.zx_before_ref.bc_before_ref, f32[2320,1024]{1,0:T(8,128)} %fusion.73.zx_ref.bc_ref.dt_ref.zx_before_ref.bc_before_ref, ...), custom_call_target="tpu_custom_call" | custom-call | tf_op jit(solution)/shard_map/scan_backward/pallas_call | solution.py:319
  528.0 19.4 %convolution_add_fusion = f32[2048,2320]{0,1:T(8,128)} fusion(f32[2048,2320]{0,1:T(8,128)} %fusion.82, bf16[2320,1024]{1,0:T(8,128)(2,1)} %get-tuple-element.37, bf16[1024,2048]{1,0:T(8,128)(2,1)} %constant_dynamic-update-slice_fusion.19), kind=kOutput, calls=%fused_computation | convolution fusion | flops 9735536640 | bytes 46956544 | tf_op jit(solution)/shard_map/dot_general | solution.py:581
  585.5 25.7 %convolution_convert_fusion.1 = bf16[1024,2048]{1,0:T(8,128)(2,1)} fusion(bf16[2320,1024]{1,0:T(8,128)(2,1)} %get-tuple-element.37, bf16[1024,2320]{0,1:T(8,128)(2,1)} %collective-permute-done, bf16[1024,16]{0,1:T(8,128)(2,1)S(1)} %copy-done.40, bf16[1024,256]{0,1:T(8,128)(2,1)} %copy-done.29, bf16[1024,2048]{0,1:T(8,128)(2,1)} %bitcast.210), kind=kOutput, calls=%fused_computation.23 | convolution fusion | flops 9770893312 | bytes 18448384 | tf_op jit(solution)/shard_map/dot_general | solution.py:572
  617.8 25.7 %convolution_convert_fusion = bf16[1024,2048]{1,0:T(8,128)(2,1)} fusion(bf16[2320,1024]{1,0:T(8,128)(2,1)} %get-tuple-element.38, bf16[1024,2320]{0,1:T(8,128)(2,1)} %collective-permute-done, bf16[1024,16]{0,1:T(8,128)(2,1)S(1)} %copy-done.40, bf16[1024,256]{0,1:T(8,128)(2,1)} %copy-done.29, bf16[1024,2048]{0,1:T(8,128)(2,1)} %bitcast.211), kind=kOutput, calls=%fused_computation.22 | convolution fusion | flops 9770893312 | bytes 18448384 | tf_op jit(solution)/shard_map/dot_general | solution.py:572
  664.1 7.2 copy.74
  678.8 29.7 %collective-permute-done.47 = bf16[256,1024]{1,0:T(8,128)(2,1)} collective-permute-done((bf16[256,1024]{1,0:T(8,128)(2,1)}, bf16[256,1024]{1,0:T(8,128)(2,1)}, u32[]{:S(2)}, u32[]{:S(2)}) %collective-permute-start.47) | collective-permute-done | bytes 524320 | tf_op jit(solution)/shard_map/ppermute | solution.py:391
  723.8 9.5 collective-permute-done.53
  760.7 32.4 %collective-permute-done.41 = f32[2049]{0:T(1024)S(1)} collective-permute-done((f32[2049]{0:T(1024)S(1)}, f32[2049]{0:T(1024)S(1)}, u32[]{:S(2)}, u32[]{:S(2)}) %collective-permute-start.41) | collective-permute-done | bytes 8228 | tf_op jit(solution)/shard_map/ppermute | solution.py:411
  803.7 38.4 %collective-permute-done.68 = f32[8224]{0:T(1024)S(1)} collective-permute-done((f32[8224]{0:T(1024)S(1)}, f32[8224]{0:T(1024)S(1)}, u32[]{:S(2)}, u32[]{:S(2)}) %collective-permute-start.68) | collective-permute-done | bytes 32928 | tf_op jit(solution)/shard_map/ppermute | solution.py:411
  842.2 50.5 %collective-permute-start.57 = (bf16[256,1024]{1,0:T(8,128)(2,1)}, bf16[256,1024]{1,0:T(8,128)(2,1)}, u32[]{:S(2)}, u32[]{:S(2)}) collective-permute-start(bf16[256,1024]{1,0:T(8,128)(2,1)} %get-tuple-element.132), channel_id=1, source_target_pairs={{0,8},{8,16},{16,24},{24,0},{1,9},{9,17},{17,25},{25,1},{2,10},{10... | collective-permute-start | bytes 1572872 | tf_op jit(solution)/shard_map/ppermute | solution.py:434
  902.9 35.7 %collective-permute-done.57 = bf16[256,1024]{1,0:T(8,128)(2,1)} collective-permute-done((bf16[256,1024]{1,0:T(8,128)(2,1)}, bf16[256,1024]{1,0:T(8,128)(2,1)}, u32[]{:S(2)}, u32[]{:S(2)}) %collective-permute-start.57) | collective-permute-done | bytes 524320 | tf_op jit(solution)/shard_map/ppermute | solution.py:434
  942.1 57.4 %all-reduce.4.cloned.1.call-done = (bf16[1024,16,128]{2,1,0:T(8,128)(2,1)}, bf16[1024,320]{0,1:T(8,128)(2,1)}, bf16[16,64,1024]{2,1,0:T(8,128)(2,1)}) async-done(((bf16[1024,16,128]{2,1,0:T(8,128)(2,1)}, bf16[1024,320]{0,1:T(8,128)(2,1)}, bf16[16,64,1024]{2,1,0:T(8,128)(2,1)}), (bf16[1024,16,128]{2,1,0:T(8,128)(2,1)}, bf16[1024,320]{0,1:T(8,128)(2,1)}, ...) | async-done | bytes 6946832 | tf_op jit(solution)/shard_map/psum | solution.py:598
  (431 shorter events, 284.2 us)
Async XLA Ops:
  7.2 992.3 %all-reduce.4.cloned.1.call-start = ((), (), s32[]{:S(2)}) async-start(), calls=%async_computation | async-start | bytes 13893632 | tf_op jit(solution)/shard_map/psum | solution.py:598
  22.0 87.7 %collective-permute-start = (bf16[1024,2320]{0,1:T(8,128)(2,1)}, bf16[1024,2320]{0,1:T(8,128)(2,1)}, u32[]{:S(2)}, u32[]{:S(2)}) collective-permute-start(bf16[1024,2320]{0,1:T(8,128)(2,1)} %pad_maximum_fusion.1), channel_id=1, source_target_pairs={{0,1},{1,0},{2,3},{3,2},{4,5},{5,4},{6,7},{7,6},{8,9},{9,8},{10,11... | collective-permute-start | bytes 14254088 | tf_op jit(solution)/shard_map/ppermute | solution.py:417
  42.9 42.0 %collective-permute-start.4 = (bf16[256,2048]{1,0:T(8,128)(2,1)}, bf16[256,2048]{1,0:T(8,128)(2,1)}, u32[]{:S(2)}, u32[]{:S(2)}) collective-permute-start(bf16[256,2048]{1,0:T(8,128)(2,1)} %get-tuple-element.117), channel_id=1, source_target_pairs={{0,4},{2,6},{4,0},{6,2},{1,5},{3,7},{5,1},{7,3},{8,12},{10,14},{12... | collective-permute-start | bytes 3145736 | tf_op jit(solution)/shard_map/ppermute | solution.py:368
  43.4 44.1 %collective-permute-start.3 = (bf16[256,2048]{1,0:T(8,128)(2,1)}, bf16[256,2048]{1,0:T(8,128)(2,1)}, u32[]{:S(2)}, u32[]{:S(2)}) collective-permute-start(bf16[256,2048]{1,0:T(8,128)(2,1)} %get-tuple-element.117), channel_id=1, source_target_pairs={{0,2},{2,0},{4,6},{6,4},{1,3},{3,1},{5,7},{7,5},{8,10},{10,8},{12,... | collective-permute-start | bytes 3145736 | tf_op jit(solution)/shard_map/ppermute | solution.py:368
  63.5 99.3 %collective-permute-start.7 = (bf16[1024,1024]{1,0:T(8,128)(2,1)}, bf16[1024,1024]{1,0:T(8,128)(2,1)}, u32[]{:S(2)}, u32[]{:S(2)}) collective-permute-start(bf16[1024,1024]{1,0:T(8,128)(2,1)} %bitcast.248), channel_id=1, source_target_pairs={{0,1},{1,0},{2,3},{3,2},{4,5},{5,4},{6,7},{7,6},{8,9},{9,8},{10,11... | collective-permute-start | bytes 6291464 | tf_op jit(solution)/shard_map/ppermute | solution.py:417
  173.4 69.7 %collective-permute-start.25 = (bf16[2,256,1024]{2,1,0:T(8,128)(2,1)}, bf16[2,256,1024]{2,1,0:T(8,128)(2,1)}, u32[]{:S(2)}, u32[]{:S(2)}) collective-permute-start(bf16[2,256,1024]{2,1,0:T(8,128)(2,1)} %dynamic-slice_bitcast_fusion.5), channel_id=1, source_target_pairs={{0,2},{2,0},{4,6},{6,4},{1,3},{3,1},{5,7},{7,5},{8,10},{10,8},{12,... | collective-permute-start | bytes 3145736 | tf_op jit(solution)/shard_map/ppermute | solution.py:391
  247.3 63.0 %collective-permute-start.10 = (bf16[2,256,1024]{2,1,0:T(8,128)(2,1)}, bf16[2,256,1024]{2,1,0:T(8,128)(2,1)}, u32[]{:S(2)}, u32[]{:S(2)}) collective-permute-start(bf16[2,256,1024]{2,1,0:T(8,128)(2,1)} %dynamic-slice_bitcast_fusion.6), channel_id=1, source_target_pairs={{0,4},{2,6},{4,0},{6,2},{1,5},{3,7},{5,1},{7,3},{8,12},{10,14},{12... | collective-permute-start | bytes 3145736 | tf_op jit(solution)/shard_map/ppermute | solution.py:391
  261.7 53.0 %collective-permute-start.14 = (bf16[2,256,1024]{2,1,0:T(8,128)(2,1)}, bf16[2,256,1024]{2,1,0:T(8,128)(2,1)}, u32[]{:S(2)}, u32[]{:S(2)}) collective-permute-start(bf16[2,256,1024]{2,1,0:T(8,128)(2,1)} %get-tuple-element.145), channel_id=1, source_target_pairs={{0,1},{1,0},{2,3},{3,2},{4,5},{5,4},{6,7},{7,6},{8,9},{9,8},{10,11... | collective-permute-start | bytes 3145736 | tf_op jit(solution)/shard_map/ppermute | solution.py:417
  317.0 64.1 %collective-permute-start.31 = (bf16[256,2048]{1,0:T(8,128)(2,1)S(1)}, bf16[256,2048]{1,0:T(8,128)(2,1)S(1)}, u32[]{:S(2)}, u32[]{:S(2)}) collective-permute-start(bf16[256,2048]{1,0:T(8,128)(2,1)S(1)} %get-tuple-element.107), channel_id=1, source_target_pairs={{0,2},{2,0},{4,6},{6,4},{1,3},{3,1},{5,7},{7,5},{8,10},{10,8},{12,... | collective-permute-start | bytes 3145736 | tf_op jit(solution)/shard_map/ppermute | solution.py:368
  318.6 62.1 %collective-permute-start.32 = (bf16[256,2048]{1,0:T(8,128)(2,1)S(1)}, bf16[256,2048]{1,0:T(8,128)(2,1)S(1)}, u32[]{:S(2)}, u32[]{:S(2)}) collective-permute-start(bf16[256,2048]{1,0:T(8,128)(2,1)S(1)} %get-tuple-element.107), channel_id=1, source_target_pairs={{0,4},{2,6},{4,0},{6,2},{1,5},{3,7},{5,1},{7,3},{8,12},{10,14},{12... | collective-permute-start | bytes 3145736 | tf_op jit(solution)/shard_map/ppermute | solution.py:368
  331.2 52.4 %collective-permute-start.15 = (bf16[256,2048]{1,0:T(8,128)(2,1)S(1)}, bf16[256,2048]{1,0:T(8,128)(2,1)S(1)}, u32[]{:S(2)}, u32[]{:S(2)}) collective-permute-start(bf16[256,2048]{1,0:T(8,128)(2,1)S(1)} %get-tuple-element.110), channel_id=1, source_target_pairs={{0,2},{2,0},{4,6},{6,4},{1,3},{3,1},{5,7},{7,5},{8,10},{10,8},{12,... | collective-permute-start | bytes 3145736 | tf_op jit(solution)/shard_map/ppermute | solution.py:368
  331.7 51.2 %collective-permute-start.16 = (bf16[256,2048]{1,0:T(8,128)(2,1)S(1)}, bf16[256,2048]{1,0:T(8,128)(2,1)S(1)}, u32[]{:S(2)}, u32[]{:S(2)}) collective-permute-start(bf16[256,2048]{1,0:T(8,128)(2,1)S(1)} %get-tuple-element.110), channel_id=1, source_target_pairs={{0,4},{2,6},{4,0},{6,2},{1,5},{3,7},{5,1},{7,3},{8,12},{10,14},{12... | collective-permute-start | bytes 3145736 | tf_op jit(solution)/shard_map/ppermute | solution.py:368
  382.9 86.5 %collective-permute-start.17 = (bf16[128,2048]{1,0:T(8,128)(2,1)S(1)}, bf16[128,2048]{1,0:T(8,128)(2,1)S(1)}, u32[]{:S(2)}, u32[]{:S(2)}) collective-permute-start(bf16[128,2048]{1,0:T(8,128)(2,1)S(1)} %slice.212), channel_id=1, source_target_pairs={{0,2},{2,0},{4,6},{6,4},{1,3},{3,1},{5,7},{7,5},{8,10},{10,8},{12,... | collective-permute-start | bytes 1572872 | tf_op jit(solution)/shard_map/ppermute | solution.py:368
  383.7 85.8 %collective-permute-start.18 = (bf16[128,2048]{1,0:T(8,128)(2,1)S(1)}, bf16[128,2048]{1,0:T(8,128)(2,1)S(1)}, u32[]{:S(2)}, u32[]{:S(2)}) collective-permute-start(bf16[128,2048]{1,0:T(8,128)(2,1)S(1)} %slice.213), channel_id=1, source_target_pairs={{0,4},{2,6},{4,0},{6,2},{1,5},{3,7},{5,1},{7,3},{8,12},{10,14},{12... | collective-permute-start | bytes 1572872 | tf_op jit(solution)/shard_map/ppermute | solution.py:368
  558.3 115.5 %collective-permute-start.42 = (bf16[2,256,1024]{2,1,0:T(8,128)(2,1)}, bf16[2,256,1024]{2,1,0:T(8,128)(2,1)}, u32[]{:S(2)}, u32[]{:S(2)}) collective-permute-start(bf16[2,256,1024]{2,1,0:T(8,128)(2,1)} %pad_maximum_fusion.8), channel_id=1, source_target_pairs={{0,1},{1,0},{2,3},{3,2},{4,5},{5,4},{6,7},{7,6},{8,9},{9,8},{10,11... | collective-permute-start | bytes 3145736 | tf_op jit(solution)/shard_map/ppermute | solution.py:417
  573.1 81.6 %collective-permute-start.69 = (bf16[1024,1024]{1,0:T(8,128)(2,1)}, bf16[1024,1024]{1,0:T(8,128)(2,1)}, u32[]{:S(2)}, u32[]{:S(2)}) collective-permute-start(bf16[1024,1024]{1,0:T(8,128)(2,1)} %slice.293), channel_id=1, source_target_pairs={{0,1},{1,0},{2,3},{3,2},{4,5},{5,4},{6,7},{7,6},{8,9},{9,8},{10,11... | collective-permute-start | bytes 6291464 | tf_op jit(solution)/shard_map/ppermute | solution.py:417
  613.5 34.9 %collective-permute-start.46 = (bf16[2,256,1024]{2,1,0:T(8,128)(2,1)}, bf16[2,256,1024]{2,1,0:T(8,128)(2,1)}, u32[]{:S(2)}, u32[]{:S(2)}) collective-permute-start(bf16[2,256,1024]{2,1,0:T(8,128)(2,1)} %dynamic-slice_bitcast_fusion.3), channel_id=1, source_target_pairs={{0,2},{2,0},{4,6},{6,4},{1,3},{3,1},{5,7},{7,5},{8,10},{10,8},{12,... | collective-permute-start | bytes 3145736 | tf_op jit(solution)/shard_map/ppermute | solution.py:391
  616.1 38.8 %collective-permute-start.65 = (bf16[1024,320]{0,1:T(8,128)(2,1)}, bf16[1024,320]{0,1:T(8,128)(2,1)}, u32[]{:S(2)}, u32[]{:S(2)}) collective-permute-start(bf16[1024,320]{0,1:T(8,128)(2,1)} %fusion.69), channel_id=1, source_target_pairs={{0,4},{2,6},{4,0},{6,2},{1,5},{3,7},{5,1},{7,3},{8,12},{10,14},{12... | collective-permute-start | bytes 1966088 | tf_op jit(solution)/shard_map/ppermute | solution.py:411
  654.6 62.1 %collective-permute-start.52 = (bf16[2,256,1024]{2,1,0:T(8,128)(2,1)}, bf16[2,256,1024]{2,1,0:T(8,128)(2,1)}, u32[]{:S(2)}, u32[]{:S(2)}) collective-permute-start(bf16[2,256,1024]{2,1,0:T(8,128)(2,1)} %dynamic-slice_bitcast_fusion), channel_id=1, source_target_pairs={{0,4},{2,6},{4,0},{6,2},{1,5},{3,7},{5,1},{7,3},{8,12},{10,14},{12... | collective-permute-start | bytes 3145736 | tf_op jit(solution)/shard_map/ppermute | solution.py:391
  654.9 53.6 %collective-permute-start.47 = (bf16[256,1024]{1,0:T(8,128)(2,1)}, bf16[256,1024]{1,0:T(8,128)(2,1)}, u32[]{:S(2)}, u32[]{:S(2)}) collective-permute-start(bf16[256,1024]{1,0:T(8,128)(2,1)} %fusion.31), channel_id=1, source_target_pairs={{0,4},{2,6},{4,0},{6,2},{1,5},{3,7},{5,1},{7,3},{8,12},{10,14},{12... | collective-permute-start | bytes 1572872 | tf_op jit(solution)/shard_map/ppermute | solution.py:391
  678.5 39.1 %collective-permute-start.51 = (bf16[256,1024]{1,0:T(8,128)(2,1)}, bf16[256,1024]{1,0:T(8,128)(2,1)}, u32[]{:S(2)}, u32[]{:S(2)}) collective-permute-start(bf16[256,1024]{1,0:T(8,128)(2,1)} %fusion.27), channel_id=1, source_target_pairs={{0,4},{2,6},{4,0},{6,2},{1,5},{3,7},{5,1},{7,3},{8,12},{10,14},{12... | collective-permute-start | bytes 1572872 | tf_op jit(solution)/shard_map/ppermute | solution.py:391
  739.0 57.8 %collective-permute-start.54 = (bf16[2,256,1024]{2,1,0:T(8,128)(2,1)}, bf16[2,256,1024]{2,1,0:T(8,128)(2,1)}, u32[]{:S(2)}, u32[]{:S(2)}) collective-permute-start(bf16[2,256,1024]{2,1,0:T(8,128)(2,1)} %pad_maximum_fusion.10), channel_id=1, source_target_pairs={{0,1},{1,0},{2,3},{3,2},{4,5},{5,4},{6,7},{7,6},{8,9},{9,8},{10,11... | collective-permute-start | bytes 3145736 | tf_op jit(solution)/shard_map/ppermute | solution.py:417
  750.4 49.6 %collective-permute-start.43 = (bf16[256,1024]{1,0:T(8,128)(2,1)}, bf16[256,1024]{1,0:T(8,128)(2,1)S(1)}, u32[]{:S(2)}, u32[]{:S(2)}) collective-permute-start(bf16[256,1024]{1,0:T(8,128)(2,1)} %get-tuple-element.136), channel_id=1, source_target_pairs={{0,24},{8,0},{16,8},{24,16},{1,25},{9,1},{17,9},{25,17},{2,26},{10... | collective-permute-start | bytes 1572872 | tf_op jit(solution)/shard_map/ppermute | solution.py:434
  753.9 39.2 %collective-permute-start.41 = (f32[2049]{0:T(1024)S(1)}, f32[2049]{0:T(1024)S(1)}, u32[]{:S(2)}, u32[]{:S(2)}) collective-permute-start(f32[2049]{0:T(1024)S(1)} %add.542), channel_id=1, source_target_pairs={{0,16},{8,24},{16,0},{24,8},{1,17},{9,25},{17,1},{25,9},{2,18},{10... | collective-permute-start | bytes 24596 | tf_op jit(solution)/shard_map/ppermute | solution.py:411
  753.9 39.8 %collective-permute-start.67 = (f32[8224]{0:T(1024)S(1)}, f32[8224]{0:T(1024)S(1)}, u32[]{:S(2)}, u32[]{:S(2)}) collective-permute-start(f32[8224]{0:T(1024)S(1)} %add.583), channel_id=1, source_target_pairs={{0,8},{8,0},{16,24},{24,16},{1,9},{9,1},{17,25},{25,17},{2,10},{10... | collective-permute-start | bytes 98696 | tf_op jit(solution)/shard_map/ppermute | solution.py:411
  793.1 107.2 %collective-permute-start.44 = (bf16[256,1024]{1,0:T(8,128)(2,1)}, bf16[256,1024]{1,0:T(8,128)(2,1)S(1)}, u32[]{:S(2)}, u32[]{:S(2)}) collective-permute-start(bf16[256,1024]{1,0:T(8,128)(2,1)} %get-tuple-element.137), channel_id=1, source_target_pairs={{0,16},{8,24},{16,0},{24,8},{1,17},{9,25},{17,1},{25,9},{2,18},{10... | collective-permute-start | bytes 1572872 | tf_op jit(solution)/shard_map/ppermute | solution.py:434
  793.7 106.6 %collective-permute-start.45 = (bf16[256,1024]{1,0:T(8,128)(2,1)}, bf16[256,1024]{1,0:T(8,128)(2,1)}, u32[]{:S(2)}, u32[]{:S(2)}) collective-permute-start(bf16[256,1024]{1,0:T(8,128)(2,1)} %get-tuple-element.138), channel_id=1, source_target_pairs={{0,8},{8,16},{16,24},{24,0},{1,9},{9,17},{17,25},{25,1},{2,10},{10... | collective-permute-start | bytes 1572872 | tf_op jit(solution)/shard_map/ppermute | solution.py:434
  793.8 48.3 %collective-permute-start.68 = (f32[8224]{0:T(1024)S(1)}, f32[8224]{0:T(1024)S(1)}, u32[]{:S(2)}, u32[]{:S(2)}) collective-permute-start(f32[8224]{0:T(1024)S(1)} %add.584), channel_id=1, source_target_pairs={{0,16},{8,24},{16,0},{24,8},{1,17},{9,25},{17,1},{25,9},{2,18},{10... | collective-permute-start | bytes 98696 | tf_op jit(solution)/shard_map/ppermute | solution.py:411
  796.8 45.4 %collective-permute-start.62 = (f32[1024]{0:T(1024)S(1)}, f32[1024]{0:T(1024)S(1)}, u32[]{:S(2)}, u32[]{:S(2)}) collective-permute-start(f32[1024]{0:T(1024)S(1)} %add.574), channel_id=1, source_target_pairs={{0,16},{8,24},{16,0},{24,8},{1,17},{9,25},{17,1},{25,9},{2,18},{10... | collective-permute-start | bytes 12296 | tf_op jit(solution)/shard_map/ppermute | solution.py:411
  800.0 100.3 %collective-permute-start.55 = (bf16[256,1024]{1,0:T(8,128)(2,1)}, bf16[256,1024]{1,0:T(8,128)(2,1)S(1)}, u32[]{:S(2)}, u32[]{:S(2)}) collective-permute-start(bf16[256,1024]{1,0:T(8,128)(2,1)} %get-tuple-element.130), channel_id=1, source_target_pairs={{0,24},{8,0},{16,8},{24,16},{1,25},{9,1},{17,9},{25,17},{2,26},{10... | collective-permute-start | bytes 1572872 | tf_op jit(solution)/shard_map/ppermute | solution.py:434
  842.1 60.8 %collective-permute-start.56 = (bf16[256,1024]{1,0:T(8,128)(2,1)}, bf16[256,1024]{1,0:T(8,128)(2,1)}, u32[]{:S(2)}, u32[]{:S(2)}) collective-permute-start(bf16[256,1024]{1,0:T(8,128)(2,1)} %get-tuple-element.131), channel_id=1, source_target_pairs={{0,16},{8,24},{16,0},{24,8},{1,17},{9,25},{17,1},{25,9},{2,18},{10... | collective-permute-start | bytes 1572872 | tf_op jit(solution)/shard_map/ppermute | solution.py:434
  842.2 96.4 %collective-permute-start.57 = (bf16[256,1024]{1,0:T(8,128)(2,1)}, bf16[256,1024]{1,0:T(8,128)(2,1)}, u32[]{:S(2)}, u32[]{:S(2)}) collective-permute-start(bf16[256,1024]{1,0:T(8,128)(2,1)} %get-tuple-element.132), channel_id=1, source_target_pairs={{0,8},{8,16},{16,24},{24,0},{1,9},{9,17},{17,25},{25,1},{2,10},{10... | collective-permute-start | bytes 1572872 | tf_op jit(solution)/shard_map/ppermute | solution.py:434
  (106 other events, 2708.2 us)
Sparse Core Ops, SparseCore 0:
  673.9 325.5 all-reduce.3

commit v2 on v1

--- a/solution.py
+++ b/solution.py
@@ -359,49 +359,96 @@
     )(zx, zx, zx, zx, zx, entering, gn, coef, taps, bc_taps, dt_par)
 
 
-def gather_row(x):
-    count = lax.axis_size("row")
-    if count != 4:
-        return lax.all_gather(x, "row", axis=0, tiled=True)
-    me = lax.axis_index("row")
-    size = x.shape[0]
-    flip = lambda v, bit: lax.ppermute(v, "row", [(i, i ^ bit) for i in range(4)])
-    from_x = flip(x, 1)
-    from_y = flip(x, 2)
-    cross_a = flip(from_y[: size // 2], 1)
-    cross_b = flip(from_x[size // 2 :], 2)
-    out = jnp.zeros((4 * size, x.shape[1]), x.dtype)
-    put = lambda o, v, bit, off: lax.dynamic_update_slice(o, v, ((me ^ bit) * size + off, 0))
-    out = put(out, x, 0, 0)
-    out = put(out, from_x, 1, 0)
-    out = put(out, from_y, 2, 0)
-    out = put(out, cross_a, 3, 0)
-    return put(out, cross_b, 3, size // 2)
-
-
-def scatter_row(x):
-    count = lax.axis_size("row")
-    if count != 4:
-        return lax.psum_scatter(x, "row", scatter_dimension=0, tiled=True).astype(F32)
-    me = lax.axis_index("row")
-    size, width = x.shape[0] // 4, x.shape[1]
-    half = width // 2
-    my_y, my_x = me // 2, me % 2
-    blocks = x.reshape(2, 2, size, width)
-    flip = lambda v, bit: lax.ppermute(v, "row", [(i, i ^ bit) for i in range(4)])
-    at_x = lambda i: lax.dynamic_slice(blocks, (0, i, 0, 0), (2, 1, size, half))[:, 0]
-    at_y = lambda i: lax.dynamic_slice(blocks, (i, 0, 0, half), (1, 2, size, half))[0]
-    got_x = flip(at_x(1 - my_x), 1)
-    got_y = flip(at_y(1 - my_y), 2)
-    pick = lambda v, i: lax.dynamic_index_in_dim(v, i, 0, keepdims=False).astype(F32)
-    keep_x, keep_y = at_x(my_x), at_y(my_y)
-    pass_x = (pick(keep_x, 1 - my_y) + pick(got_x, 1 - my_y)).astype(BF)
-    pass_y = (pick(keep_y, 1 - my_x) + pick(got_y, 1 - my_x)).astype(BF)
-    end_x = flip(pass_x, 2)
-    end_y = flip(pass_y, 1)
-    left = pick(keep_x, my_y) + pick(got_x, my_y) + end_x.astype(F32)
-    right = pick(keep_y, my_x) + pick(got_y, my_x) + end_y.astype(F32)
-    return jnp.concatenate([left, right], axis=1)
+def tie(value, *before):
+    return lax.optimization_barrier((value, *before))[0]
+
+
+def split(v, width):
+    rows = []
+    rest = v
+    for _ in range(3):
+        part = lax.reduce_precision(rest, 8, 7)
+        rows.append(part.astype(BF))
+        rest = rest - part
+    return jnp.pad(jnp.stack(rows), ((0, 13), (0, width - v.shape[0])))
+
+
+def joined(rows, size):
+    return jnp.sum(rows[:3, :size].astype(F32), axis=0)
+
+
+def flip(v, bit):
+    return lax.ppermute(v, "row", [(i, i ^ bit) for i in range(4)])
+
+
+class Scatter:
+    def __init__(self, x, small=None):
+        self.count = lax.axis_size("row")
+        self.x, self.small = x, small
+        if self.count != 4:
+            self.sent = (x,)
+            return
+        me = lax.axis_index("row")
+        self.size, width = x.shape[0] // 4, x.shape[1]
+        half = width // 2
+        self.half = half
+        self.my_y, self.my_x = me // 2, me % 2
+        blocks = x.reshape(2, 2, self.size, width)
+        self.at_x = lambda i: lax.dynamic_slice(blocks, (0, i, 0, 0), (2, 1, self.size, half))[:, 0]
+        self.at_y = lambda i: lax.dynamic_slice(blocks, (i, 0, 0, half), (1, 2, self.size, half))[0]
+        send_x = self.at_x(1 - self.my_x)
+        if small is not None:
+            pieces = small.reshape(2, 2, self.size)
+            there = lax.dynamic_index_in_dim(pieces, 1 - self.my_x, 1, keepdims=False)
+            self.here = lax.dynamic_index_in_dim(pieces, self.my_x, 1, keepdims=False)
+            send_x = jnp.concatenate(
+                [send_x, jnp.stack([split(there[0], half), split(there[1], half)])], axis=1
+            )
+        self.sent = (send_x, self.at_y(1 - self.my_y))
+
+    def first(self):
+        self.got = self.sent
+        if self.count == 4:
+            self.got = (flip(self.sent[0], 1), flip(self.sent[1], 2))
+
+    def second(self, *before):
+        if self.count != 4:
+            self.passed = self.ended = self.sent
+            return
+        got_x, got_y = tie(self.got, *before)
+        pick = lambda v, i: lax.dynamic_index_in_dim(v, i, 0, keepdims=False).astype(F32)
+        size = self.size
+        both_x = lambda i: pick(self.at_x(self.my_x), i) + pick(got_x[:, :size], i)
+        both_y = lambda i: pick(self.at_y(self.my_y), i) + pick(got_y, i)
+        pass_x = both_x(1 - self.my_y).astype(BF)
+        if self.small is not None:
+            little = lambda i: pick(self.here, i) + joined(
+                lax.dynamic_index_in_dim(got_x[:, size:], i, 0, keepdims=False), size
+            )
+            pass_x = jnp.concatenate([pass_x, split(little(1 - self.my_y), self.half)], axis=0)
+            self.little = little(self.my_y)
+        self.passed = (pass_x, both_y(1 - self.my_x).astype(BF))
+        self.left = both_x(self.my_y)
+        self.right = both_y(self.my_x)
+        self.ended = (flip(self.passed[0], 2), flip(self.passed[1], 1))
+
+    def last(self, *before):
+        if self.count != 4:
+            total = lax.psum_scatter(self.passed[0], "row", scatter_dimension=0, tiled=True).astype(F32)
+            little = None
+            if self.small is not None:
+                size = total.shape[0]
+                little = butterfly(self.small, "row")[0]
+                little = lax.dynamic_slice_in_dim(little, lax.axis_index("row") * size, size, 0)
+            return total, little
+        end_x, end_y = tie(self.ended, *before)
+        size = self.size
+        left = self.left + end_x[:size].astype(F32)
+        right = self.right + end_y.astype(F32)
+        little = None
+        if self.small is not None:
+            little = self.little + joined(end_x[size:], size)
+        return jnp.concatenate([left, right], axis=1), little
 
 
 def butterfly(v, axis):
@@ -413,31 +460,59 @@
     return v
 
 
+def sum_over_row_dp(v):
+    if lax.axis_size("row") != 4:
+        return lax.psum(butterfly(v, "row"), "dp")
+    me = lax.axis_index("row")
+    for bit in (1, 2):
+        size = v.shape[0] // 2
+        side = me // bit % 2
+        away = lax.dynamic_slice_in_dim(v, (1 - side) * size, size, 0)
+        keep = lax.dynamic_slice_in_dim(v, side * size, size, 0)
+        v = keep + flip(away, bit)
+    v = butterfly(v, "dp")
+    for bit in (2, 1):
+        other = flip(v, bit)
+        first = me // bit % 2 == 0
+        v = jnp.concatenate([jnp.where(first, v, other), jnp.where(first, other, v)], axis=0)
+    return v
+
+
 def other_col(v):
     return lax.ppermute(v, "col", [(0, 1), (1, 0)])
 
 
-def deal_back(rows, dest_group):
-    groups = lax.axis_size("dp")
-    me = lax.axis_index("dp")
-    col = lax.axis_index("col")
+def dealt_rows(rows):
     half = rows[0].shape[1] // 2
     own = jnp.stack([r[:, :half] for r in rows])
     got = other_col(jnp.stack([r[:, half:] for r in rows]))
-    first = jnp.where(col == 0, own, got)
-    second = jnp.where(col == 0, got, own)
-    dealt = jnp.concatenate([first, second], axis=0)
+    at_start = lax.axis_index("col") == 0
+    return jnp.concatenate([jnp.where(at_start, own, got), jnp.where(at_start, got, own)], axis=0)
+
+
+def sent_back(dealt):
+    groups = lax.axis_size("dp")
+    me = lax.axis_index("dp")
     parts = []
     for hop in range(groups):
         piece = lax.dynamic_index_in_dim(dealt, (me + hop) % groups, 0, keepdims=False)
         if hop:
             piece = lax.ppermute(piece, "dp", [(i, (i + hop) % groups) for i in range(groups)])
         parts.append(piece)
-    hops = ((me - dest_group) % groups)[:, None, None]
+    return parts
+
+
+def in_given_order(parts, dest_group):
+    groups = lax.axis_size("dp")
+    hops = ((lax.axis_index("dp") - dest_group) % groups)[:, None, None]
     out = jnp.where(hops == 0, parts[0][None], jnp.zeros((), BF))
     for hop in range(1, groups):
         out = jnp.where(hops == hop, parts[hop][None], out)
     return out
+
+
+def matmul(a, b, over_a, over_b):
+    return lax.dot_general(a, b, (((over_a,), (over_b,)), ((), ())), preferred_element_type=F32)
 
 
 def per_device(
@@ -473,24 +548,29 @@
 
     u_low = widened(hidden)
     gain = jnp.concatenate([norm_gain, other_col(norm_gain)])
-    in_own = jnp.concatenate(
-        [
-            gate_input_weight.reshape(width_col, wide),
-            auxiliary_weight[:, :aux],
-            lax.dynamic_slice_in_dim(auxiliary_weight, aux + row_index * heads, heads, 1),
-            jnp.zeros((width_col, steps - heads), BF),
-        ],
-        axis=1,
-    )
-    in_weight = jnp.concatenate([in_own, other_col(in_own)], axis=0)
-    out_own = output_weight.reshape(inner, width_col)
-    out_weight = jnp.concatenate([out_own, other_col(out_own)], axis=1)
-
     u = [u_low[k].astype(F32) for k in range(seq_col)]
     inv_rms = [lax.rsqrt(jnp.mean(v * v, axis=1, keepdims=True) + EPSILON) for v in u]
-    scaled = [
-        gather_row((v * r * gain[None, :]).astype(BF)) for v, r in zip(u, inv_rms, strict=True)
-    ]
+    spread = lambda v: lax.all_gather(v, "row", axis=0, tiled=True)
+    normed = [(v * r * gain[None, :]).astype(BF) for v, r in zip(u, inv_rms, strict=True)]
+    scaled = [spread(normed[0])]
+    for v in normed[1:]:
+        scaled.append(spread(tie(v, scaled[-1])))
+    in_own = tie(
+        jnp.concatenate(
+            [
+                gate_input_weight.reshape(width_col, wide),
+                auxiliary_weight[:, :aux],
+                lax.dynamic_slice_in_dim(auxiliary_weight, aux + row_index * heads, heads, 1),
+                jnp.zeros((width_col, steps - heads), BF),
+            ],
+            axis=1,
+        )
+    )
+    out_own = output_weight.reshape(inner, width_col)
+    in_weight = tie(jnp.concatenate([in_own, other_col(in_own)], axis=0))
+    out_weight = tie(jnp.concatenate([out_own, other_col(out_own)], axis=1))
+
+    scaled[0] = tie(scaled[0], in_weight)
 
     column = lambda v: v.reshape(-1, 1)
     taps = jnp.concatenate(
@@ -506,29 +586,18 @@
     bc_taps = jnp.concatenate([conv_bc.T, column(conv_bc_bias), jnp.zeros((aux, 3), F32)], axis=1)
     dt_par = jnp.pad(jnp.stack([dt_bias, a_log], axis=1), ((0, steps - heads), (0, 6)))
 
-    zx, gated, square, entering = [], [], [], []
-    for k in range(seq_col):
-        projected = lax.dot_general(
-            in_weight, scaled[k], (((0,), (1,)), ((), ())), preferred_element_type=F32
-        )
-        zx.append(projected)
-        g, s, e = scan_forward(projected, taps, bc_taps, dt_par, heads)
-        gated.append(g)
-        square.append(s)
-        entering.append(e)
-
     targets_own = widened(targets)
     positions = row_index * local_len + jnp.arange(local_len, dtype=jnp.int32)
+
+    zx, gated, entering, scatters = [], [], [], []
     result, g_result, g_rows, coef = [], [], [], []
     loss_part = jnp.zeros((), F32)
-    for k in range(seq_col):
-        part = lax.dot_general(
-            gated[k], out_weight, (((0,), (0,)), ((), ())), preferred_element_type=F32
-        ).astype(BF)
-        total_square = butterfly(square[k], "row")[0]
-        mine = lax.dynamic_slice_in_dim(total_square, row_index * local_len, local_len, 0)
-        gate_inv = lax.rsqrt(mine / inner_width + EPSILON)[:, None]
-        branch = scatter_row(part) * gate_inv
+
+    def finish(k, *before):
+        nonlocal loss_part
+        summed, total_square = scatters[k].last(*before)
+        gate_inv = lax.rsqrt(total_square / inner_width + EPSILON)[:, None]
+        branch = summed * gate_inv
         full = u[k] + branch
         valid = (positions < own_lengths[k]).astype(F32)[:, None]
         difference = (full - targets_own[k].astype(F32)) * valid
@@ -541,82 +610,127 @@
             jnp.zeros((local_len * row_count,), F32), share, row_index * local_len, 0
         )
         coef.append(butterfly(placed[None, :], "row"))
-        g_rows.append(gather_row((grad * gate_inv).astype(BF)))
-
-    output = deal_back(result, dest_group)
-
-    w_out_part = 0.0
-    g_in = []
+        sent = (grad * gate_inv).astype(BF)
+        g_rows.append(spread(tie(sent, *g_rows[-1:])))
+        return sent
+
+    for k in range(seq_col):
+        source = scaled[k] if k == 0 else tie(scaled[k], *scatters[-1].sent)
+        projected = matmul(in_weight, source, 0, 1)
+        if k > 0:
+            scatters[-1].second(projected)
+            projected = tie(projected, *scatters[-1].passed)
+        zx.append(projected)
+        g, square, e = scan_forward(projected, taps, bc_taps, dt_par, heads)
+        gated.append(g)
+        entering.append(e)
+        if k > 0:
+            g = tie(g, finish(k - 1, g))
+        part = matmul(g, out_weight, 0, 0).astype(BF)
+        scatters.append(Scatter(part, square))
+        scatters[-1].first()
+    scatters[-1].second()
+    finish(seq_col - 1)
+
+    g_in, scatters = [], []
     sums = [0.0, 0.0, 0.0]
     for k in range(seq_col):
-        gn = lax.dot_general(
-            out_weight, g_rows[k], (((1,), (1,)), ((), ())), preferred_element_type=F32
-        )
+        final = k == seq_col - 1
+        whole = g_rows[k] if k == 0 else tie(g_rows[k], g_in[-1], coef[k])
+        if k == 0:
+            dealt_output = dealt_rows(result)
+            output_parts = sent_back(dealt_output)
+        gn = matmul(out_weight, whole, 1, 1)
+        if final:
+            w_out_part = sum(
+                matmul(gated[i], whole if i == k else g_rows[i], 1, 0) for i in range(seq_col)
+            )
+            received = tie(other_col(w_out_part[:, width_col:].astype(BF)), gn)
+            w_out_low = (w_out_part[:, :width_col] + received.astype(F32)).astype(BF)
+            w_out_sum = lax.psum(w_out_low, "dp")
+            if k > 0:
+                scatters.append(Scatter(matmul(tie(g_in[-1], w_out_low), in_weight, 0, 1).astype(BF)))
+        elif k > 0:
+            scatters.append(Scatter(matmul(g_in[-1], in_weight, 0, 1).astype(BF)))
+        if k > 0:
+            scatters[-1].first()
+            gn = tie(gn, *scatters[-1].sent)
         g, gx, gbc, gdt = scan_backward(
             zx[k], entering[k], gn, coef[k], taps, bc_taps, dt_par, heads
         )
+        sums = [a + b for a, b in zip(sums, (gx, gbc, gdt), strict=True)]
+        if k == 0:
+            g = tie(g, *output_parts)
+        if k > 0:
+            scatters[-1].second(g)
+            g = tie(g, *scatters[-1].passed)
+        if final:
+            g = tie(g, w_out_sum)
         g_in.append(g)
-        sums = [a + b for a, b in zip(sums, (gx, gbc, gdt), strict=True)]
-        w_out_part = w_out_part + lax.dot_general(
-            gated[k], g_rows[k], (((1,), (0,)), ((), ())), preferred_element_type=F32
-        )
-    w_out_half = w_out_part[:, :width_col] + other_col(
-        w_out_part[:, width_col:].astype(BF)
-    ).astype(F32)
-    w_out_sum = lax.psum(w_out_half.astype(BF), "dp")
-
-    in_part = 0.0
+
+    scatters.append(Scatter(matmul(g_in[-1], in_weight, 0, 1).astype(BF)))
+    scatters[-1].first()
+    half_of = lambda start, g: sum(
+        matmul(scaled[i][:, start : start + width_col], g[i], 0, 1) for i in range(seq_col)
+    )
+    g_wide = [g[:wide] for g in g_in]
+    g_wide[-1] = tie(g_wide[-1], *scatters[-1].sent)
+    in_there = half_of(width_col, g_wide).astype(BF)
+    scatters[-1].second(in_there)
+    g_wide[-1] = tie(g_wide[-1], *scatters[-1].passed)
+    in_low = (half_of(0, g_wide) + other_col(in_there).astype(F32)).astype(BF)
+    in_low = tie(in_low.reshape(width_col, heads, pair))
+    w_zx = lax.psum(in_low, "dp")
+    g_aux = [g[wide:] for g in g_in]
+    g_aux[-1] = tie(g_aux[-1], in_low)
+    aux_part = sum(matmul(scaled[i], g_aux[i], 0, 1) for i in range(seq_col))
+    aux_half = aux_part[:width_col] + other_col(aux_part[width_col:])
+    aux_half = jnp.concatenate(
+        [
+            aux_half[:, :aux],
+            lax.dynamic_update_slice_in_dim(
+                jnp.zeros((width_col, head_total), F32),
+                aux_half[:, aux : aux + heads],
+                row_index * heads,
+                1,
+            ),
+        ],
+        axis=1,
+    )
+    w_aux = sum_over_row_dp(aux_half)
     gain_part = jnp.zeros((model_width,), F32)
     g_u = []
     for k in range(seq_col):
-        part = lax.dot_general(
-            g_in[k], in_weight, (((0,), (1,)), ((), ())), preferred_element_type=F32
-        ).astype(BF)
-        g_scaled = scatter_row(part)
+        g_scaled, _ = scatters[k].last()
         gain_part = gain_part + jnp.sum(g_scaled * u[k] * inv_rms[k], axis=0)
         weighted = g_scaled * gain[None, :]
         dot = jnp.sum(weighted * u[k], axis=1, keepdims=True) / model_width
         cube = inv_rms[k] * inv_rms[k] * inv_rms[k]
         g_u.append((g_result[k] + inv_rms[k] * weighted - u[k] * (cube * dot)).astype(BF))
-        in_part = in_part + lax.dot_general(
-            scaled[k], g_in[k], (((0,), (1,)), ((), ())), preferred_element_type=F32
-        )
-    in_half = in_part[:width_col] + other_col(in_part[width_col:].astype(BF)).astype(F32)
-    aux_half = jnp.concatenate(
-        [
-            in_half[:, wide : wide + aux],
-            lax.dynamic_update_slice_in_dim(
-                jnp.zeros((width_col, head_total), F32),
-                in_half[:, wide + aux : wide + aux + heads],
-                row_index * heads,
-                1,
-            ),
-        ],
-        axis=1,
-    )
-    w_aux = lax.psum(butterfly(aux_half.astype(BF), "row"), "dp")
-    w_zx = lax.psum(in_half[:, :wide].astype(BF), "dp")
-    hidden_grad = deal_back(g_u, dest_group)
+    hidden_parts = sent_back(tie(dealt_rows(g_u), w_zx))
 
     gx, gbc, gdt = sums
-    own = butterfly(
-        butterfly(jnp.concatenate([gx.reshape(-1), gdt[:, 1:3].reshape(-1)]), "col"), "dp"
-    )
-    shared = jnp.concatenate([gbc.reshape(-1), loss_part[None]])
-    shared = butterfly(butterfly(butterfly(shared, "col"), "row"), "dp")
-    gain_half = gain_part[:width_col] + other_col(gain_part[width_col:])
-    gain_sum = butterfly(butterfly(gain_half, "row"), "dp")
-
-    gx = own[: inner * 8].reshape(inner, 8)
-    gdt = own[inner * 8 :].reshape(steps, 2)
+    flat = jnp.concatenate(
+        [gx.reshape(-1), gdt[:, 1:3].reshape(-1), gbc.reshape(-1), loss_part[None]]
+    )
+    vector = jnp.concatenate([flat, gain_part[:width_col]]) + other_col(
+        jnp.concatenate([flat, gain_part[width_col:]])
+    )
+    own_size = inner * 8 + steps * 2
+    vector = jnp.concatenate([vector[:own_size], butterfly(vector[own_size:], "row")])
+    vector = butterfly(vector, "dp")
+    gx = vector[: inner * 8].reshape(inner, 8)
+    gdt = vector[inner * 8 : own_size].reshape(steps, 2)
+    shared = vector[own_size:]
     gbc = shared[: aux * 8].reshape(aux, 8)
     loss = shared[aux * 8] * 0.5 / valid_count
+    gain_sum = shared[aux * 8 + 1 :]
     return (
         loss,
-        output,
-        hidden_grad,
+        in_given_order(output_parts, dest_group),
+        in_given_order(hidden_parts, dest_group),
         gain_sum,
-        w_zx.astype(F32).reshape(width_col, heads, pair),
+        w_zx.astype(F32),
         w_aux.astype(F32),
         gx[:, :4].T.reshape(4, heads, head_dim),
         gx[:, 4].reshape(heads, head_dim),

time: 1020 us -> 838 us (0.82)
  starting transfers between devices: 121 us -> 42.5 us
  matrix products: 195 us -> 155 us
  local copies, waits for them, and re-layouts: 91.8 us -> 55 us
  waiting for transfers between devices: 357 us -> 335 us
    ppermute x22 -> x10, waiting for transfers between devices: 145 us -> 64.1 us  [butterfly(): v = v + lax.ppermute(v, axis, [(i, i ^ bit) for i in range(count)])]
    ppermute x38 -> x26, starting transfers between devices: 92.9 us -> 30.4 us  [the longest x20 21.4 us: flip(): return lax.ppermute(v, 'row', [(i, i ^ bit) for i in range(4)])]
    all_gather x0 -> x4, waiting for transfers between devices: none -> 44.1 us  [per_device(): spread = lambda v: lax.all_gather(v, 'row', axis=0, tiled=True)]
    dot_general x12 -> x16, matrix products: 195 us -> 155 us  [matmul(): lax.dot_general(a, b, (((over_a,), (over_b,)), ((), ())), preferred_eleme...]
    psum x1 -> x2, waiting for transfers between devices: 57.4 us -> 76.4 us  [the longest x1 62.1 us: per_device(): w_zx = lax.psum(in_low, 'dp')]
    ppermute x22 -> x10, starting transfers between devices: 26.3 us -> 10.1 us  [butterfly(): v = v + lax.ppermute(v, axis, [(i, i ^ bit) for i in range(count)])]
    concatenate x2 -> x11, other arithmetic: 0.88 us -> 14.8 us  [the longest x1 6.03 us: per_device(): in_weight = tie(jnp.concatenate([in_own, other_col(in_own)], axis=0))]
    dynamic_update_slice x16 -> x0, local copies, waits for them, and re-layouts: 13.3 us -> none  [gather_row(): lax.dynamic_update_slice(o, v, ((me ^ bit) * size + off, 0))]
  transfers between devices with their start and end apart: 71 -> 53, of which waited for: 29 -> 23; matrix products, arithmetic and copies ran while one was open for 31% -> 23% of each run, Pallas kernels for 9% -> 17%
where the time goes in v2:
time: 838 us; the launch traced here: 832 us
  waiting for transfers between devices  335 us (40%)
  matrix products  155 us (18%)
  Pallas kernels  142 us (17%)
  other arithmetic  83.1 us (10%)
  local copies, waits for them, and re-layouts  55 us (7%)
  starting transfers between devices  42.5 us (5%)
  between operations  20 us (2%)
    dot_general x16, matrix products, matmul(): lax.dot_general(a, b, (((over_a,), (over_b,)), ((), ())), preferred_eleme...  155 us
    ppermute x20, waiting for transfers between devices, flip(): return lax.ppermute(v, 'row', [(i, i ^ bit) for i in range(4)])  112 us
    pallas_call x2, Pallas kernels, scan_backward(): pl.pallas_call(body, grid=(count,), in_specs=[pl.BlockSpec((2 * inner, sp...  99.4 us
    ppermute x10, waiting for transfers between devices, butterfly(): v = v + lax.ppermute(v, axis, [(i, i ^ bit) for i in range(count)])  64.1 us
    psum x1, waiting for transfers between devices, per_device(): w_zx = lax.psum(in_low, 'dp')  62.1 us
    all_gather x4, waiting for transfers between devices, per_device(): spread = lambda v: lax.all_gather(v, 'row', axis=0, tiled=True)  44.1 us
    pallas_call x2, Pallas kernels, scan_forward(): pl.pallas_call(body, grid=(length // span,), in_specs=[pl.BlockSpec((2 *...  42.2 us
    ppermute x6, waiting for transfers between devices, sent_back(): lax.ppermute(piece, 'dp', [(i, (i + hop) % groups) for i in range(groups)])  36.2 us
  transfers between devices with their start and end apart: 53, of which 23 were waited for; matrix products, arithmetic and copies ran while one was open for 23% of the time, Pallas kernels for 17%

profile of v2, /device:TPU:0, one launch (start us, length us, event | category | flops | bytes accessed | tf_op | source)
XLA Modules:
  0.0 831.7 jit_solution(2794120837964621815)
XLA Ops:
  14.4 6.7 copy.61
  25.7 44.1 %all-gather.5.cloned.1.call-done = bf16[1024,2048]{1,0:T(8,128)(2,1)} async-done(((bf16[256,2048]{1,0:T(8,128)(2,1)}), bf16[1024,2048]{1,0:T(8,128)(2,1)}) %all-gather.5.cloned.1.call-update) | async-done | bytes 4194320 | tf_op jit(solution)/shard_map/all_gather | solution.py:553
  75.3 6.0 pad_maximum_fusion
  85.1 13.2 %fusion.154.zx_ref.bc_ref.dt_ref.zx_before_ref.bc_before_ref = f32[2320,1024]{1,0:T(8,128)} fusion(bf16[2048,2320]{0,1:T(8,128)(2,1)S(1)} %pad_maximum_fusion, bf16[1024,2048]{1,0:T(8,128)(2,1)S(1)} %copy-done.91), kind=kOutput, calls=%fused_computation.352 | convolution fusion | flops 9730785280 | bytes 23199744 | tf_op jit(solution)/shard_map/dot_general | solution.py:515
  98.3 21.5 %scan_forward.2 = (bf16[1024,1024]{1,0:T(8,128)(2,1)S(1)}, f32[1,1024]{1,0:T(1,128)S(1)}, bf16[2048,128]{1,0:T(8,128)(2,1)S(1)}) custom-call(f32[2320,1024]{1,0:T(8,128)} %fusion.154.zx_ref.bc_ref.dt_ref.zx_before_ref.bc_before_ref, f32[2320,1024]{1,0:T(8,128)} %fusion.154.zx_ref.bc_ref.dt_ref.zx_before_ref.bc_before_ref, ...), custom_call_target="tpu_custom_call" | custom-call | tf_op jit(solution)/shard_map/scan_forward/pallas_call | solution.py:276
  121.7 7.0 convolution_convert_fusion.3
  132.9 27.1 %fusion.155.zx_ref.bc_ref.dt_ref.zx_before_ref.bc_before_ref = f32[2320,1024]{1,0:T(8,128)} fusion(bf16[2048,2320]{0,1:T(8,128)(2,1)} %copy-done.16, bf16[1024,2048]{1,0:T(8,128)(2,1)} %all-gather.7.cloned.1.call-done), kind=kOutput, calls=%fused_computation.353 | convolution fusion | flops 9730785280 | bytes 23199744 | tf_op jit(solution)/shard_map/dot_general | solution.py:515
  172.5 20.7 %scan_forward.3 = (bf16[1024,1024]{1,0:T(8,128)(2,1)S(1)}, f32[1,1024]{1,0:T(1,128)S(1)}, bf16[2048,128]{1,0:T(8,128)(2,1)S(1)}) custom-call(f32[2320,1024]{1,0:T(8,128)} %fusion.155.zx_ref.bc_ref.dt_ref.zx_before_ref.bc_before_ref, f32[2320,1024]{1,0:T(8,128)} %fusion.155.zx_ref.bc_ref.dt_ref.zx_before_ref.bc_before_ref, ...), custom_call_target="tpu_custom_call" | custom-call | tf_op jit(solution)/shard_map/scan_forward/pallas_call | solution.py:276
  203.7 7.4 convolution_convert_fusion.2
  213.2 38.5 %collective-permute-done.12 = bf16[2,256,1024]{2,1,0:T(8,128)(2,1)S(1)} collective-permute-done((bf16[2,256,1024]{2,1,0:T(8,128)(2,1)S(1)}, bf16[2,256,1024]{2,1,0:T(8,128)(2,1)S(1)}, u32[]{:S(2)}, u32[]{:S(2)}) %collective-permute-start.12) | collective-permute-done | bytes 1048608 | tf_op jit(solution)/shard_map/ppermute | solution.py:381
  256.8 24.2 %collective-permute-done.14 = bf16[256,1024]{1,0:T(8,128)(2,1)S(1)} collective-permute-done((bf16[256,1024]{1,0:T(8,128)(2,1)S(1)}, bf16[256,1024]{1,0:T(8,128)(2,1)S(1)}, u32[]{:S(2)}, u32[]{:S(2)}) %collective-permute-start.14) | collective-permute-done | bytes 524320 | tf_op jit(solution)/shard_map/ppermute | solution.py:381
  308.8 6.1 fusion.156.gn_ref
  314.9 50.0 %scan_backward.2 = (bf16[2320,1024]{1,0:T(8,128)(2,1)}, f32[1024,8]{1,0:T(8,128)}, f32[256,8]{1,0:T(8,128)}, f32[16,128]{1,0:T(8,128)}) custom-call(f32[2320,1024]{1,0:T(8,128)} %fusion.154.zx_ref.bc_ref.dt_ref.zx_before_ref.bc_before_ref, f32[2320,1024]{1,0:T(8,128)} %fusion.154.zx_ref.bc_ref.dt_ref.zx_before_ref.bc_before_ref, ...), custom_call_target="tpu_custom_call" | custom-call | tf_op jit(solution)/shard_map/scan_backward/pallas_call | solution.py:319
  364.9 8.9 %fusion.158 = f32[1024,2048]{1,0:T(8,128)} fusion(bf16[1024,1024]{1,0:T(8,128)(2,1)S(1)} %get-tuple-element.64, bf16[1024,2048]{1,0:T(8,128)(2,1)} %all-gather.9.cloned.1.call-done), kind=kOutput, calls=%fused_computation.356 | convolution fusion | flops 4294967296 | bytes 14680064 | tf_op jit(solution)/shard_map/dot_general | solution.py:515
  373.8 9.9 %convolution_add_fusion = f32[1024,2048]{1,0:T(8,128)S(1)} fusion(f32[1024,2048]{1,0:T(8,128)} %fusion.158, bf16[1024,1024]{1,0:T(8,128)(2,1)} %copy-done.5, bf16[1024,2048]{1,0:T(8,128)(2,1)} %all-gather.11.cloned.1.call-done), kind=kOutput, calls=%fused_computation.21 | convolution fusion | flops 4297064448 | bytes 23068672 | tf_op jit(solution)/shard_map/dot_general | solution.py:515
  385.9 6.1 fusion.157.gn_ref
  394.2 15.6 %convolution_convert_fusion.1 = bf16[1024,2048]{1,0:T(8,128)(2,1)S(1)} fusion(bf16[2320,1024]{1,0:T(8,128)(2,1)} %get-tuple-element.87, bf16[2048,2320]{0,1:T(8,128)(2,1)} %copy-done.16), kind=kOutput, calls=%fused_computation.23 | convolution fusion | flops 9732882432 | bytes 18448384 | tf_op jit(solution)/shard_map/dot_general | solution.py:515
  412.9 49.4 %scan_backward.3 = (bf16[2320,1024]{1,0:T(8,128)(2,1)}, f32[1024,8]{1,0:T(8,128)}, f32[256,8]{1,0:T(8,128)}, f32[16,128]{1,0:T(8,128)}) custom-call(f32[2320,1024]{1,0:T(8,128)} %fusion.155.zx_ref.bc_ref.dt_ref.zx_before_ref.bc_before_ref, f32[2320,1024]{1,0:T(8,128)} %fusion.155.zx_ref.bc_ref.dt_ref.zx_before_ref.bc_before_ref, ...), custom_call_target="tpu_custom_call" | custom-call | tf_op jit(solution)/shard_map/scan_backward/pallas_call | solution.py:319
  463.8 14.3 %all-reduce.10.cloned.1.call-done = bf16[1024,1024]{1,0:T(8,128)(2,1)} async-done(((bf16[1024,1024]{1,0:T(8,128)(2,1)}), bf16[1024,1024]{1,0:T(8,128)(2,1)}) %all-reduce.10.cloned.1.call-update) | async-done | bytes 2097168 | tf_op jit(solution)/shard_map/psum | solution.py:650
  478.1 16.5 %convolution_convert_fusion = bf16[1024,2048]{1,0:T(8,128)(2,1)S(1)} fusion(bf16[2320,1024]{1,0:T(8,128)(2,1)} %get-tuple-element.100, bf16[2048,2320]{0,1:T(8,128)(2,1)} %copy-done.16), kind=kOutput, calls=%fused_computation.22 | convolution fusion | flops 9732882432 | bytes 18448384 | tf_op jit(solution)/shard_map/dot_general | solution.py:515
  500.3 6.8 fusion.22
  507.2 8.7 %add_convert_fusion.1 = bf16[1024,2048]{1,0:T(8,128)(2,1)} fusion(f32[1024,2048]{1,0:T(8,128)} %fusion.22, bf16[2320,1024]{1,0:T(8,128)(2,1)S(1)} %bitcast.341, bf16[1024,2048]{1,0:T(8,128)(2,1)S(1)} %copy-done.92), kind=kOutput, calls=%fused_computation.2 | convolution fusion | flops 4299161600 | bytes 18874368 | tf_op jit(solution)/shard_map/dot_general | solution.py:515
  522.7 30.5 %collective-permute-done.25 = bf16[256,1024]{1,0:T(8,128)(2,1)} collective-permute-done((bf16[256,1024]{1,0:T(8,128)(2,1)}, bf16[256,1024]{1,0:T(8,128)(2,1)}, u32[]{:S(2)}, u32[]{:S(2)}) %collective-permute-start.25) | collective-permute-done | bytes 524320 | tf_op jit(solution)/shard_map/ppermute | solution.py:381
  564.3 6.8 fusion.20
  576.8 8.6 %fusion = bf16[128,8,16,128]{3,1,2,0:T(8,128)(2,1)S(1)} fusion(bf16[1024,2048]{1,0:T(8,128)(2,1)} %collective-permute-done.36, f32[1024,2048]{1,0:T(8,128)} %fusion.20, bf16[2320,1024]{1,0:T(8,128)(2,1)S(1)} %bitcast.343, bf16[1024,2048]{1,0:T(8,128)(2,1)} %all-gather.5.cloned.1.call-done), kind=kOutput, calls=%fused_computation.16 | convolution fusion | flops 4303355904 | bytes 23068672 | tf_op jit(solution)/shard_map/dot_general | solution.py:515
  612.9 10.3 %collective-permute-done.41 = f32[512,320]{0,1:T(8,128)} collective-permute-done((f32[512,320]{0,1:T(8,128)}, f32[512,320]{0,1:T(8,128)}, u32[]{:S(2)}, u32[]{:S(2)}) %collective-permute-start.41) | collective-permute-done | bytes 655392 | tf_op jit(solution)/shard_map/ppermute | solution.py:381
  626.7 7.3 collective-permute-done.32
  637.3 29.4 %collective-permute-done.43 = f32[256,320]{0,1:T(8,128)S(1)} collective-permute-done((f32[256,320]{0,1:T(8,128)S(1)}, f32[256,320]{0,1:T(8,128)S(1)}, u32[]{:S(2)}, u32[]{:S(2)}) %collective-permute-start.43) | collective-permute-done | bytes 327712 | tf_op jit(solution)/shard_map/ppermute | solution.py:458
  675.4 21.4 %collective-permute-done.34 = f32[11297]{0:T(1024)S(1)} collective-permute-done((f32[11297]{0:T(1024)S(1)}, f32[11297]{0:T(1024)S(1)}, u32[]{:S(2)}, u32[]{:S(2)}) %collective-permute-start.34) | collective-permute-done | bytes 45220 | tf_op jit(solution)/shard_map/ppermute | solution.py:458
  710.4 62.1 %all-reduce.12.cloned.1.call-done = bf16[1024,16,128]{2,1,0:T(8,128)(2,1)} async-done(((bf16[1024,16,128]{2,1,0:T(8,128)(2,1)}), bf16[1024,16,128]{2,1,0:T(8,128)(2,1)}) %all-reduce.12.cloned.1.call-update) | async-done | bytes 4194320 | tf_op jit(solution)/shard_map/psum | solution.py:683
  783.5 14.5 %collective-permute-done.37 = bf16[256,1024]{1,0:T(8,128)(2,1)S(1)} collective-permute-done((bf16[256,1024]{1,0:T(8,128)(2,1)S(1)}, bf16[256,1024]{1,0:T(8,128)(2,1)S(1)}, u32[]{:S(2)}, u32[]{:S(2)}) %collective-permute-start.37) | collective-permute-done | bytes 524320 | tf_op jit(solution)/shard_map/ppermute | solution.py:500
  799.7 20.0 %collective-permute-done.38 = bf16[256,1024]{1,0:T(8,128)(2,1)S(1)} collective-permute-done((bf16[256,1024]{1,0:T(8,128)(2,1)S(1)}, bf16[256,1024]{1,0:T(8,128)(2,1)S(1)}, u32[]{:S(2)}, u32[]{:S(2)}) %collective-permute-start.38) | collective-permute-done | bytes 524320 | tf_op jit(solution)/shard_map/ppermute | solution.py:500
  (482 shorter events, 192.1 us)
Async XLA Ops:
  7.2 62.7 %all-gather.5.cloned.1.call-start = ((), (), s32[]{:S(2)}) async-start(), calls=%async_computation | async-start | bytes 5242880 | tf_op jit(solution)/shard_map/all_gather | solution.py:553
  14.4 118.5 %all-gather.7.cloned.1.call-start = ((), (), s32[]{:S(2)}) async-start(), calls=%async_computation.1 | async-start | bytes 5242880 | tf_op jit(solution)/shard_map/all_gather | solution.py:553
  25.2 50.1 %collective-permute-start = (bf16[1024,2320]{0,1:T(8,128)(2,1)}, bf16[1024,2320]{0,1:T(8,128)(2,1)}, u32[]{:S(2)}, u32[]{:S(2)}) collective-permute-start(bf16[1024,2320]{0,1:T(8,128)(2,1)} %pad_maximum_fusion.1), channel_id=1, source_target_pairs={{0,1},{1,0},{2,3},{3,2},{4,5},{5,4},{6,7},{7,6},{8,9},{9,8},{10,11... | collective-permute-start | bytes 14254088 | tf_op jit(solution)/shard_map/ppermute | solution.py:482
  25.6 45.5 %collective-permute-start.3 = (bf16[1024,1024]{1,0:T(8,128)(2,1)}, bf16[1024,1024]{1,0:T(8,128)(2,1)S(1)}, u32[]{:S(2)}, u32[]{:S(2)}) collective-permute-start(bf16[1024,1024]{1,0:T(8,128)(2,1)} %bitcast.8), channel_id=1, source_target_pairs={{0,1},{1,0},{2,3},{3,2},{4,5},{5,4},{6,7},{7,6},{8,9},{9,8},{10,11... | collective-permute-start | bytes 6291464 | tf_op jit(solution)/shard_map/ppermute | solution.py:482
  69.9 218.8 %all-gather.9.cloned.1.call-start = ((), (), s32[]{:S(2)}) async-start(), calls=%async_computation.2 | async-start | bytes 5242880 | tf_op jit(solution)/shard_map/all_gather | solution.py:553
  129.9 30.1 %collective-permute-start.5 = (bf16[2,256,1024]{2,1,0:T(8,128)(2,1)}, bf16[2,256,1024]{2,1,0:T(8,128)(2,1)}, u32[]{:S(2)}, u32[]{:S(2)}) collective-permute-start(bf16[2,256,1024]{2,1,0:T(8,128)(2,1)} %dynamic-slice_bitcast_fusion.6), channel_id=1, source_target_pairs={{0,4},{2,6},{4,0},{6,2},{1,5},{3,7},{5,1},{7,3},{8,12},{10,14},{12... | collective-permute-start | bytes 3145736 | tf_op jit(solution)/shard_map/ppermute | solution.py:381
  132.1 27.9 %collective-permute-start.4 = (bf16[2,272,1024]{2,1,0:T(8,128)(2,1)}, bf16[2,272,1024]{2,1,0:T(8,128)(2,1)}, u32[]{:S(2)}, u32[]{:S(2)}) collective-permute-start(bf16[2,272,1024]{2,1,0:T(8,128)(2,1)} %maximum_maximum_fusion), channel_id=1, source_target_pairs={{0,2},{2,0},{4,6},{6,4},{1,3},{3,1},{5,7},{7,5},{8,10},{10,8},{12,... | collective-permute-start | bytes 3342344 | tf_op jit(solution)/shard_map/ppermute | solution.py:381
  165.9 27.4 %collective-permute-start.7 = (bf16[256,1024]{1,0:T(8,128)(2,1)}, bf16[256,1024]{1,0:T(8,128)(2,1)}, u32[]{:S(2)}, u32[]{:S(2)}) collective-permute-start(bf16[256,1024]{1,0:T(8,128)(2,1)} %get-tuple-element.199), channel_id=1, source_target_pairs={{0,2},{2,0},{4,6},{6,4},{1,3},{3,1},{5,7},{7,5},{8,10},{10,8},{12,... | collective-permute-start | bytes 1572872 | tf_op jit(solution)/shard_map/ppermute | solution.py:381
  167.2 26.1 %collective-permute-start.6 = (bf16[272,1024]{1,0:T(8,128)(2,1)S(1)}, bf16[272,1024]{1,0:T(8,128)(2,1)}, u32[]{:S(2)}, u32[]{:S(2)}) collective-permute-start(bf16[272,1024]{1,0:T(8,128)(2,1)S(1)} %pad_maximum_fusion.14), channel_id=1, source_target_pairs={{0,4},{2,6},{4,0},{6,2},{1,5},{3,7},{5,1},{7,3},{8,12},{10,14},{12... | collective-permute-start | bytes 1671176 | tf_op jit(solution)/shard_map/ppermute | solution.py:381
  169.8 26.7 %collective-permute-start.8 = (bf16[2,256,1024]{2,1,0:T(8,128)(2,1)}, bf16[2,256,1024]{2,1,0:T(8,128)(2,1)}, u32[]{:S(2)}, u32[]{:S(2)}) collective-permute-start(bf16[2,256,1024]{2,1,0:T(8,128)(2,1)} %get-tuple-element.216), channel_id=1, source_target_pairs={{0,1},{1,0},{2,3},{3,2},{4,5},{5,4},{6,7},{7,6},{8,9},{9,8},{10,11... | collective-permute-start | bytes 3145736 | tf_op jit(solution)/shard_map/ppermute | solution.py:482
  202.5 171.3 %all-gather.11.cloned.1.call-start = ((), (), s32[]{:S(2)}) async-start(), calls=%async_computation.3 | async-start | bytes 5242880 | tf_op jit(solution)/shard_map/all_gather | solution.py:553
  211.3 42.1 %collective-permute-start.11 = (bf16[2,272,1024]{2,1,0:T(8,128)(2,1)S(1)}, bf16[2,272,1024]{2,1,0:T(8,128)(2,1)S(1)}, u32[]{:S(2)}, u32[]{:S(2)}) collective-permute-start(bf16[2,272,1024]{2,1,0:T(8,128)(2,1)S(1)} %maximum_maximum_fusion.1), channel_id=1, source_target_pairs={{0,2},{2,0},{4,6},{6,4},{1,3},{3,1},{5,7},{7,5},{8,10},{10,8},{12,... | collective-permute-start | bytes 3342344 | tf_op jit(solution)/shard_map/ppermute | solution.py:381
  212.2 39.6 %collective-permute-start.12 = (bf16[2,256,1024]{2,1,0:T(8,128)(2,1)S(1)}, bf16[2,256,1024]{2,1,0:T(8,128)(2,1)S(1)}, u32[]{:S(2)}, u32[]{:S(2)}) collective-permute-start(bf16[2,256,1024]{2,1,0:T(8,128)(2,1)S(1)} %dynamic-slice_bitcast_fusion.4), channel_id=1, source_target_pairs={{0,4},{2,6},{4,0},{6,2},{1,5},{3,7},{5,1},{7,3},{8,12},{10,14},{12... | collective-permute-start | bytes 3145736 | tf_op jit(solution)/shard_map/ppermute | solution.py:381
  254.0 27.0 %collective-permute-start.13 = (bf16[272,1024]{1,0:T(8,128)(2,1)S(1)}, bf16[272,1024]{1,0:T(8,128)(2,1)S(1)}, u32[]{:S(2)}, u32[]{:S(2)}) collective-permute-start(bf16[272,1024]{1,0:T(8,128)(2,1)S(1)} %pad_maximum_fusion.15), channel_id=1, source_target_pairs={{0,4},{2,6},{4,0},{6,2},{1,5},{3,7},{5,1},{7,3},{8,12},{10,14},{12... | collective-permute-start | bytes 1671176 | tf_op jit(solution)/shard_map/ppermute | solution.py:381
  288.7 189.4 %all-reduce.10.cloned.1.call-start = ((), (), s32[]{:S(2)}) async-start(), calls=%async_computation.4 | async-start | bytes 4194304 | tf_op jit(solution)/shard_map/psum | solution.py:650
  303.3 61.6 %collective-permute-start.16 = (bf16[256,1024]{1,0:T(8,128)(2,1)S(1)}, bf16[256,1024]{1,0:T(8,128)(2,1)}, u32[]{:S(2)}, u32[]{:S(2)}) collective-permute-start(bf16[256,1024]{1,0:T(8,128)(2,1)S(1)} %get-tuple-element.210), channel_id=1, source_target_pairs={{0,8},{8,16},{16,24},{24,0},{1,9},{9,17},{17,25},{25,1},{2,10},{10... | collective-permute-start | bytes 1572872 | tf_op jit(solution)/shard_map/ppermute | solution.py:500
  305.0 59.9 %collective-permute-start.17 = (bf16[256,1024]{1,0:T(8,128)(2,1)S(1)}, bf16[256,1024]{1,0:T(8,128)(2,1)}, u32[]{:S(2)}, u32[]{:S(2)}) collective-permute-start(bf16[256,1024]{1,0:T(8,128)(2,1)S(1)} %get-tuple-element.211), channel_id=1, source_target_pairs={{0,16},{8,24},{16,0},{24,8},{1,17},{9,25},{17,1},{25,9},{2,18},{10... | collective-permute-start | bytes 1572872 | tf_op jit(solution)/shard_map/ppermute | solution.py:500
  307.4 57.5 %collective-permute-start.18 = (bf16[256,1024]{1,0:T(8,128)(2,1)S(1)}, bf16[256,1024]{1,0:T(8,128)(2,1)}, u32[]{:S(2)}, u32[]{:S(2)}) collective-permute-start(bf16[256,1024]{1,0:T(8,128)(2,1)S(1)} %get-tuple-element.212), channel_id=1, source_target_pairs={{0,24},{8,0},{16,8},{24,16},{1,25},{9,1},{17,9},{25,17},{2,26},{10... | collective-permute-start | bytes 1572872 | tf_op jit(solution)/shard_map/ppermute | solution.py:500
  394.1 378.3 %all-reduce.12.cloned.1.call-start = ((), (), s32[]{:S(2)}) async-start(), calls=%async_computation.5 | async-start | bytes 8388608 | tf_op jit(solution)/shard_map/psum | solution.py:683
  411.2 51.1 %collective-permute-start.22 = (bf16[2,256,1024]{2,1,0:T(8,128)(2,1)}, bf16[2,256,1024]{2,1,0:T(8,128)(2,1)S(1)}, u32[]{:S(2)}, u32[]{:S(2)}) collective-permute-start(bf16[2,256,1024]{2,1,0:T(8,128)(2,1)} %dynamic-slice_bitcast_fusion.3), channel_id=1, source_target_pairs={{0,2},{2,0},{4,6},{6,4},{1,3},{3,1},{5,7},{7,5},{8,10},{10,8},{12,... | collective-permute-start | bytes 3145736 | tf_op jit(solution)/shard_map/ppermute | solution.py:381
  411.7 50.6 %collective-permute-start.23 = (bf16[2,256,1024]{2,1,0:T(8,128)(2,1)S(1)}, bf16[2,256,1024]{2,1,0:T(8,128)(2,1)S(1)}, u32[]{:S(2)}, u32[]{:S(2)}) collective-permute-start(bf16[2,256,1024]{2,1,0:T(8,128)(2,1)S(1)} %dynamic-slice_bitcast_fusion.2), channel_id=1, source_target_pairs={{0,4},{2,6},{4,0},{6,2},{1,5},{3,7},{5,1},{7,3},{8,12},{10,14},{12... | collective-permute-start | bytes 3145736 | tf_op jit(solution)/shard_map/ppermute | solution.py:381
  515.9 60.8 %collective-permute-start.36 = (bf16[1024,2048]{1,0:T(8,128)(2,1)}, bf16[1024,2048]{1,0:T(8,128)(2,1)}, u32[]{:S(2)}, u32[]{:S(2)}) collective-permute-start(bf16[1024,2048]{1,0:T(8,128)(2,1)} %add_convert_fusion.1), channel_id=1, source_target_pairs={{0,1},{1,0},{2,3},{3,2},{4,5},{5,4},{6,7},{7,6},{8,9},{9,8},{10,11... | collective-permute-start | bytes 12582920 | tf_op jit(solution)/shard_map/ppermute | solution.py:482
  516.0 44.2 %collective-permute-start.26 = (bf16[2,256,1024]{2,1,0:T(8,128)(2,1)}, bf16[2,256,1024]{2,1,0:T(8,128)(2,1)S(1)}, u32[]{:S(2)}, u32[]{:S(2)}) collective-permute-start(bf16[2,256,1024]{2,1,0:T(8,128)(2,1)} %dynamic-slice_bitcast_fusion.1), channel_id=1, source_target_pairs={{0,2},{2,0},{4,6},{6,4},{1,3},{3,1},{5,7},{7,5},{8,10},{10,8},{12,... | collective-permute-start | bytes 3145736 | tf_op jit(solution)/shard_map/ppermute | solution.py:381
  517.6 42.7 %collective-permute-start.27 = (bf16[2,256,1024]{2,1,0:T(8,128)(2,1)}, bf16[2,256,1024]{2,1,0:T(8,128)(2,1)}, u32[]{:S(2)}, u32[]{:S(2)}) collective-permute-start(bf16[2,256,1024]{2,1,0:T(8,128)(2,1)} %dynamic-slice_bitcast_fusion), channel_id=1, source_target_pairs={{0,4},{2,6},{4,0},{6,2},{1,5},{3,7},{5,1},{7,3},{8,12},{10,14},{12... | collective-permute-start | bytes 3145736 | tf_op jit(solution)/shard_map/ppermute | solution.py:381
  519.1 34.1 %collective-permute-start.25 = (bf16[256,1024]{1,0:T(8,128)(2,1)}, bf16[256,1024]{1,0:T(8,128)(2,1)}, u32[]{:S(2)}, u32[]{:S(2)}) collective-permute-start(bf16[256,1024]{1,0:T(8,128)(2,1)} %get-tuple-element.191), channel_id=1, source_target_pairs={{0,2},{2,0},{4,6},{6,4},{1,3},{3,1},{5,7},{7,5},{8,10},{10,8},{12,... | collective-permute-start | bytes 1572872 | tf_op jit(solution)/shard_map/ppermute | solution.py:381
  519.4 35.0 %collective-permute-start.24 = (bf16[256,1024]{1,0:T(8,128)(2,1)S(1)}, bf16[256,1024]{1,0:T(8,128)(2,1)}, u32[]{:S(2)}, u32[]{:S(2)}) collective-permute-start(bf16[256,1024]{1,0:T(8,128)(2,1)S(1)} %get-tuple-element.192), channel_id=1, source_target_pairs={{0,4},{2,6},{4,0},{6,2},{1,5},{3,7},{5,1},{7,3},{8,12},{10,14},{12... | collective-permute-start | bytes 1572872 | tf_op jit(solution)/shard_map/ppermute | solution.py:381
  634.0 32.7 %collective-permute-start.43 = (f32[256,320]{0,1:T(8,128)S(1)}, f32[256,320]{0,1:T(8,128)S(1)}, u32[]{:S(2)}, u32[]{:S(2)}) collective-permute-start(f32[256,320]{0,1:T(8,128)S(1)} %dynamic-slice_add_fusion), channel_id=1, source_target_pairs={{0,8},{8,0},{16,24},{24,16},{1,9},{9,1},{17,25},{25,17},{2,10},{10... | collective-permute-start | bytes 983048 | tf_op jit(solution)/shard_map/ppermute | solution.py:458
  634.2 37.0 %collective-permute-start.33 = (f32[11297]{0:T(1024)S(1)}, f32[11297]{0:T(1024)S(1)}, u32[]{:S(2)}, u32[]{:S(2)}) collective-permute-start(f32[11297]{0:T(1024)S(1)} %pad_maximum_fusion.16), channel_id=1, source_target_pairs={{0,8},{8,0},{16,24},{24,16},{1,9},{9,1},{17,25},{25,17},{2,10},{10... | collective-permute-start | bytes 135572 | tf_op jit(solution)/shard_map/ppermute | solution.py:458
  637.3 71.6 %collective-permute-start.35 = (bf16[2,256,1024]{2,1,0:T(8,128)(2,1)}, bf16[2,256,1024]{2,1,0:T(8,128)(2,1)}, u32[]{:S(2)}, u32[]{:S(2)}) collective-permute-start(bf16[2,256,1024]{2,1,0:T(8,128)(2,1)} %pad_maximum_fusion.12), channel_id=1, source_target_pairs={{0,1},{1,0},{2,3},{3,2},{4,5},{5,4},{6,7},{7,6},{8,9},{9,8},{10,11... | collective-permute-start | bytes 3145736 | tf_op jit(solution)/shard_map/ppermute | solution.py:482
  666.7 30.3 %collective-permute-start.44 = (f32[256,320]{0,1:T(8,128)S(1)}, f32[256,320]{0,1:T(8,128)S(1)}, u32[]{:S(2)}, u32[]{:S(2)}) collective-permute-start(f32[256,320]{0,1:T(8,128)S(1)} %add.710), channel_id=1, source_target_pairs={{0,16},{8,24},{16,0},{24,8},{1,17},{9,25},{17,1},{25,9},{2,18},{10... | collective-permute-start | bytes 983048 | tf_op jit(solution)/shard_map/ppermute | solution.py:458
  707.5 69.4 %collective-permute-start.46 = (f32[512,320]{0,1:T(8,128)}, f32[512,320]{0,1:T(8,128)}, u32[]{:S(2)}, u32[]{:S(2)}) collective-permute-start(f32[512,320]{0,1:T(8,128)} %pad_maximum_fusion.13), channel_id=1, source_target_pairs={{0,2},{2,0},{4,6},{6,4},{1,3},{3,1},{5,7},{7,5},{8,10},{10,8},{12,... | collective-permute-start | bytes 1966088 | tf_op jit(solution)/shard_map/ppermute | solution.py:381
  774.8 45.0 %collective-permute-start.38 = (bf16[256,1024]{1,0:T(8,128)(2,1)S(1)}, bf16[256,1024]{1,0:T(8,128)(2,1)S(1)}, u32[]{:S(2)}, u32[]{:S(2)}) collective-permute-start(bf16[256,1024]{1,0:T(8,128)(2,1)S(1)} %get-tuple-element.206), channel_id=1, source_target_pairs={{0,16},{8,24},{16,0},{24,8},{1,17},{9,25},{17,1},{25,9},{2,18},{10... | collective-permute-start | bytes 1572872 | tf_op jit(solution)/shard_map/ppermute | solution.py:500
  (125 other events, 1717.1 us)
Sparse Core Ops, SparseCore 0:
  14.5 55.3 all-gather.4
  72.3 52.6 all-gather.6
  202.6 79.4 all-gather.8
  288.8 52.6 all-gather.10
  394.3 83.7 all-reduce.9
  602.6 169.8 all-reduce.11

commit v3 on v2

--- a/solution.py
+++ b/solution.py
@@ -9,6 +9,8 @@
 BF = jnp.bfloat16
 F32 = jnp.float32
 SPAN = 512
+PART = 128
+LOG2E = 1.4426950408889634
 EDGE = 128
 EPSILON = 1e-05
 
@@ -39,90 +41,148 @@
     return jnp.maximum(v, 0.0) + jnp.log1p(jnp.exp(-jnp.abs(v)))
 
 
-def shifted(before, now):
-    joined = jnp.concatenate([before, now], axis=1)
-    return [now] + [pltpu.roll(joined, k, 1)[:, EDGE:] for k in (1, 2, 3)]
-
-
-def ahead(now, after):
-    joined = jnp.concatenate([now, after], axis=1)
-    size = joined.shape[1]
-    return [now] + [pltpu.roll(joined, size - k, 1)[:, : now.shape[1]] for k in (1, 2, 3)]
-
-
-def conv_of(shifts, taps):
-    total = taps[:, 4:5] + taps[:, 3:4] * shifts[0]
-    for k in (1, 2, 3):
-        total = total + taps[:, 3 - k : 4 - k] * shifts[k]
+def wide(v, span):
+    return jnp.concatenate([v] * (span // v.shape[1]), axis=1)
+
+
+def taps_at(taps_ref, at, span):
+    return lambda k: wide(taps_ref[k, at, :], span)
+
+
+def spread_taps(from_ref, to_ref):
+    for k in range(to_ref.shape[0]):
+        to_ref[k] = jnp.broadcast_to(from_ref[:, k : k + 1], to_ref.shape[1:])
+
+
+def move_matrix(ahead):
+    rows = lax.broadcasted_iota(jnp.int32, (2 * EDGE, EDGE), 0)
+    cols = lax.broadcasted_iota(jnp.int32, (2 * EDGE, EDGE), 1)
+    moves = [rows == (cols + k if ahead else cols + EDGE - k) for k in (1, 2, 3)]
+    return jnp.concatenate([m.astype(F32).astype(BF) for m in moves], axis=1)
+
+
+def moved(joined, matrix):
+    size = joined.shape[0]
+    parts = range(joined.shape[1] // EDGE - 1)
+    low = joined.astype(BF)
+    stacked = jnp.concatenate([low[:, q * EDGE : (q + 2) * EDGE] for q in parts], axis=0)
+    out = nn(stacked, matrix)
+    return [
+        jnp.concatenate(
+            [out[q * size : (q + 1) * size, k * EDGE : (k + 1) * EDGE] for q in parts], axis=1
+        )
+        for k in range(3)
+    ]
+
+
+def conv_of(before, now, tap, matrix):
+    one, two, three = moved(jnp.concatenate([before, now], axis=1), matrix)
+    return tap(4) + tap(3) * now + tap(2) * one + tap(1) * two + tap(0) * three
+
+
+def conv_back(now, after, tap, matrix):
+    one, two, three = moved(jnp.concatenate([now, after], axis=1), matrix)
+    return tap(3) * now + tap(2) * one + tap(1) * two + tap(0) * three, (one, two, three)
+
+
+def fold(v):
+    total = v[:, :EDGE]
+    for k in range(1, v.shape[1] // EDGE):
+        total = total + v[:, k * EDGE : (k + 1) * EDGE]
     return total
 
 
-def span_common(bc_before, bc_now, dt_raw, bc_taps, dt_par):
-    shifts = shifted(bc_before, bc_now)
-    pre = conv_of(shifts, bc_taps)
+def lanes(q):
+    return slice(q * PART, (q + 1) * PART)
+
+
+def span_common(bc_before, bc_now, dt_raw, bc_tap, dt_par, matrix):
+    pre = conv_of(bc_before, bc_now, bc_tap, matrix)
     sig = sigmoid(pre)
     act = pre * sig
     half = act.shape[0] // 2
     b_t = act[:half].astype(BF)
     c_t = act[half:].astype(BF)
-    span = bc_now.shape[1]
-    rows = lax.broadcasted_iota(jnp.int32, (span, span), 0)
-    cols = lax.broadcasted_iota(jnp.int32, (span, span), 1)
+    parts = range(bc_now.shape[1] // PART)
+    rows = lax.broadcasted_iota(jnp.int32, (PART, PART), 0)
+    cols = lax.broadcasted_iota(jnp.int32, (PART, PART), 1)
     causal = rows <= cols
     steps = softplus(dt_raw + dt_par[:, 0:1])
     rate = -jnp.exp(dt_par[:, 1:2])
-    decay = exact(steps * rate, causal.astype(F32))
-    return shifts, pre, sig, b_t, c_t, causal, steps, rate, decay
+    gone = steps * (rate * LOG2E)
+    decay = [exact(gone[:, lanes(q)], causal.astype(F32)) for q in parts]
+    last = [d[:, PART - 1 :] for d in decay]
+    decay_n = [d.T for d in decay]
+    left = jnp.concatenate([jnp.exp2(e - d) for e, d in zip(last, decay)], axis=1)
+    kept = [jnp.exp2(e) for e in last]
+    decay = jnp.concatenate(decay, axis=1)
+    grown = jnp.exp2(decay)
+    b_n = [b_t[:, lanes(q)].astype(F32).T.astype(BF) for q in parts]
+    scores = [jnp.where(causal, nn(b_n[q], c_t[:, lanes(q)]), 0.0) for q in parts]
+    return pre, sig, b_t, c_t, b_n, scores, causal, steps, rate, decay, decay_n, grown, left, kept
 
 
 def forward_kernel(
     heads, zx_ref, bc_ref, dt_ref, taps_ref, bc_taps_ref, dt_par_ref,
     gated_ref, square_ref, enter_ref,
-    state, x_tail, bc_tail, carry, tailed,
+    state, x_tail, bc_tail, carry, x_all, xd_all, tailed, scores_all, x_taps, bc_taps, matrix_ref,
 ):
     span = zx_ref.shape[1]
-    size = zx_ref.shape[0] // heads // 2
+    inner = state.shape[0]
+    size = inner // heads
+    parts = range(span // PART)
 
     @pl.when(pl.program_id(0) == 0)
     def _():
         state[...] = jnp.zeros_like(state)
         x_tail[...] = jnp.zeros_like(x_tail)
         bc_tail[...] = jnp.zeros_like(bc_tail)
-
+        spread_taps(taps_ref, x_taps)
+        spread_taps(bc_taps_ref, bc_taps)
+        matrix_ref[...] = move_matrix(False)
+
+    matrix = matrix_ref[...]
     bc_now = bc_ref[...]
-    _, _, _, b_t, c_t, causal, steps, rate, decay = span_common(
-        bc_tail[...], bc_now, dt_ref[...], bc_taps_ref[...], dt_par_ref[...]
+    _, _, _, c_t, b_n, scores, _, steps, _, decay, decay_n, grown, left, kept = span_common(
+        bc_tail[...], bc_now, dt_ref[...], taps_at(bc_taps, slice(None), span), dt_par_ref[...], matrix
     )
     bc_tail[...] = bc_now[:, span - EDGE :]
-    b_n = b_t.astype(F32).T.astype(BF)
-    scores = jnp.where(causal, nn(b_n, c_t), 0.0)
-    decay_n = decay.T
-    grown = jnp.exp(decay)
-    last = decay[:, span - 1 : span]
-    left = jnp.exp(last - decay)
-    kept = jnp.exp(last)
-    entering = state[...].astype(BF)
-    enter_ref[...] = entering
-    carry[...] = nn(entering, c_t)
+    for q in parts:
+        scores_all[q] = scores[q]
+    for h in range(heads):
+        at = slice(h * size, (h + 1) * size)
+        x_raw = zx_ref[(2 * h + 1) * size : (2 * h + 2) * size, :]
+        pre = conv_of(x_tail[at, :], x_raw, taps_at(x_taps, at, span), matrix)
+        x_tail[at, :] = x_raw[:, span - EDGE :]
+        x = pre * sigmoid(pre)
+        xd = x * steps[h : h + 1, :]
+        x_all[at, :] = x
+        xd_all[at, :] = xd.astype(BF)
+        tailed[at, :] = (xd * left[h : h + 1, :]).astype(BF)
+    for q in parts:
+        entering = state[...].astype(BF)
+        enter_ref[q * inner : (q + 1) * inner, :] = entering
+        carry[:, lanes(q)] = nn(entering, c_t[:, lanes(q)])
+        more = nn(tailed[:, lanes(q)], b_n[q])
+        for h in range(heads):
+            at = slice(h * size, (h + 1) * size)
+            state[at, :] = state[at, :] * kept[q][h : h + 1, :] + more[at, :]
     square = jnp.zeros((size, span), F32)
     for h in range(heads):
         at = slice(h * size, (h + 1) * size)
         z = zx_ref[2 * h * size : (2 * h + 1) * size, :]
-        x_raw = zx_ref[(2 * h + 1) * size : (2 * h + 2) * size, :]
-        taps = taps_ref[at, :]
-        pre = conv_of(shifted(x_tail[at, :], x_raw), taps)
-        x_tail[at, :] = x_raw[:, span - EDGE :]
-        x = pre * sigmoid(pre)
-        xd = x * steps[h : h + 1, :]
-        mixing = scores * jnp.exp(jnp.minimum(decay[h : h + 1, :] - decay_n[:, h : h + 1], 0.0))
-        y = nn(xd.astype(BF), mixing.astype(BF)) + carry[at, :] * grown[h : h + 1, :] + taps[:, 5:6] * x
-        tailed[at, :] = (xd * left[h : h + 1, :]).astype(BF)
+        tap = taps_at(x_taps, at, span)
+        mixed = []
+        for q in parts:
+            gap = decay[h : h + 1, lanes(q)] - decay_n[q][:, h : h + 1]
+            mixing = scores_all[q] * jnp.exp2(jnp.minimum(gap, 0.0))
+            mixed.append(nn(xd_all[at, lanes(q)], mixing.astype(BF)))
+        y = jnp.concatenate(mixed, axis=1) + carry[at, :] * grown[h : h + 1, :]
+        y = y + tap(5) * x_all[at, :]
         gated = y * (z * sigmoid(z))
         square = square + gated * gated
-        gated_ref[at, :] = (gated * taps[:, 6:7]).astype(BF)
-        state[at, :] = state[at, :] * kept[h : h + 1, :]
+        gated_ref[at, :] = (gated * tap(6)).astype(BF)
     square_ref[...] = jnp.sum(square, axis=0, keepdims=True)
-    state[...] = state[...] + nn(tailed[...], b_n)
 
 
 def backward_kernel(
@@ -130,11 +190,15 @@
     taps_ref, bc_taps_ref, dt_par_ref,
     gzx_ref, gx_sum_ref, gbc_sum_ref, gdt_sum_ref,
     dstate, x_head, bc_head, carry, from_state, grown_g, tailed, x_acc, bc_acc, dt_acc, rsum, dsum,
+    x_all, slope_all, dxd_all, gy_all, scores_all, dscores_all, held_all, x_taps, bc_taps_all, matrix_ref,
+    back_matrix_ref,
 ):
     span = zx_ref.shape[1]
-    size = zx_ref.shape[0] // heads // 2
+    inner = dstate.shape[0]
+    size = inner // heads
     half = bc_ref.shape[0] // 2
     wide = zx_ref.shape[0]
+    parts = range(span // PART)
     step = pl.program_id(0)
     count = pl.num_programs(0)
     first = step == count - 1
@@ -149,107 +213,121 @@
         dt_acc[...] = jnp.zeros_like(dt_acc)
         rsum[...] = jnp.zeros_like(rsum)
         dsum[...] = jnp.zeros_like(dsum)
-
+        held_all[...] = jnp.zeros_like(held_all)
+        spread_taps(taps_ref, x_taps)
+        spread_taps(bc_taps_ref, bc_taps_all)
+        matrix_ref[...] = move_matrix(False)
+        back_matrix_ref[...] = move_matrix(True)
+
+    matrix, back_matrix = matrix_ref[...], back_matrix_ref[...]
     live = jnp.where(first, 0.0, 1.0)
-    bc_taps = bc_taps_ref[...]
+    bc_tap = taps_at(bc_taps_all, slice(None), span)
     dt_raw = dt_ref[...]
-    bc_shifts, bc_pre, bc_sig, b_t, c_t, causal, steps, rate, decay = span_common(
-        bc_before_ref[...] * live, bc_ref[...], dt_raw, bc_taps, dt_par_ref[...]
-    )
-    b_n = b_t.astype(F32).T.astype(BF)
-    scores = jnp.where(causal, nn(b_n, c_t), 0.0)
-    decay_n = decay.T
-    grown = jnp.exp(decay)
-    last = decay[:, span - 1 : span]
-    left = jnp.exp(last - decay)
-    kept = jnp.exp(last)
-    entering = enter_ref[...]
-    leaving = dstate[...].astype(BF)
-    carry[...] = nn(entering, c_t)
-    from_state[...] = nn(leaving, b_t)
+    bc_now = bc_ref[...]
+    (
+        bc_pre, bc_sig, b_t, c_t, b_n, scores, causal, steps, rate, decay, decay_n, grown, left, kept
+    ) = span_common(bc_before_ref[...] * live, bc_now, dt_raw, bc_tap, dt_par_ref[...], matrix)
+    for q in parts:
+        scores_all[q] = scores[q]
+        dscores_all[q] = jnp.zeros((PART, PART), F32)
+        carry[:, lanes(q)] = nn(enter_ref[q * inner : (q + 1) * inner, :], c_t[:, lanes(q)])
     coef = coef_ref[...]
-    dscores = jnp.zeros((span, span), F32)
-    def fold(v):
-        total = v[:, :EDGE]
-        for k in range(1, span // EDGE):
-            total = total + v[:, k * EDGE : (k + 1) * EDGE]
-        return total
     for h in range(heads):
         at = slice(h * size, (h + 1) * size)
         z = zx_ref[2 * h * size : (2 * h + 1) * size, :]
         x_raw = zx_ref[(2 * h + 1) * size : (2 * h + 2) * size, :]
         x_before = zx_before_ref[(2 * h + 1) * size : (2 * h + 2) * size, :] * live
-        taps = taps_ref[at, :]
-        shifts = shifted(x_before, x_raw)
-        pre = conv_of(shifts, taps)
+        tap = taps_at(x_taps, at, span)
+        pre = conv_of(x_before, x_raw, tap, matrix)
         sig = sigmoid(pre)
         x = pre * sig
-        steps_h = steps[h : h + 1, :]
+        x_all[at, :] = x
+        slope_all[at, :] = sig + x * (1.0 - sig)
+        xd = x * steps[h : h + 1, :]
+        xd_low = xd.astype(BF)
+        tailed[at, :] = (xd * left[h : h + 1, :]).astype(BF)
+        ratios, mixings, mixed = [], [], []
+        for q in parts:
+            gap = decay[h : h + 1, lanes(q)] - decay_n[q][:, h : h + 1]
+            ratios.append(jnp.exp2(jnp.minimum(gap, 0.0)))
+            mixings.append((scores_all[q] * ratios[q]).astype(BF))
+            mixed.append(nn(xd_low[:, lanes(q)], mixings[q]))
         grown_h = grown[h : h + 1, :]
-        left_h = left[h : h + 1, :]
-        xd = x * steps_h
-        xd_low = xd.astype(BF)
-        ratio = jnp.exp(jnp.minimum(decay[h : h + 1, :] - decay_n[:, h : h + 1], 0.0))
-        mixing = (scores * ratio).astype(BF)
-        skip = taps[:, 5:6]
-        y_scan = nn(xd_low, mixing) + carry[at, :] * grown_h
-        y = y_scan + skip * x
+        y_scan = jnp.concatenate(mixed, axis=1) + carry[at, :] * grown_h
+        y = y_scan + tap(5) * x
         zsig = sigmoid(z)
         silu_z = z * zsig
         gated = y * silu_z
         gn = gn_ref[at, :].astype(F32)
-        g_gated = taps[:, 6:7] * gn - gated * coef
+        g_gated = tap(6) * gn - gated * coef
         gy = g_gated * silu_z
         gzx_ref[2 * h * size : (2 * h + 1) * size, :] = (
             g_gated * y * (zsig + silu_z * (1.0 - zsig))
         ).astype(BF)
         gy_low = gy.astype(BF)
-        gy_wide = gy_low.astype(F32)
+        gy_all[at, :] = gy_low
         grown_g[at, :] = (gy * grown_h).astype(BF)
-        tailed[at, :] = (xd * left_h).astype(BF)
-        dx_state = from_state[at, :] * left_h
-        dxd = nt(gy_low, mixing) + dx_state
-        xd_wide = xd_low.astype(F32)
-        rsum[h : h + 1, :] = jnp.sum(gy_wide * y_scan - xd_wide * dxd, axis=0, keepdims=True)
+        rsum[h : h + 1, :] = jnp.sum(gy_low.astype(F32) * y_scan, axis=0, keepdims=True)
+        x_acc[5, at, :] = x_acc[5, at, :] + fold(gy * x)
+        x_acc[6, at, :] = x_acc[6, at, :] + fold(gn * gated)
+        for q in parts:
+            dxd_all[at, lanes(q)] = nt(gy_low[:, lanes(q)], mixings[q])
+            dscores_all[q] = dscores_all[q] + tn(xd_low[:, lanes(q)], gy_low[:, lanes(q)]) * ratios[q]
+    db, dc, flows = [], [], []
+    for q in reversed(parts):
+        entering = enter_ref[q * inner : (q + 1) * inner, :]
+        leaving = dstate[...].astype(BF)
+        from_state[:, lanes(q)] = nn(leaving, b_t[:, lanes(q)])
+        low = jnp.where(causal, dscores_all[q], 0.0).astype(BF)
+        dc.insert(0, nn(b_t[:, lanes(q)], low) + tn(entering, grown_g[:, lanes(q)]))
+        db.insert(0, nt(c_t[:, lanes(q)], low) + tn(leaving, tailed[:, lanes(q)]))
+        more = nt(grown_g[:, lanes(q)], c_t[:, lanes(q)])
+        for h in range(heads):
+            at = slice(h * size, (h + 1) * size)
+            passed = dstate[at, :] * kept[q][h : h + 1, :]
+            held_all[q, h : h + 1, :] = jnp.sum(passed * entering[at, :].astype(F32), axis=0, keepdims=True)
+            dstate[at, :] = passed + more[at, :]
+    for h in range(heads):
+        at = slice(h * size, (h + 1) * size)
+        x_raw = zx_ref[(2 * h + 1) * size : (2 * h + 2) * size, :]
+        tap = taps_at(x_taps, at, span)
+        x = x_all[at, :]
+        steps_h = steps[h : h + 1, :]
+        dx_state = from_state[at, :] * left[h : h + 1, :]
+        dxd = dxd_all[at, :] + dx_state
+        xd_wide = (x * steps_h).astype(BF).astype(F32)
+        rsum[h : h + 1, :] = rsum[h : h + 1, :] - jnp.sum(xd_wide * dxd, axis=0, keepdims=True)
         dsum[h : h + 1, :] = jnp.sum(x * dxd, axis=0, keepdims=True)
         held = jnp.sum(xd_wide * dx_state, axis=0, keepdims=True)
-        held = jnp.sum(held, axis=1, keepdims=True)
-        flow = jnp.sum(dstate[at, :] * entering[at, :].astype(F32), axis=0, keepdims=True)
-        flow = jnp.sum(flow, axis=1, keepdims=True) * kept[h : h + 1, :]
-        dt_acc[h : h + 1, 0:1] = held + flow
-        dscores = dscores + tn(xd_low, gy_low) * ratio
-        dx = dxd * steps_h + skip * gy
-        gpre = dx * (sig + x * (1.0 - sig))
-        later = ahead(gpre, x_head[at, :])
+        for q in parts:
+            held_all[q, h : h + 1, :] = held_all[q, h : h + 1, :] + held[:, lanes(q)]
+        dx = dxd * steps_h + tap(5) * gy_all[at, :].astype(F32)
+        gpre = dx * slope_all[at, :]
+        g_raw, later = conv_back(gpre, x_head[at, :], tap, back_matrix)
         x_head[at, :] = gpre[:, :EDGE]
-        g_raw = taps[:, 3:4] * later[0]
-        for k in (1, 2, 3):
-            g_raw = g_raw + taps[:, 3 - k : 4 - k] * later[k]
         gzx_ref[(2 * h + 1) * size : (2 * h + 2) * size, :] = g_raw.astype(BF)
-        for k in range(4):
-            x_acc[3 - k, at, :] = x_acc[3 - k, at, :] + fold(gpre * shifts[k])
+        for k, moved_g in enumerate((gpre, *later)):
+            x_acc[3 - k, at, :] = x_acc[3 - k, at, :] + fold(moved_g * x_raw)
         x_acc[4, at, :] = x_acc[4, at, :] + fold(gpre)
-        x_acc[5, at, :] = x_acc[5, at, :] + fold(gy * x)
-        x_acc[6, at, :] = x_acc[6, at, :] + fold(gn * gated)
-    dscores = jnp.where(causal, dscores, 0.0).astype(BF)
-    dc = nn(b_t, dscores) + tn(entering, grown_g[...])
-    db = nt(c_t, dscores) + tn(leaving, tailed[...])
-    dstate[...] = nt(grown_g[...], c_t)  + dstate[...] * jnp.concatenate(
-        [jnp.broadcast_to(kept[h : h + 1, :], (size, dstate.shape[1])) for h in range(heads)], axis=0
-    )
-    gbc = jnp.concatenate([db, dc], axis=0) * (bc_sig + bc_pre * bc_sig * (1.0 - bc_sig))
-    later = ahead(gbc, bc_head[...])
+    gbc = jnp.concatenate([jnp.concatenate(db, axis=1), jnp.concatenate(dc, axis=1)], axis=0)
+    gbc = gbc * (bc_sig + bc_pre * bc_sig * (1.0 - bc_sig))
+    g_raw, later = conv_back(gbc, bc_head[...], bc_tap, back_matrix)
     bc_head[...] = gbc[:, :EDGE]
-    g_raw = bc_taps[:, 3:4] * later[0]
-    for k in (1, 2, 3):
-        g_raw = g_raw + bc_taps[:, 3 - k : 4 - k] * later[k]
     gzx_ref[wide : wide + 2 * half, :] = g_raw.astype(BF)
-    for k in range(4):
-        bc_acc[3 - k] = bc_acc[3 - k] + fold(gbc * bc_shifts[k])
+    for k, moved_g in enumerate((gbc, *later)):
+        bc_acc[3 - k] = bc_acc[3 - k] + fold(moved_g * bc_now)
     bc_acc[4] = bc_acc[4] + fold(gbc)
-    rows = lax.broadcasted_iota(jnp.int32, (span, span), 0)
-    cols = lax.broadcasted_iota(jnp.int32, (span, span), 1)
-    da = exact(rsum[...], (rows >= cols).astype(F32)) + dt_acc[:, 0:1]
+    after = jnp.logical_or(
+        jnp.logical_not(causal),
+        lax.broadcasted_iota(jnp.int32, (PART, PART), 0) == lax.broadcasted_iota(jnp.int32, (PART, PART), 1),
+    ).astype(F32)
+    da = jnp.concatenate(
+        [
+            exact(rsum[:, lanes(q)], after) + jnp.sum(held_all[q], axis=1, keepdims=True)
+            for q in parts
+        ],
+        axis=1,
+    )
     g_steps = dsum[...] + rate * da
     g_dt = g_steps * sigmoid(dt_raw + dt_par_ref[:, 0:1])
     gzx_ref[wide + 2 * half :, :] = g_dt.astype(BF)
@@ -285,19 +363,25 @@
         out_specs=[
             pl.BlockSpec((inner, span), lambda i: (0, i)),
             pl.BlockSpec((1, span), lambda i: (0, i)),
-            pl.BlockSpec((inner, states), lambda i: (i, 0)),
+            pl.BlockSpec((span // PART * inner, states), lambda i: (i, 0)),
         ],
         out_shape=[
             jax.ShapeDtypeStruct((inner, length), BF),
             jax.ShapeDtypeStruct((1, length), F32),
-            jax.ShapeDtypeStruct((length // span * inner, states), BF),
+            jax.ShapeDtypeStruct((length // PART * inner, states), BF),
         ],
         scratch_shapes=[
             pltpu.VMEM((inner, states), F32),
             pltpu.VMEM((inner, EDGE), F32),
             pltpu.VMEM((aux, EDGE), F32),
             pltpu.VMEM((inner, span), F32),
+            pltpu.VMEM((inner, span), F32),
             pltpu.VMEM((inner, span), BF),
+            pltpu.VMEM((inner, span), BF),
+            pltpu.VMEM((span // PART, PART, PART), F32),
+            pltpu.VMEM((7, inner, EDGE), F32),
+            pltpu.VMEM((5, aux, EDGE), F32),
+            pltpu.VMEM((2 * EDGE, 3 * EDGE), BF),
         ],
         compiler_params=pltpu.CompilerParams(vmem_limit_bytes=48 * 2**20),
         name="scan_forward",
@@ -325,7 +409,7 @@
             pl.BlockSpec((aux, span), lambda i: (2 * inner // aux, rev(i))),
             pl.BlockSpec((aux, EDGE), lambda i: (2 * inner // aux, before(i))),
             pl.BlockSpec((steps, span), lambda i: ((2 * inner + aux) // steps, rev(i))),
-            pl.BlockSpec((inner, states), lambda i: (rev(i), 0)),
+            pl.BlockSpec((span // PART * inner, states), lambda i: (rev(i), 0)),
             pl.BlockSpec((inner, span), lambda i: (0, rev(i))),
             pl.BlockSpec((1, span), lambda i: (0, rev(i))),
             whole(inner, 8), whole(aux, 8), whole(steps, 8),
@@ -353,6 +437,17 @@
             pltpu.VMEM((steps, EDGE), F32),
             pltpu.VMEM((steps, span), F32),
             pltpu.VMEM((steps, span), F32),
+            pltpu.VMEM((inner, span), F32),
+            pltpu.VMEM((inner, span), F32),
+            pltpu.VMEM((inner, span), F32),
+            pltpu.VMEM((inner, span), BF),
+            pltpu.VMEM((span // PART, PART, PART), F32),
+            pltpu.VMEM((span // PART, PART, PART), F32),
+            pltpu.VMEM((span // PART, steps, PART), F32),
+            pltpu.VMEM((7, inner, EDGE), F32),
+            pltpu.VMEM((5, aux, EDGE), F32),
+            pltpu.VMEM((2 * EDGE, 3 * EDGE), BF),
+            pltpu.VMEM((2 * EDGE, 3 * EDGE), BF),
         ],
         compiler_params=pltpu.CompilerParams(vmem_limit_bytes=56 * 2**20),
         name="scan_backward",
@@ -382,20 +477,20 @@
 
 
 class Scatter:
-    def __init__(self, x, small=None):
+    def __init__(self, left, right, small=None):
         self.count = lax.axis_size("row")
-        self.x, self.small = x, small
+        self.small = small
         if self.count != 4:
-            self.sent = (x,)
+            self.sent = (jnp.concatenate([left, right], axis=1),)
             return
         me = lax.axis_index("row")
-        self.size, width = x.shape[0] // 4, x.shape[1]
-        half = width // 2
+        self.size, half = left.shape[0] // 4, left.shape[1]
         self.half = half
         self.my_y, self.my_x = me // 2, me % 2
-        blocks = x.reshape(2, 2, self.size, width)
-        self.at_x = lambda i: lax.dynamic_slice(blocks, (0, i, 0, 0), (2, 1, self.size, half))[:, 0]
-        self.at_y = lambda i: lax.dynamic_slice(blocks, (i, 0, 0, half), (1, 2, self.size, half))[0]
+        left = left.reshape(2, 2, self.size, half)
+        right = right.reshape(2, 2, self.size, half)
+        self.at_x = lambda i: lax.dynamic_index_in_dim(left, i, 1, keepdims=False)
+        self.at_y = lambda i: lax.dynamic_index_in_dim(right, i, 0, keepdims=False)
         send_x = self.at_x(1 - self.my_x)
         if small is not None:
             pieces = small.reshape(2, 2, self.size)
@@ -460,7 +555,7 @@
     return v
 
 
-def sum_over_row_dp(v):
+def sum_over_row_dp(v, *before):
     if lax.axis_size("row") != 4:
         return lax.psum(butterfly(v, "row"), "dp")
     me = lax.axis_index("row")
@@ -470,12 +565,18 @@
         away = lax.dynamic_slice_in_dim(v, (1 - side) * size, size, 0)
         keep = lax.dynamic_slice_in_dim(v, side * size, size, 0)
         v = keep + flip(away, bit)
-    v = butterfly(v, "dp")
+    v = butterfly(tie(v, *before), "dp")
     for bit in (2, 1):
         other = flip(v, bit)
         first = me // bit % 2 == 0
         v = jnp.concatenate([jnp.where(first, v, other), jnp.where(first, other, v)], axis=0)
     return v
+
+
+def sum_over_row(v):
+    if lax.axis_size("row") != 4:
+        return butterfly(v, "row")
+    return v + flip(v, 1) + flip(v, 2) + flip(v, 3)
 
 
 def other_col(v):
@@ -567,8 +668,8 @@
         )
     )
     out_own = output_weight.reshape(inner, width_col)
-    in_weight = tie(jnp.concatenate([in_own, other_col(in_own)], axis=0))
-    out_weight = tie(jnp.concatenate([out_own, other_col(out_own)], axis=1))
+    in_other, out_other = other_col(in_own), other_col(out_own)
+    in_weight = tie(jnp.concatenate([in_own, in_other], axis=0))
 
     scaled[0] = tie(scaled[0], in_weight)
 
@@ -609,7 +710,7 @@
         placed = lax.dynamic_update_slice_in_dim(
             jnp.zeros((local_len * row_count,), F32), share, row_index * local_len, 0
         )
-        coef.append(butterfly(placed[None, :], "row"))
+        coef.append(sum_over_row(placed[None, :]))
         sent = (grad * gate_inv).astype(BF)
         g_rows.append(spread(tie(sent, *g_rows[-1:])))
         return sent
@@ -626,35 +727,36 @@
         entering.append(e)
         if k > 0:
             g = tie(g, finish(k - 1, g))
-        part = matmul(g, out_weight, 0, 0).astype(BF)
-        scatters.append(Scatter(part, square))
+        left, right = (matmul(g, w, 0, 0).astype(BF) for w in (out_own, out_other))
+        scatters.append(Scatter(left, right, square))
         scatters[-1].first()
-    scatters[-1].second()
+    out_weight = tie(jnp.concatenate(tie((out_own, out_other), *scatters[-1].sent), axis=1))
+    scatters[-1].second(out_weight, *coef)
     finish(seq_col - 1)
 
+    to_rows = lambda g: Scatter(*(matmul(g, w, 0, 1).astype(BF) for w in (in_own, in_other)))
     g_in, scatters = [], []
     sums = [0.0, 0.0, 0.0]
+    w_out_part = 0.0
     for k in range(seq_col):
         final = k == seq_col - 1
         whole = g_rows[k] if k == 0 else tie(g_rows[k], g_in[-1], coef[k])
+        w_out_part = w_out_part + matmul(gated[k], whole, 1, 0)
+        before = (w_out_part,)
         if k == 0:
             dealt_output = dealt_rows(result)
             output_parts = sent_back(dealt_output)
-        gn = matmul(out_weight, whole, 1, 1)
         if final:
-            w_out_part = sum(
-                matmul(gated[i], whole if i == k else g_rows[i], 1, 0) for i in range(seq_col)
-            )
-            received = tie(other_col(w_out_part[:, width_col:].astype(BF)), gn)
+            received = other_col(w_out_part[:, width_col:].astype(BF))
             w_out_low = (w_out_part[:, :width_col] + received.astype(F32)).astype(BF)
             w_out_sum = lax.psum(w_out_low, "dp")
-            if k > 0:
-                scatters.append(Scatter(matmul(tie(g_in[-1], w_out_low), in_weight, 0, 1).astype(BF)))
-        elif k > 0:
-            scatters.append(Scatter(matmul(g_in[-1], in_weight, 0, 1).astype(BF)))
+            before = (w_out_low,)
+        gn = matmul(out_weight, whole, 1, 1)
         if k > 0:
+            scatters.append(to_rows(tie(g_in[-1], *before)))
             scatters[-1].first()
-            gn = tie(gn, *scatters[-1].sent)
+            before = scatters[-1].sent
+        gn = tie(gn, *before)
         g, gx, gbc, gdt = scan_backward(
             zx[k], entering[k], gn, coef[k], taps, bc_taps, dt_par, heads
         )
@@ -664,22 +766,20 @@
         if k > 0:
             scatters[-1].second(g)
             g = tie(g, *scatters[-1].passed)
-        if final:
-            g = tie(g, w_out_sum)
         g_in.append(g)
 
-    scatters.append(Scatter(matmul(g_in[-1], in_weight, 0, 1).astype(BF)))
+    def rows_of(start, g):
+        return sum(matmul(scaled[i][:, start : start + width_col], g[i], 0, 1) for i in range(seq_col))
+
+    g_in[-1] = tie(g_in[-1], w_out_sum)
+    g_wide = [g[:wide] for g in g_in]
+    there = rows_of(width_col, g_wide).astype(BF)
+    scatters.append(to_rows(tie(g_in[-1], there)))
     scatters[-1].first()
-    half_of = lambda start, g: sum(
-        matmul(scaled[i][:, start : start + width_col], g[i], 0, 1) for i in range(seq_col)
-    )
-    g_wide = [g[:wide] for g in g_in]
     g_wide[-1] = tie(g_wide[-1], *scatters[-1].sent)
-    in_there = half_of(width_col, g_wide).astype(BF)
-    scatters[-1].second(in_there)
-    g_wide[-1] = tie(g_wide[-1], *scatters[-1].passed)
-    in_low = (half_of(0, g_wide) + other_col(in_there).astype(F32)).astype(BF)
+    in_low = (rows_of(0, g_wide) + other_col(there).astype(F32)).astype(BF)
     in_low = tie(in_low.reshape(width_col, heads, pair))
+    scatters[-1].second(in_low)
     w_zx = lax.psum(in_low, "dp")
     g_aux = [g[wide:] for g in g_in]
     g_aux[-1] = tie(g_aux[-1], in_low)
@@ -697,7 +797,6 @@
         ],
         axis=1,
     )
-    w_aux = sum_over_row_dp(aux_half)
     gain_part = jnp.zeros((model_width,), F32)
     g_u = []
     for k in range(seq_col):
@@ -708,6 +807,7 @@
         cube = inv_rms[k] * inv_rms[k] * inv_rms[k]
         g_u.append((g_result[k] + inv_rms[k] * weighted - u[k] * (cube * dot)).astype(BF))
     hidden_parts = sent_back(tie(dealt_rows(g_u), w_zx))
+    w_aux = sum_over_row_dp(aux_half)
 
     gx, gbc, gdt = sums
     flat = jnp.concatenate(

time: 838 us -> 741 us (0.88)
  waiting for transfers between devices: 335 us -> 288 us
  Pallas kernels: 142 us -> 96.3 us
  matrix products: 155 us -> 144 us
  other arithmetic: 83.1 us -> 92.8 us
    pallas_call x2, Pallas kernels: 99.4 us -> 70 us  [scan_backward(): pl.pallas_call(body, grid=(count,), in_specs=[pl.BlockSpec((2 * inner, sp...]
    ppermute x20 -> x26, waiting for transfers between devices: 112 us -> 83.2 us  [flip(): return lax.ppermute(v, 'row', [(i, i ^ bit) for i in range(4)])]
    pallas_call x2, Pallas kernels: 42.2 us -> 26.3 us  [scan_forward(): pl.pallas_call(body, grid=(length // span,), in_specs=[pl.BlockSpec((2 *...]
    psum x1, waiting for transfers between devices: 62.1 us -> 49.3 us  [per_device(): w_zx = lax.psum(in_low, 'dp')]
    dot_general x16 -> x20, matrix products: 155 us -> 144 us  [matmul(): lax.dot_general(a, b, (((over_a,), (over_b,)), ((), ())), preferred_eleme...]
    psum x1, waiting for transfers between devices: 14.3 us -> 4.07 us  [per_device(): w_out_sum = lax.psum(w_out_low, 'dp')]
    add x0 -> x8, other arithmetic: none -> 8.63 us  [the longest x4 7.41 us: last(): right = self.right + end_y.astype(F32)]
    ppermute x20 -> x26, starting transfers between devices: 21.4 us -> 29.3 us  [flip(): return lax.ppermute(v, 'row', [(i, i ^ bit) for i in range(4)])]
  transfers between devices with their start and end apart: 53 -> 55, of which waited for: 23 -> 26; matrix products, arithmetic and copies ran while one was open for 23% -> 31% of each run, Pallas kernels for 17% -> 13%
where the time goes in v3:
time: 741 us; the launch traced here: 737 us
  waiting for transfers between devices  288 us (39%)
  matrix products  144 us (19%)
  Pallas kernels  96.3 us (13%)
  other arithmetic  92.8 us (13%)
  local copies, waits for them, and re-layouts  54.6 us (7%)
  starting transfers between devices  41.5 us (6%)
  between operations  19.9 us (3%)
    dot_general x20, matrix products, matmul(): lax.dot_general(a, b, (((over_a,), (over_b,)), ((), ())), preferred_eleme...  144 us
    ppermute x26, waiting for transfers between devices, flip(): return lax.ppermute(v, 'row', [(i, i ^ bit) for i in range(4)])  83.2 us
    pallas_call x2, Pallas kernels, scan_backward(): pl.pallas_call(body, grid=(count,), in_specs=[pl.BlockSpec((2 * inner, sp...  70 us
    ppermute x6, waiting for transfers between devices, butterfly(): v = v + lax.ppermute(v, axis, [(i, i ^ bit) for i in range(count)])  58.3 us
    all_gather x4, waiting for transfers between devices, per_device(): spread = lambda v: lax.all_gather(v, 'row', axis=0, tiled=True)  51 us
    psum x1, waiting for transfers between devices, per_device(): w_zx = lax.psum(in_low, 'dp')  49.3 us
    ppermute x6, waiting for transfers between devices, sent_back(): lax.ppermute(piece, 'dp', [(i, (i + hop) % groups) for i in range(groups)])  36 us
    ppermute x26, starting transfers between devices, flip(): return lax.ppermute(v, 'row', [(i, i ^ bit) for i in range(4)])  29.3 us
  transfers between devices with their start and end apart: 55, of which 26 were waited for; matrix products, arithmetic and copies ran while one was open for 31% of the time, Pallas kernels for 13%

profile of v3, /device:TPU:0, one launch (start us, length us, event | category | flops | bytes accessed | tf_op | source)
XLA Modules:
  0.0 737.4 jit_solution(1733381092982146466)
XLA Ops:
  14.4 6.7 copy.61
  25.6 44.2 %all-gather.5.cloned.1.call-done = bf16[1024,2048]{1,0:T(8,128)(2,1)} async-done(((bf16[256,2048]{1,0:T(8,128)(2,1)}), bf16[1024,2048]{1,0:T(8,128)(2,1)}) %all-gather.5.cloned.1.call-update) | async-done | bytes 4194320 | tf_op jit(solution)/shard_map/all_gather | solution.py:654
  71.7 5.5 pad_maximum_fusion
  81.3 13.2 %fusion.155.zx_ref.bc_ref.dt_ref.zx_before_ref.bc_before_ref = f32[2320,1024]{1,0:T(8,128)} fusion(bf16[2048,2320]{0,1:T(8,128)(2,1)S(1)} %pad_maximum_fusion, bf16[1024,2048]{1,0:T(8,128)(2,1)S(1)} %copy-done.76), kind=kOutput, calls=%fused_computation.359 | convolution fusion | flops 9730785280 | bytes 23199744 | tf_op jit(solution)/shard_map/dot_general | solution.py:616
  94.5 13.1 %scan_forward.2 = (bf16[1024,1024]{1,0:T(8,128)(2,1)S(1)}, f32[1,1024]{1,0:T(1,128)S(1)}, bf16[8192,128]{1,0:T(8,128)(2,1)S(1)}) custom-call(f32[2320,1024]{1,0:T(8,128)} %fusion.155.zx_ref.bc_ref.dt_ref.zx_before_ref.bc_before_ref, f32[2320,1024]{1,0:T(8,128)} %fusion.155.zx_ref.bc_ref.dt_ref.zx_before_ref.bc_before_ref, ...), custom_call_target="tpu_custom_call" | custom-call | tf_op jit(solution)/shard_map/scan_forward/pallas_call | solution.py:354
  123.8 6.8 all-gather.7.cloned.1.call-done
  130.6 16.1 %fusion.156.zx_ref.bc_ref.dt_ref.zx_before_ref.bc_before_ref = f32[2320,1024]{1,0:T(8,128)} fusion(bf16[2048,2320]{0,1:T(8,128)(2,1)} %copy-done.16, bf16[1024,2048]{1,0:T(8,128)(2,1)} %all-gather.7.cloned.1.call-done), kind=kOutput, calls=%fused_computation.360 | convolution fusion | flops 9730785280 | bytes 23199744 | tf_op jit(solution)/shard_map/dot_general | solution.py:616
  161.4 13.2 %scan_forward.3 = (bf16[1024,1024]{1,0:T(8,128)(2,1)S(1)}, f32[1,1024]{1,0:T(1,128)S(1)}, bf16[8192,128]{1,0:T(8,128)(2,1)S(1)}) custom-call(f32[2320,1024]{1,0:T(8,128)} %fusion.156.zx_ref.bc_ref.dt_ref.zx_before_ref.bc_before_ref, f32[2320,1024]{1,0:T(8,128)} %fusion.156.zx_ref.bc_ref.dt_ref.zx_before_ref.bc_before_ref, ...), custom_call_target="tpu_custom_call" | custom-call | tf_op jit(solution)/shard_map/scan_forward/pallas_call | solution.py:354
  212.2 26.1 %collective-permute-done.9 = f32[1,1024]{1,0:T(1,128)S(1)} collective-permute-done((f32[1,1024]{1,0:T(1,128)S(1)}, f32[1,1024]{1,0:T(1,128)S(1)}, u32[]{:S(2)}, u32[]{:S(2)}) %collective-permute-start.9) | collective-permute-done | bytes 4128 | tf_op jit(solution)/shard_map/ppermute | solution.py:476
  246.5 20.9 %collective-permute-done.15 = bf16[256,1024]{1,0:T(8,128)(2,1)S(1)} collective-permute-done((bf16[256,1024]{1,0:T(8,128)(2,1)S(1)}, bf16[256,1024]{1,0:T(8,128)(2,1)S(1)}, u32[]{:S(2)}, u32[]{:S(2)}) %collective-permute-start.15) | collective-permute-done | bytes 524320 | tf_op jit(solution)/shard_map/ppermute | solution.py:476
  293.9 6.1 fusion.157.gn_ref
  300.0 6.8 fusion.158
  306.8 35.1 %scan_backward.2 = (bf16[2320,1024]{1,0:T(8,128)(2,1)}, f32[1024,8]{1,0:T(8,128)}, f32[256,8]{1,0:T(8,128)}, f32[16,128]{1,0:T(8,128)}) custom-call(f32[2320,1024]{1,0:T(8,128)} %fusion.155.zx_ref.bc_ref.dt_ref.zx_before_ref.bc_before_ref, f32[2320,1024]{1,0:T(8,128)} %fusion.155.zx_ref.bc_ref.dt_ref.zx_before_ref.bc_before_ref, ...), custom_call_target="tpu_custom_call" | custom-call | tf_op jit(solution)/shard_map/scan_backward/pallas_call | solution.py:403
  342.0 8.2 %convolution_add_fusion = f32[1024,2048]{1,0:T(8,128)S(1)} fusion(f32[1024,2048]{1,0:T(8,128)} %fusion.158, bf16[1024,1024]{1,0:T(8,128)(2,1)S(1)} %copy-done.7, bf16[1024,2048]{1,0:T(8,128)(2,1)} %all-gather.11.cloned.1.call-done), kind=kOutput, calls=%fused_computation.21 | convolution fusion | flops 4297064448 | bytes 23068672 | tf_op jit(solution)/shard_map/dot_general | solution.py:616
  357.1 8.9 %convolution_convert_fusion.3 = bf16[1024,1024]{1,0:T(8,128)(2,1)S(1)} fusion(bf16[2320,1024]{1,0:T(8,128)(2,1)} %get-tuple-element.91, bf16[1024,2320]{0,1:T(8,128)(2,1)} %pad_maximum_fusion.1), kind=kOutput, calls=%fused_computation.79 | convolution fusion | flops 4866441216 | bytes 11599872 | tf_op jit(solution)/shard_map/dot_general | solution.py:616
  366.0 9.8 %convolution_convert_fusion.2 = bf16[1024,1024]{1,0:T(8,128)(2,1)S(1)} fusion(bf16[2320,1024]{1,0:T(8,128)(2,1)} %get-tuple-element.91, bf16[1024,2320]{0,1:T(8,128)(2,1)} %collective-permute-done), kind=kOutput, calls=%fused_computation.78 | convolution fusion | flops 4866441216 | bytes 11599872 | tf_op jit(solution)/shard_map/dot_general | solution.py:616
  378.8 6.1 fusion.159.gn_ref
  384.8 34.9 %scan_backward.3 = (bf16[2320,1024]{1,0:T(8,128)(2,1)}, f32[1024,8]{1,0:T(8,128)}, f32[256,8]{1,0:T(8,128)}, f32[16,128]{1,0:T(8,128)}) custom-call(f32[2320,1024]{1,0:T(8,128)} %fusion.156.zx_ref.bc_ref.dt_ref.zx_before_ref.bc_before_ref, f32[2320,1024]{1,0:T(8,128)} %fusion.156.zx_ref.bc_ref.dt_ref.zx_before_ref.bc_before_ref, ...), custom_call_target="tpu_custom_call" | custom-call | tf_op jit(solution)/shard_map/scan_backward/pallas_call | solution.py:403
  427.2 10.0 %collective-permute-done.27 = bf16[256,1024]{1,0:T(8,128)(2,1)} collective-permute-done((bf16[256,1024]{1,0:T(8,128)(2,1)}, bf16[256,1024]{1,0:T(8,128)(2,1)}, u32[]{:S(2)}, u32[]{:S(2)}) %collective-permute-start.27) | collective-permute-done | bytes 524320 | tf_op jit(solution)/shard_map/ppermute | solution.py:476
  441.7 7.2 fusion.22
  448.9 8.5 %add_convert_fusion.1 = bf16[1024,2048]{1,0:T(8,128)(2,1)} fusion(f32[1024,2048]{1,0:T(8,128)S(1)} %fusion.22, bf16[2320,1024]{1,0:T(8,128)(2,1)} %get-tuple-element.91, bf16[1024,2048]{1,0:T(8,128)(2,1)S(1)} %copy-done.77), kind=kOutput, calls=%fused_computation.2 | convolution fusion | flops 4299161600 | bytes 18874368 | tf_op jit(solution)/shard_map/dot_general | solution.py:616
  462.9 7.5 %convolution_convert_fusion = bf16[1024,1024]{1,0:T(8,128)(2,1)S(1)} fusion(bf16[2320,1024]{1,0:T(8,128)(2,1)S(1)} %bitcast.320, bf16[1024,2320]{0,1:T(8,128)(2,1)} %collective-permute-done), kind=kOutput, calls=%fused_computation.76 | convolution fusion | flops 4866441216 | bytes 11599872 | tf_op jit(solution)/shard_map/dot_general | solution.py:616
  473.1 7.7 %convolution_convert_fusion.1 = bf16[1024,1024]{1,0:T(8,128)(2,1)S(1)} fusion(bf16[2320,1024]{1,0:T(8,128)(2,1)S(1)} %bitcast.320, bf16[1024,2320]{0,1:T(8,128)(2,1)} %pad_maximum_fusion.1), kind=kOutput, calls=%fused_computation.77 | convolution fusion | flops 4866441216 | bytes 11599872 | tf_op jit(solution)/shard_map/dot_general | solution.py:616
  483.3 7.0 fusion.20
  490.3 8.4 %fusion = bf16[128,8,16,128]{3,1,2,0:T(8,128)(2,1)S(1)} fusion(bf16[1024,2048]{1,0:T(8,128)(2,1)} %collective-permute-done.30, f32[1024,2048]{1,0:T(8,128)} %fusion.20, bf16[2320,1024]{1,0:T(8,128)(2,1)S(1)} %bitcast.362, bf16[1024,2048]{1,0:T(8,128)(2,1)} %all-gather.5.cloned.1.call-done), kind=kOutput, calls=%fused_computation.16 | convolution fusion | flops 4303355904 | bytes 23068672 | tf_op jit(solution)/shard_map/dot_general | solution.py:616
  542.8 13.7 %collective-permute-done.34 = f32[3073]{0:T(1024)S(1)} collective-permute-done((f32[3073]{0:T(1024)S(1)}, f32[3073]{0:T(1024)S(1)}, u32[]{:S(2)}, u32[]{:S(2)}) %collective-permute-start.34) | collective-permute-done | bytes 12324 | tf_op jit(solution)/shard_map/ppermute | solution.py:553
  561.1 6.5 collective-permute-done.44
  569.9 24.6 %collective-permute-done.45 = f32[256,320]{0,1:T(8,128)S(1)} collective-permute-done((f32[256,320]{0,1:T(8,128)S(1)}, f32[256,320]{0,1:T(8,128)S(1)}, u32[]{:S(2)}, u32[]{:S(2)}) %collective-permute-start.45) | collective-permute-done | bytes 327712 | tf_op jit(solution)/shard_map/ppermute | solution.py:553
  602.1 17.9 %collective-permute-done.46 = f32[256,320]{0,1:T(8,128)S(1)} collective-permute-done((f32[256,320]{0,1:T(8,128)S(1)}, f32[256,320]{0,1:T(8,128)S(1)}, u32[]{:S(2)}, u32[]{:S(2)}) %collective-permute-start.46) | collective-permute-done | bytes 327712 | tf_op jit(solution)/shard_map/ppermute | solution.py:553
  630.6 49.3 %all-reduce.12.cloned.1.call-done = bf16[1024,16,128]{2,1,0:T(8,128)(2,1)} async-done(((bf16[1024,16,128]{2,1,0:T(8,128)(2,1)}), bf16[1024,16,128]{2,1,0:T(8,128)(2,1)}) %all-reduce.12.cloned.1.call-update) | async-done | bytes 4194320 | tf_op jit(solution)/shard_map/psum | solution.py:783
  689.4 6.5 collective-permute-done.39
  696.0 29.4 %collective-permute-done.40 = bf16[256,1024]{1,0:T(8,128)(2,1)S(1)} collective-permute-done((bf16[256,1024]{1,0:T(8,128)(2,1)S(1)}, bf16[256,1024]{1,0:T(8,128)(2,1)S(1)}, u32[]{:S(2)}, u32[]{:S(2)}) %collective-permute-start.40) | collective-permute-done | bytes 524320 | tf_op jit(solution)/shard_map/ppermute | solution.py:601
  (466 shorter events, 231.7 us)
Async XLA Ops:
  7.2 62.7 %all-gather.5.cloned.1.call-start = ((), (), s32[]{:S(2)}) async-start(), calls=%async_computation | async-start | bytes 5242880 | tf_op jit(solution)/shard_map/all_gather | solution.py:654
  14.4 116.2 %all-gather.7.cloned.1.call-start = ((), (), s32[]{:S(2)}) async-start(), calls=%async_computation.1 | async-start | bytes 5242880 | tf_op jit(solution)/shard_map/all_gather | solution.py:654
  25.3 46.4 %collective-permute-start = (bf16[1024,2320]{0,1:T(8,128)(2,1)}, bf16[1024,2320]{0,1:T(8,128)(2,1)}, u32[]{:S(2)}, u32[]{:S(2)}) collective-permute-start(bf16[1024,2320]{0,1:T(8,128)(2,1)} %pad_maximum_fusion.1), channel_id=1, source_target_pairs={{0,1},{1,0},{2,3},{3,2},{4,5},{5,4},{6,7},{7,6},{8,9},{9,8},{10,11... | collective-permute-start | bytes 14254088 | tf_op jit(solution)/shard_map/ppermute | solution.py:583
  69.9 205.7 %all-gather.9.cloned.1.call-start = ((), (), s32[]{:S(2)}) async-start(), calls=%async_computation.2 | async-start | bytes 5242880 | tf_op jit(solution)/shard_map/all_gather | solution.py:654
  70.4 46.7 %collective-permute-start.3 = (bf16[1024,1024]{1,0:T(8,128)(2,1)}, bf16[1024,1024]{1,0:T(8,128)(2,1)}, u32[]{:S(2)}, u32[]{:S(2)}) collective-permute-start(bf16[1024,1024]{1,0:T(8,128)(2,1)} %bitcast.8), channel_id=1, source_target_pairs={{0,1},{1,0},{2,3},{3,2},{4,5},{5,4},{6,7},{7,6},{8,9},{9,8},{10,11... | collective-permute-start | bytes 6291464 | tf_op jit(solution)/shard_map/ppermute | solution.py:583
  115.8 33.3 %collective-permute-start.4 = (bf16[2,272,1024]{2,1,0:T(8,128)(2,1)}, bf16[2,272,1024]{2,1,0:T(8,128)(2,1)}, u32[]{:S(2)}, u32[]{:S(2)}) collective-permute-start(bf16[2,272,1024]{2,1,0:T(8,128)(2,1)} %maximum_maximum_fusion), channel_id=1, source_target_pairs={{0,2},{2,0},{4,6},{6,4},{1,3},{3,1},{5,7},{7,5},{8,10},{10,8},{12,... | collective-permute-start | bytes 3342344 | tf_op jit(solution)/shard_map/ppermute | solution.py:476
  123.4 25.7 %collective-permute-start.5 = (bf16[2,256,1024]{2,1,0:T(8,128)(2,1)}, bf16[2,256,1024]{2,1,0:T(8,128)(2,1)}, u32[]{:S(2)}, u32[]{:S(2)}) collective-permute-start(bf16[2,256,1024]{2,1,0:T(8,128)(2,1)} %dynamic-slice_bitcast_fusion.6), channel_id=1, source_target_pairs={{0,4},{2,6},{4,0},{6,2},{1,5},{3,7},{5,1},{7,3},{8,12},{10,14},{12... | collective-permute-start | bytes 3145736 | tf_op jit(solution)/shard_map/ppermute | solution.py:476
  158.7 23.4 %collective-permute-start.8 = (bf16[2,256,1024]{2,1,0:T(8,128)(2,1)}, bf16[2,256,1024]{2,1,0:T(8,128)(2,1)}, u32[]{:S(2)}, u32[]{:S(2)}) collective-permute-start(bf16[2,256,1024]{2,1,0:T(8,128)(2,1)} %get-tuple-element.204), channel_id=1, source_target_pairs={{0,1},{1,0},{2,3},{3,2},{4,5},{5,4},{6,7},{7,6},{8,9},{9,8},{10,11... | collective-permute-start | bytes 3145736 | tf_op jit(solution)/shard_map/ppermute | solution.py:583
  188.3 153.7 %all-gather.11.cloned.1.call-start = ((), (), s32[]{:S(2)}) async-start(), calls=%async_computation.3 | async-start | bytes 5242880 | tf_op jit(solution)/shard_map/all_gather | solution.py:654
  195.1 43.8 %collective-permute-start.12 = (bf16[2,272,1024]{2,1,0:T(8,128)(2,1)}, bf16[2,272,1024]{2,1,0:T(8,128)(2,1)}, u32[]{:S(2)}, u32[]{:S(2)}) collective-permute-start(bf16[2,272,1024]{2,1,0:T(8,128)(2,1)} %maximum_maximum_fusion.1), channel_id=1, source_target_pairs={{0,2},{2,0},{4,6},{6,4},{1,3},{3,1},{5,7},{7,5},{8,10},{10,8},{12,... | collective-permute-start | bytes 3342344 | tf_op jit(solution)/shard_map/ppermute | solution.py:476
  202.8 36.1 %collective-permute-start.13 = (bf16[2,256,1024]{2,1,0:T(8,128)(2,1)}, bf16[2,256,1024]{2,1,0:T(8,128)(2,1)}, u32[]{:S(2)}, u32[]{:S(2)}) collective-permute-start(bf16[2,256,1024]{2,1,0:T(8,128)(2,1)} %dynamic-slice_bitcast_fusion.4), channel_id=1, source_target_pairs={{0,4},{2,6},{4,0},{6,2},{1,5},{3,7},{5,1},{7,3},{8,12},{10,14},{12... | collective-permute-start | bytes 3145736 | tf_op jit(solution)/shard_map/ppermute | solution.py:476
  203.9 34.4 %collective-permute-start.9 = (f32[1,1024]{1,0:T(1,128)S(1)}, f32[1,1024]{1,0:T(1,128)S(1)}, u32[]{:S(2)}, u32[]{:S(2)}) collective-permute-start(f32[1,1024]{1,0:T(1,128)S(1)} %get-tuple-element.180), channel_id=1, source_target_pairs={{0,2},{2,0},{4,6},{6,4},{1,3},{3,1},{5,7},{7,5},{8,10},{10,8},{12,... | collective-permute-start | bytes 12296 | tf_op jit(solution)/shard_map/ppermute | solution.py:476
  205.0 33.3 %collective-permute-start.10 = (f32[1,1024]{1,0:T(1,128)S(1)}, f32[1,1024]{1,0:T(1,128)S(1)}, u32[]{:S(2)}, u32[]{:S(2)}) collective-permute-start(f32[1,1024]{1,0:T(1,128)S(1)} %get-tuple-element.180), channel_id=1, source_target_pairs={{0,4},{2,6},{4,0},{6,2},{1,5},{3,7},{5,1},{7,3},{8,12},{10,14},{12... | collective-permute-start | bytes 12296 | tf_op jit(solution)/shard_map/ppermute | solution.py:476
  206.1 32.2 %collective-permute-start.11 = (f32[1,1024]{1,0:T(1,128)S(1)}, f32[1,1024]{1,0:T(1,128)S(1)}, u32[]{:S(2)}, u32[]{:S(2)}) collective-permute-start(f32[1,1024]{1,0:T(1,128)S(1)} %get-tuple-element.180), channel_id=1, source_target_pairs={{0,6},{2,4},{4,2},{6,0},{1,7},{3,5},{5,3},{7,1},{8,14},{10,12},{12... | collective-permute-start | bytes 12296 | tf_op jit(solution)/shard_map/ppermute | solution.py:476
  241.6 26.4 %collective-permute-start.14 = (bf16[272,1024]{1,0:T(8,128)(2,1)S(1)}, bf16[272,1024]{1,0:T(8,128)(2,1)S(1)}, u32[]{:S(2)}, u32[]{:S(2)}) collective-permute-start(bf16[272,1024]{1,0:T(8,128)(2,1)S(1)} %pad_maximum_fusion.15), channel_id=1, source_target_pairs={{0,4},{2,6},{4,0},{6,2},{1,5},{3,7},{5,1},{7,3},{8,12},{10,14},{12... | collective-permute-start | bytes 1671176 | tf_op jit(solution)/shard_map/ppermute | solution.py:476
  275.6 166.2 %all-reduce.10.cloned.1.call-start = ((), (), s32[]{:S(2)}) async-start(), calls=%async_computation.4 | async-start | bytes 4194304 | tf_op jit(solution)/shard_map/psum | solution.py:752
  288.6 53.4 %collective-permute-start.17 = (bf16[256,1024]{1,0:T(8,128)(2,1)S(1)}, bf16[256,1024]{1,0:T(8,128)(2,1)}, u32[]{:S(2)}, u32[]{:S(2)}) collective-permute-start(bf16[256,1024]{1,0:T(8,128)(2,1)S(1)} %get-tuple-element.198), channel_id=1, source_target_pairs={{0,8},{8,16},{16,24},{24,0},{1,9},{9,17},{17,25},{25,1},{2,10},{10... | collective-permute-start | bytes 1572872 | tf_op jit(solution)/shard_map/ppermute | solution.py:601
  290.0 51.9 %collective-permute-start.18 = (bf16[256,1024]{1,0:T(8,128)(2,1)S(1)}, bf16[256,1024]{1,0:T(8,128)(2,1)}, u32[]{:S(2)}, u32[]{:S(2)}) collective-permute-start(bf16[256,1024]{1,0:T(8,128)(2,1)S(1)} %get-tuple-element.199), channel_id=1, source_target_pairs={{0,16},{8,24},{16,0},{24,8},{1,17},{9,25},{17,1},{25,9},{2,18},{10... | collective-permute-start | bytes 1572872 | tf_op jit(solution)/shard_map/ppermute | solution.py:601
  292.4 49.5 %collective-permute-start.19 = (bf16[256,1024]{1,0:T(8,128)(2,1)S(1)}, bf16[256,1024]{1,0:T(8,128)(2,1)}, u32[]{:S(2)}, u32[]{:S(2)}) collective-permute-start(bf16[256,1024]{1,0:T(8,128)(2,1)S(1)} %get-tuple-element.200), channel_id=1, source_target_pairs={{0,24},{8,0},{16,8},{24,16},{1,25},{9,1},{17,9},{25,17},{2,26},{10... | collective-permute-start | bytes 1572872 | tf_op jit(solution)/shard_map/ppermute | solution.py:601
  357.0 322.8 %all-reduce.12.cloned.1.call-start = ((), (), s32[]{:S(2)}) async-start(), calls=%async_computation.5 | async-start | bytes 8388608 | tf_op jit(solution)/shard_map/psum | solution.py:783
  375.9 43.9 %collective-permute-start.25 = (bf16[2,256,1024]{2,1,0:T(8,128)(2,1)S(1)}, bf16[2,256,1024]{2,1,0:T(8,128)(2,1)S(1)}, u32[]{:S(2)}, u32[]{:S(2)}) collective-permute-start(bf16[2,256,1024]{2,1,0:T(8,128)(2,1)S(1)} %dynamic-slice_bitcast_fusion.2), channel_id=1, source_target_pairs={{0,4},{2,6},{4,0},{6,2},{1,5},{3,7},{5,1},{7,3},{8,12},{10,14},{12... | collective-permute-start | bytes 3145736 | tf_op jit(solution)/shard_map/ppermute | solution.py:476
  377.5 42.3 %collective-permute-start.24 = (bf16[2,256,1024]{2,1,0:T(8,128)(2,1)S(1)}, bf16[2,256,1024]{2,1,0:T(8,128)(2,1)}, u32[]{:S(2)}, u32[]{:S(2)}) collective-permute-start(bf16[2,256,1024]{2,1,0:T(8,128)(2,1)S(1)} %dynamic-slice_bitcast_fusion.3), channel_id=1, source_target_pairs={{0,2},{2,0},{4,6},{6,4},{1,3},{3,1},{5,7},{7,5},{8,10},{10,8},{12,... | collective-permute-start | bytes 3145736 | tf_op jit(solution)/shard_map/ppermute | solution.py:476
  457.4 32.8 %collective-permute-start.30 = (bf16[1024,2048]{1,0:T(8,128)(2,1)}, bf16[1024,2048]{1,0:T(8,128)(2,1)}, u32[]{:S(2)}, u32[]{:S(2)}) collective-permute-start(bf16[1024,2048]{1,0:T(8,128)(2,1)} %add_convert_fusion.1), channel_id=1, source_target_pairs={{0,1},{1,0},{2,3},{3,2},{4,5},{5,4},{6,7},{7,6},{8,9},{9,8},{10,11... | collective-permute-start | bytes 12582920 | tf_op jit(solution)/shard_map/ppermute | solution.py:583
  471.6 30.4 %collective-permute-start.29 = (bf16[2,256,1024]{2,1,0:T(8,128)(2,1)}, bf16[2,256,1024]{2,1,0:T(8,128)(2,1)}, u32[]{:S(2)}, u32[]{:S(2)}) collective-permute-start(bf16[2,256,1024]{2,1,0:T(8,128)(2,1)} %dynamic-slice_bitcast_fusion), channel_id=1, source_target_pairs={{0,4},{2,6},{4,0},{6,2},{1,5},{3,7},{5,1},{7,3},{8,12},{10,14},{12... | collective-permute-start | bytes 3145736 | tf_op jit(solution)/shard_map/ppermute | solution.py:476
  481.8 25.5 %collective-permute-start.28 = (bf16[2,256,1024]{2,1,0:T(8,128)(2,1)}, bf16[2,256,1024]{2,1,0:T(8,128)(2,1)}, u32[]{:S(2)}, u32[]{:S(2)}) collective-permute-start(bf16[2,256,1024]{2,1,0:T(8,128)(2,1)} %dynamic-slice_bitcast_fusion.1), channel_id=1, source_target_pairs={{0,2},{2,0},{4,6},{6,4},{1,3},{3,1},{5,7},{7,5},{8,10},{10,8},{12,... | collective-permute-start | bytes 3145736 | tf_op jit(solution)/shard_map/ppermute | solution.py:476
  561.0 68.1 %collective-permute-start.38 = (bf16[2,256,1024]{2,1,0:T(8,128)(2,1)}, bf16[2,256,1024]{2,1,0:T(8,128)(2,1)}, u32[]{:S(2)}, u32[]{:S(2)}) collective-permute-start(bf16[2,256,1024]{2,1,0:T(8,128)(2,1)} %pad_maximum_fusion.12), channel_id=1, source_target_pairs={{0,1},{1,0},{2,3},{3,2},{4,5},{5,4},{6,7},{7,6},{8,9},{9,8},{10,11... | collective-permute-start | bytes 3145736 | tf_op jit(solution)/shard_map/ppermute | solution.py:583
  567.7 26.9 %collective-permute-start.45 = (f32[256,320]{0,1:T(8,128)S(1)}, f32[256,320]{0,1:T(8,128)S(1)}, u32[]{:S(2)}, u32[]{:S(2)}) collective-permute-start(f32[256,320]{0,1:T(8,128)S(1)} %dynamic-slice_add_fusion), channel_id=1, source_target_pairs={{0,8},{8,0},{16,24},{24,16},{1,9},{9,1},{17,25},{25,17},{2,10},{10... | collective-permute-start | bytes 983048 | tf_op jit(solution)/shard_map/ppermute | solution.py:553
  569.9 27.3 %collective-permute-start.37 = (f32[11297]{0:T(1024)S(1)}, f32[11297]{0:T(1024)S(1)}, u32[]{:S(2)}, u32[]{:S(2)}) collective-permute-start(f32[11297]{0:T(1024)S(1)} %fusion.193), channel_id=1, source_target_pairs={{0,16},{8,24},{16,0},{24,8},{1,17},{9,25},{17,1},{25,9},{2,18},{10... | collective-permute-start | bytes 135572 | tf_op jit(solution)/shard_map/ppermute | solution.py:553
  594.6 25.4 %collective-permute-start.46 = (f32[256,320]{0,1:T(8,128)S(1)}, f32[256,320]{0,1:T(8,128)S(1)}, u32[]{:S(2)}, u32[]{:S(2)}) collective-permute-start(f32[256,320]{0,1:T(8,128)S(1)} %add.720), channel_id=1, source_target_pairs={{0,16},{8,24},{16,0},{24,8},{1,17},{9,25},{17,1},{25,9},{2,18},{10... | collective-permute-start | bytes 983048 | tf_op jit(solution)/shard_map/ppermute | solution.py:553
  628.2 54.6 %collective-permute-start.48 = (f32[512,320]{0,1:T(8,128)}, f32[512,320]{0,1:T(8,128)}, u32[]{:S(2)}, u32[]{:S(2)}) collective-permute-start(f32[512,320]{0,1:T(8,128)} %pad_maximum_fusion.13), channel_id=1, source_target_pairs={{0,2},{2,0},{4,6},{6,4},{1,3},{3,1},{5,7},{7,5},{8,10},{10,8},{12,... | collective-permute-start | bytes 1966088 | tf_op jit(solution)/shard_map/ppermute | solution.py:476
  681.4 44.0 %collective-permute-start.40 = (bf16[256,1024]{1,0:T(8,128)(2,1)S(1)}, bf16[256,1024]{1,0:T(8,128)(2,1)S(1)}, u32[]{:S(2)}, u32[]{:S(2)}) collective-permute-start(bf16[256,1024]{1,0:T(8,128)(2,1)S(1)} %get-tuple-element.194), channel_id=1, source_target_pairs={{0,16},{8,24},{16,0},{24,8},{1,17},{9,25},{17,1},{25,9},{2,18},{10... | collective-permute-start | bytes 1572872 | tf_op jit(solution)/shard_map/ppermute | solution.py:601
  681.4 44.0 %collective-permute-start.41 = (bf16[256,1024]{1,0:T(8,128)(2,1)S(1)}, bf16[256,1024]{1,0:T(8,128)(2,1)S(1)}, u32[]{:S(2)}, u32[]{:S(2)}) collective-permute-start(bf16[256,1024]{1,0:T(8,128)(2,1)S(1)} %get-tuple-element.193), channel_id=1, source_target_pairs={{0,8},{8,16},{16,24},{24,0},{1,9},{9,17},{17,25},{25,1},{2,10},{10... | collective-permute-start | bytes 1572872 | tf_op jit(solution)/shard_map/ppermute | solution.py:601
  (111 other events, 1578.9 us)
Sparse Core Ops, SparseCore 0:
  14.5 55.3 all-gather.4
  72.3 58.2 all-gather.6
  188.4 79.5 all-gather.8
  275.7 52.6 all-gather.10
  357.2 84.5 all-reduce.9
  513.8 165.9 all-reduce.11

commit v4 on v3

--- a/solution.py
+++ b/solution.py
@@ -10,6 +10,7 @@
 F32 = jnp.float32
 SPAN = 512
 PART = 128
+TILE = 256
 LOG2E = 1.4426950408889634
 EDGE = 128
 EPSILON = 1e-05
@@ -124,8 +125,8 @@
 
 def forward_kernel(
     heads, zx_ref, bc_ref, dt_ref, taps_ref, bc_taps_ref, dt_par_ref,
-    gated_ref, square_ref, enter_ref,
-    state, x_tail, bc_tail, carry, x_all, xd_all, tailed, scores_all, x_taps, bc_taps, matrix_ref,
+    gated_ref, square_ref, enter_ref, x_ref, slope_ref, y_ref,
+    state, x_tail, bc_tail, carry, xd_all, tailed, scores_all, x_taps, bc_taps, matrix_ref,
 ):
     span = zx_ref.shape[1]
     inner = state.shape[0]
@@ -154,9 +155,11 @@
         x_raw = zx_ref[(2 * h + 1) * size : (2 * h + 2) * size, :]
         pre = conv_of(x_tail[at, :], x_raw, taps_at(x_taps, at, span), matrix)
         x_tail[at, :] = x_raw[:, span - EDGE :]
-        x = pre * sigmoid(pre)
+        sig = sigmoid(pre)
+        x = pre * sig
         xd = x * steps[h : h + 1, :]
-        x_all[at, :] = x
+        x_ref[at, :] = x
+        slope_ref[at, :] = sig + x * (1.0 - sig)
         xd_all[at, :] = xd.astype(BF)
         tailed[at, :] = (xd * left[h : h + 1, :]).astype(BF)
     for q in parts:
@@ -178,7 +181,8 @@
             mixing = scores_all[q] * jnp.exp2(jnp.minimum(gap, 0.0))
             mixed.append(nn(xd_all[at, lanes(q)], mixing.astype(BF)))
         y = jnp.concatenate(mixed, axis=1) + carry[at, :] * grown[h : h + 1, :]
-        y = y + tap(5) * x_all[at, :]
+        y_ref[at, :] = y
+        y = y + tap(5) * x_ref[at, :]
         gated = y * (z * sigmoid(z))
         square = square + gated * gated
         gated_ref[at, :] = (gated * tap(6)).astype(BF)
@@ -186,11 +190,11 @@
 
 
 def backward_kernel(
-    heads, zx_ref, zx_before_ref, bc_ref, bc_before_ref, dt_ref, enter_ref, gn_ref, coef_ref,
+    heads, zx_ref, x_ref, slope_ref, y_ref, bc_ref, bc_before_ref, dt_ref, enter_ref, gn_ref, coef_ref,
     taps_ref, bc_taps_ref, dt_par_ref,
     gzx_ref, gx_sum_ref, gbc_sum_ref, gdt_sum_ref,
-    dstate, x_head, bc_head, carry, from_state, grown_g, tailed, x_acc, bc_acc, dt_acc, rsum, dsum,
-    x_all, slope_all, dxd_all, gy_all, scores_all, dscores_all, held_all, x_taps, bc_taps_all, matrix_ref,
+    dstate, x_head, bc_head, from_state, grown_g, tailed, x_acc, bc_acc, dt_acc, rsum, dsum,
+    dxd_all, gy_all, scores_all, dscores_all, held_all, x_taps, bc_taps_all, matrix_ref,
     back_matrix_ref,
 ):
     span = zx_ref.shape[1]
@@ -230,30 +234,22 @@
     for q in parts:
         scores_all[q] = scores[q]
         dscores_all[q] = jnp.zeros((PART, PART), F32)
-        carry[:, lanes(q)] = nn(enter_ref[q * inner : (q + 1) * inner, :], c_t[:, lanes(q)])
     coef = coef_ref[...]
     for h in range(heads):
         at = slice(h * size, (h + 1) * size)
         z = zx_ref[2 * h * size : (2 * h + 1) * size, :]
-        x_raw = zx_ref[(2 * h + 1) * size : (2 * h + 2) * size, :]
-        x_before = zx_before_ref[(2 * h + 1) * size : (2 * h + 2) * size, :] * live
         tap = taps_at(x_taps, at, span)
-        pre = conv_of(x_before, x_raw, tap, matrix)
-        sig = sigmoid(pre)
-        x = pre * sig
-        x_all[at, :] = x
-        slope_all[at, :] = sig + x * (1.0 - sig)
+        x = x_ref[at, :]
         xd = x * steps[h : h + 1, :]
         xd_low = xd.astype(BF)
         tailed[at, :] = (xd * left[h : h + 1, :]).astype(BF)
-        ratios, mixings, mixed = [], [], []
+        ratios, mixings = [], []
         for q in parts:
             gap = decay[h : h + 1, lanes(q)] - decay_n[q][:, h : h + 1]
             ratios.append(jnp.exp2(jnp.minimum(gap, 0.0)))
             mixings.append((scores_all[q] * ratios[q]).astype(BF))
-            mixed.append(nn(xd_low[:, lanes(q)], mixings[q]))
         grown_h = grown[h : h + 1, :]
-        y_scan = jnp.concatenate(mixed, axis=1) + carry[at, :] * grown_h
+        y_scan = y_ref[at, :]
         y = y_scan + tap(5) * x
         zsig = sigmoid(z)
         silu_z = z * zsig
@@ -291,7 +287,7 @@
         at = slice(h * size, (h + 1) * size)
         x_raw = zx_ref[(2 * h + 1) * size : (2 * h + 2) * size, :]
         tap = taps_at(x_taps, at, span)
-        x = x_all[at, :]
+        x = x_ref[at, :]
         steps_h = steps[h : h + 1, :]
         dx_state = from_state[at, :] * left[h : h + 1, :]
         dxd = dxd_all[at, :] + dx_state
@@ -302,7 +298,7 @@
         for q in parts:
             held_all[q, h : h + 1, :] = held_all[q, h : h + 1, :] + held[:, lanes(q)]
         dx = dxd * steps_h + tap(5) * gy_all[at, :].astype(F32)
-        gpre = dx * slope_all[at, :]
+        gpre = dx * slope_ref[at, :]
         g_raw, later = conv_back(gpre, x_head[at, :], tap, back_matrix)
         x_head[at, :] = gpre[:, :EDGE]
         gzx_ref[(2 * h + 1) * size : (2 * h + 2) * size, :] = g_raw.astype(BF)
@@ -364,17 +360,18 @@
             pl.BlockSpec((inner, span), lambda i: (0, i)),
             pl.BlockSpec((1, span), lambda i: (0, i)),
             pl.BlockSpec((span // PART * inner, states), lambda i: (i, 0)),
-        ],
+        ]
+        + [pl.BlockSpec((inner, span), lambda i: (0, i))] * 3,
         out_shape=[
             jax.ShapeDtypeStruct((inner, length), BF),
             jax.ShapeDtypeStruct((1, length), F32),
             jax.ShapeDtypeStruct((length // PART * inner, states), BF),
-        ],
+        ]
+        + [jax.ShapeDtypeStruct((inner, length), F32)] * 3,
         scratch_shapes=[
             pltpu.VMEM((inner, states), F32),
             pltpu.VMEM((inner, EDGE), F32),
             pltpu.VMEM((aux, EDGE), F32),
-            pltpu.VMEM((inner, span), F32),
             pltpu.VMEM((inner, span), F32),
             pltpu.VMEM((inner, span), BF),
             pltpu.VMEM((inner, span), BF),
@@ -383,12 +380,12 @@
             pltpu.VMEM((5, aux, EDGE), F32),
             pltpu.VMEM((2 * EDGE, 3 * EDGE), BF),
         ],
-        compiler_params=pltpu.CompilerParams(vmem_limit_bytes=48 * 2**20),
+        compiler_params=pltpu.CompilerParams(vmem_limit_bytes=56 * 2**20),
         name="scan_forward",
     )(zx, zx, zx, taps, bc_taps, dt_par)
 
 
-def scan_backward(zx, entering, gn, coef, taps, bc_taps, dt_par, heads, span=SPAN):
+def scan_backward(zx, kept, entering, gn, coef, taps, bc_taps, dt_par, heads, span=SPAN):
     inner = taps.shape[0]
     length = zx.shape[1]
     aux = bc_taps.shape[0]
@@ -405,7 +402,9 @@
         grid=(count,),
         in_specs=[
             pl.BlockSpec((2 * inner, span), lambda i: (0, rev(i))),
-            pl.BlockSpec((2 * inner, EDGE), lambda i: (0, before(i))),
+            pl.BlockSpec((inner, span), lambda i: (0, rev(i))),
+            pl.BlockSpec((inner, span), lambda i: (0, rev(i))),
+            pl.BlockSpec((inner, span), lambda i: (0, rev(i))),
             pl.BlockSpec((aux, span), lambda i: (2 * inner // aux, rev(i))),
             pl.BlockSpec((aux, EDGE), lambda i: (2 * inner // aux, before(i))),
             pl.BlockSpec((steps, span), lambda i: ((2 * inner + aux) // steps, rev(i))),
@@ -428,7 +427,6 @@
             pltpu.VMEM((inner, states), F32),
             pltpu.VMEM((inner, EDGE), F32),
             pltpu.VMEM((aux, EDGE), F32),
-            pltpu.VMEM((inner, span), F32),
             pltpu.VMEM((inner, span), F32),
             pltpu.VMEM((inner, span), BF),
             pltpu.VMEM((inner, span), BF),
@@ -438,8 +436,6 @@
             pltpu.VMEM((steps, span), F32),
             pltpu.VMEM((steps, span), F32),
             pltpu.VMEM((inner, span), F32),
-            pltpu.VMEM((inner, span), F32),
-            pltpu.VMEM((inner, span), F32),
             pltpu.VMEM((inner, span), BF),
             pltpu.VMEM((span // PART, PART, PART), F32),
             pltpu.VMEM((span // PART, PART, PART), F32),
@@ -451,7 +447,113 @@
         ],
         compiler_params=pltpu.CompilerParams(vmem_limit_bytes=56 * 2**20),
         name="scan_backward",
-    )(zx, zx, zx, zx, zx, entering, gn, coef, taps, bc_taps, dt_par)
+    )(zx, *kept, zx, zx, zx, entering, gn, coef, taps, bc_taps, dt_par)
+
+
+def product_kernel(form, count, added, *refs):
+    out_ref = refs[-1]
+    total = refs[2 * count][...].astype(F32) if added else None
+    for i in range(count):
+        a, b = refs[2 * i][...], refs[2 * i + 1][...]
+        if form == "tt":
+            a = a.T
+        over = 0 if form == "nn" else 1
+        term = lax.dot_general(a, b, (((1,), (over,)), ((), ())), preferred_element_type=F32)
+        total = term if total is None else total + term
+    out_ref[...] = total.astype(out_ref.dtype)
+
+
+def product(form, pairs, tile, added=None, dtype=BF, start=0, columns=None, wide=None):
+    first, other = pairs[0]
+    rows = columns or first.shape[1 if form == "tt" else 0]
+    cols = wide or other.shape[1 if form == "nn" else 0]
+    operands, specs = [], []
+    for a, b in pairs:
+        operands += [a, b]
+        if form == "tt":
+            specs.append(pl.BlockSpec((a.shape[0], tile), lambda i: (0, start // tile + i)))
+        else:
+            specs.append(pl.BlockSpec((tile, a.shape[1]), lambda i: (i, 0)))
+        block = b.shape if form == "nn" else (cols, b.shape[1])
+        specs.append(pl.BlockSpec(block, lambda i: (0, 0), pipeline_mode=pl.Buffered(1)))
+    if added is not None:
+        operands.append(added)
+        specs.append(pl.BlockSpec((tile, cols), lambda i: (i, 0)))
+    return pl.pallas_call(
+        functools.partial(product_kernel, form, len(pairs), added is not None),
+        grid=(rows // tile,),
+        in_specs=specs,
+        out_specs=pl.BlockSpec((tile, cols), lambda i: (i, 0)),
+        out_shape=jax.ShapeDtypeStruct((rows, cols), dtype),
+        compiler_params=pltpu.CompilerParams(vmem_limit_bytes=56 * 2**20),
+        name="product_" + form,
+    )(*operands)
+
+
+def late_kernel(count, wide, first, *refs):
+    scaled, g_all, g_tile = refs[:count], refs[count : 2 * count], refs[2 * count]
+    weights, outs = refs[2 * count + 1 : 2 * count + 3], refs[2 * count + 3 : 2 * count + 6]
+    held, sems = refs[2 * count + 6 : 2 * count + 8], refs[2 * count + 8]
+    step = pl.program_id(0)
+    copies = [pltpu.make_async_copy(weights[k], held[k], sems.at[k]) for k in range(2)]
+
+    @pl.when(step == 0)
+    def _():
+        for copy in copies:
+            copy.start()
+
+    @pl.when(step < first)
+    def _():
+        total = None
+        for s, g in zip(scaled, g_all):
+            term = nt(s[...].T, g[:wide, :])
+            total = term if total is None else total + term
+        outs[0][...] = total.astype(BF)
+
+    @pl.when(step == first)
+    def _():
+        for copy in copies:
+            copy.wait()
+
+    @pl.when(step >= first)
+    def _():
+        rows = g_tile[...].T
+        for k in range(2):
+            outs[1 + k][...] = nn(rows, held[k][...]).astype(BF)
+
+
+def late_products(scaled, g_in, own, other, wide):
+    depth, width = own.shape
+    length = scaled[0].shape[0]
+    first = width // TILE
+    count = len(scaled)
+    at = lambda i: jnp.maximum(i - first, 0)
+    until = lambda i: jnp.minimum(i, first - 1)
+    return pl.pallas_call(
+        functools.partial(late_kernel, count, wide, first),
+        grid=(first + length // TILE,),
+        in_specs=[pl.BlockSpec((length, TILE), lambda i: (0, first + until(i))) for _ in scaled]
+        + [pl.BlockSpec(g.shape, lambda i: (0, 0), pipeline_mode=pl.Buffered(1)) for g in g_in]
+        + [pl.BlockSpec((depth, TILE), lambda i: (0, at(i)))]
+        + [pl.BlockSpec(memory_space=pl.ANY)] * 2,
+        out_specs=[
+            pl.BlockSpec((TILE, wide), lambda i: (until(i), 0)),
+            pl.BlockSpec((TILE, width), lambda i: (at(i), 0)),
+            pl.BlockSpec((TILE, width), lambda i: (at(i), 0)),
+        ],
+        out_shape=[
+            jax.ShapeDtypeStruct((width, wide), BF),
+            jax.ShapeDtypeStruct((length, width), BF),
+            jax.ShapeDtypeStruct((length, width), BF),
+        ],
+        scratch_shapes=[
+            pltpu.VMEM(own.shape, BF),
+            pltpu.VMEM(own.shape, BF),
+            pltpu.SemaphoreType.DMA((2,)),
+        ],
+        compiler_params=pltpu.CompilerParams(vmem_limit_bytes=56 * 2**20),
+        name="late_products",
+    )(*scaled, *g_in, g_in[-1], own, other)
 
 
 def tie(value, *before):
@@ -690,7 +792,7 @@
     targets_own = widened(targets)
     positions = row_index * local_len + jnp.arange(local_len, dtype=jnp.int32)
 
-    zx, gated, entering, scatters = [], [], [], []
+    zx, gated, entering, kept_rows, scatters = [], [], [], [], []
     result, g_result, g_rows, coef = [], [], [], []
     loss_part = jnp.zeros((), F32)
 
@@ -722,7 +824,8 @@
             scatters[-1].second(projected)
             projected = tie(projected, *scatters[-1].passed)
         zx.append(projected)
-        g, square, e = scan_forward(projected, taps, bc_taps, dt_par, heads)
+        g, square, e, *kept = scan_forward(projected, taps, bc_taps, dt_par, heads)
+        kept_rows.append(kept)
         gated.append(g)
         entering.append(e)
         if k > 0:
@@ -742,6 +845,7 @@
         final = k == seq_col - 1
         whole = g_rows[k] if k == 0 else tie(g_rows[k], g_in[-1], coef[k])
         w_out_part = w_out_part + matmul(gated[k], whole, 1, 0)
+        gn = matmul(out_weight, tie(whole, w_out_part) if final else whole, 1, 1)
         before = (w_out_part,)
         if k == 0:
             dealt_output = dealt_rows(result)
@@ -751,14 +855,13 @@
             w_out_low = (w_out_part[:, :width_col] + received.astype(F32)).astype(BF)
             w_out_sum = lax.psum(w_out_low, "dp")
             before = (w_out_low,)
-        gn = matmul(out_weight, whole, 1, 1)
         if k > 0:
             scatters.append(to_rows(tie(g_in[-1], *before)))
             scatters[-1].first()
             before = scatters[-1].sent
         gn = tie(gn, *before)
         g, gx, gbc, gdt = scan_backward(
-            zx[k], entering[k], gn, coef[k], taps, bc_taps, dt_par, heads
+            zx[k], kept_rows[k], entering[k], gn, coef[k], taps, bc_taps, dt_par, heads
         )
         sums = [a + b for a, b in zip(sums, (gx, gbc, gdt), strict=True)]
         if k == 0:
@@ -768,17 +871,14 @@
             g = tie(g, *scatters[-1].passed)
         g_in.append(g)
 
-    def rows_of(start, g):
-        return sum(matmul(scaled[i][:, start : start + width_col], g[i], 0, 1) for i in range(seq_col))
-
-    g_in[-1] = tie(g_in[-1], w_out_sum)
-    g_wide = [g[:wide] for g in g_in]
-    there = rows_of(width_col, g_wide).astype(BF)
-    scatters.append(to_rows(tie(g_in[-1], there)))
+    there, left, right = late_products(scaled, g_in, in_own.T, in_other.T, wide)
+    there, left, right, g_in[-1] = tie((there, left, right, g_in[-1]), w_out_sum)
+    scatters.append(Scatter(left, right))
     scatters[-1].first()
-    g_wide[-1] = tie(g_wide[-1], *scatters[-1].sent)
-    in_low = (rows_of(0, g_wide) + other_col(there).astype(F32)).astype(BF)
-    in_low = tie(in_low.reshape(width_col, heads, pair))
+    g_late = g_in[:-1] + [tie(g_in[-1], *scatters[-1].sent)]
+    in_low = product(
+        "tt", list(zip(scaled, g_late)), TILE, added=other_col(there), columns=width_col, wide=wide
+    )
     scatters[-1].second(in_low)
     w_zx = lax.psum(in_low, "dp")
     g_aux = [g[wide:] for g in g_in]
@@ -800,7 +900,7 @@
     gain_part = jnp.zeros((model_width,), F32)
     g_u = []
     for k in range(seq_col):
-        g_scaled, _ = scatters[k].last()
+        g_scaled, _ = scatters[k].last(*((in_low,) if k < seq_col - 1 else ()))
         gain_part = gain_part + jnp.sum(g_scaled * u[k] * inv_rms[k], axis=0)
         weighted = g_scaled * gain[None, :]
         dot = jnp.sum(weighted * u[k], axis=1, keepdims=True) / model_width
@@ -830,7 +930,7 @@
         in_given_order(output_parts, dest_group),
         in_given_order(hidden_parts, dest_group),
         gain_sum,
-        w_zx.astype(F32),
+        w_zx.astype(F32).reshape(width_col, heads, pair),
         w_aux.astype(F32),
         gx[:, :4].T.reshape(4, heads, head_dim),
         gx[:, 4].reshape(heads, head_dim),

time: 741 us -> 725 us (0.978)
  matrix products: 144 us -> 100 us
  Pallas kernels: 96.3 us -> 138 us
  waiting for transfers between devices: 288 us -> 269 us
    dot_general x20 -> x14, matrix products: 144 us -> 100 us  [matmul(): lax.dot_general(a, b, (((over_a,), (over_b,)), ((), ())), preferred_eleme...]
    pallas_call x0 -> x2, Pallas kernels: none -> 42.7 us  [the longest x1 27.7 us: late_products(): pl.pallas_call(functools.partial(late_kernel, count, wide, first), grid=(...]
    ppermute x26, waiting for transfers between devices: 83.2 us -> 95.5 us  [flip(): return lax.ppermute(v, 'row', [(i, i ^ bit) for i in range(4)])]
    ppermute x6, waiting for transfers between devices: 58.3 us -> 47.2 us  [butterfly(): v = v + lax.ppermute(v, axis, [(i, i ^ bit) for i in range(count)])]
    psum x1, waiting for transfers between devices: 49.3 us -> 38.9 us  [per_device(): w_zx = lax.psum(in_low, 'dp')]
    pallas_call x2, Pallas kernels: 70 us -> 61.8 us  [scan_backward(): pl.pallas_call(body, grid=(count,), in_specs=[pl.BlockSpec((2 * inner, sp...]
    unnamed x178 -> x154, local copies, waits for them, and re-layouts: 28 us -> 26.1 us
  transfers between devices with their start and end apart: 55 -> 55, of which waited for: 26 -> 23; matrix products, arithmetic and copies ran while one was open for 31% -> 28% of each run, Pallas kernels for 13% -> 19%
where the time goes in v4:
time: 725 us; the launch traced here: 721 us
  waiting for transfers between devices  269 us (37%)
  Pallas kernels  138 us (19%)
  matrix products  100 us (14%)
  other arithmetic  91.2 us (13%)
  local copies, waits for them, and re-layouts  56.5 us (8%)
  starting transfers between devices  46.5 us (6%)
  between operations  19.7 us (3%)
    dot_general x14, matrix products, matmul(): lax.dot_general(a, b, (((over_a,), (over_b,)), ((), ())), preferred_eleme...  100 us
    ppermute x26, waiting for transfers between devices, flip(): return lax.ppermute(v, 'row', [(i, i ^ bit) for i in range(4)])  95.5 us
    pallas_call x2, Pallas kernels, scan_backward(): pl.pallas_call(body, grid=(count,), in_specs=[pl.BlockSpec((2 * inner, sp...  61.8 us
    ppermute x6, waiting for transfers between devices, butterfly(): v = v + lax.ppermute(v, axis, [(i, i ^ bit) for i in range(count)])  47.2 us
    all_gather x4, waiting for transfers between devices, per_device(): spread = lambda v: lax.all_gather(v, 'row', axis=0, tiled=True)  44.2 us
    psum x1, waiting for transfers between devices, per_device(): w_zx = lax.psum(in_low, 'dp')  38.9 us
    ppermute x6, waiting for transfers between devices, sent_back(): lax.ppermute(piece, 'dp', [(i, (i + hop) % groups) for i in range(groups)])  36.8 us
    pallas_call x2, Pallas kernels, scan_forward(): pl.pallas_call(body, grid=(length // span,), in_specs=[pl.BlockSpec((2 *...  33.3 us
  transfers between devices with their start and end apart: 55, of which 23 were waited for; matrix products, arithmetic and copies ran while one was open for 28% of the time, Pallas kernels for 19%

profile of v4, /device:TPU:0, one launch (start us, length us, event | category | flops | bytes accessed | tf_op | source)
XLA Modules:
  0.0 720.9 jit_solution(1709638708569476500)
XLA Ops:
  14.3 6.7 copy.58
  25.6 44.2 %all-gather.5.cloned.1.call-done.refs_0_ = bf16[1024,2048]{1,0:T(8,128)(2,1)} async-done(((bf16[256,2048]{1,0:T(8,128)(2,1)}), bf16[1024,2048]{1,0:T(8,128)(2,1)}) %all-gather.5.cloned.1.call-update) | async-done | bytes 4194320 | tf_op jit(solution)/shard_map/all_gather | solution.py:756
  73.7 5.6 pad_maximum_fusion
  83.0 13.1 %fusion.145.zx_ref.bc_ref.dt_ref.bc_before_ref = f32[2320,1024]{1,0:T(8,128)} fusion(bf16[2048,2320]{0,1:T(8,128)(2,1)S(1)} %pad_maximum_fusion, bf16[1024,2048]{1,0:T(8,128)(2,1)S(1)} %copy-done.4), kind=kOutput, calls=%fused_computation.346 | convolution fusion | flops 9730785280 | bytes 23199744 | tf_op jit(solution)/shard_map/dot_general | solution.py:718
  96.2 16.6 %scan_forward.2 = (bf16[1024,1024]{1,0:T(8,128)(2,1)}, f32[1,1024]{1,0:T(1,128)}, bf16[8192,128]{1,0:T(8,128)(2,1)}, f32[1024,1024]{1,0:T(8,128)}, f32[1024,1024]{1,0:T(8,128)}, /*index=5*/f32[1024,1024]{1,0:T(8,128)}) custom-call(f32[2320,1024]{1,0:T(8,128)} %fusion.145.zx_ref.bc_ref.dt_ref.bc_before_ref, ...), custom_call_target="tpu_custom_call" | custom-call | tf_op jit(solution)/shard_map/scan_forward/pallas_call | solution.py:350
  114.7 4.6 convolution_convert_fusion.5
  129.6 16.0 %fusion.146.zx_ref.bc_ref.dt_ref.bc_before_ref = f32[2320,1024]{1,0:T(8,128)} fusion(bf16[2048,2320]{0,1:T(8,128)(2,1)} %copy-done.6, bf16[1024,2048]{1,0:T(8,128)(2,1)} %all-gather.7.cloned.1.call-done.refs_1_.refs_2_), kind=kOutput, calls=%fused_computation.347 | convolution fusion | flops 9730785280 | bytes 23199744 | tf_op jit(solution)/shard_map/dot_general | solution.py:718
  145.6 8.5 %collective-permute-done.5 = bf16[2,256,1024]{2,1,0:T(8,128)(2,1)} collective-permute-done((bf16[2,256,1024]{2,1,0:T(8,128)(2,1)}, bf16[2,256,1024]{2,1,0:T(8,128)(2,1)}, u32[]{:S(2)}, u32[]{:S(2)}) %collective-permute-start.5) | collective-permute-done | bytes 1048608 | tf_op jit(solution)/shard_map/ppermute | solution.py:578
  166.8 16.7 %scan_forward.3 = (bf16[1024,1024]{1,0:T(8,128)(2,1)}, f32[1,1024]{1,0:T(1,128)}, bf16[8192,128]{1,0:T(8,128)(2,1)}, f32[1024,1024]{1,0:T(8,128)}, f32[1024,1024]{1,0:T(8,128)}, /*index=5*/f32[1024,1024]{1,0:T(8,128)}) custom-call(f32[2320,1024]{1,0:T(8,128)} %fusion.146.zx_ref.bc_ref.dt_ref.bc_before_ref, ...), custom_call_target="tpu_custom_call" | custom-call | tf_op jit(solution)/shard_map/scan_forward/pallas_call | solution.py:350
  195.6 4.6 convolution_convert_fusion.3
  214.5 4.7 pad_maximum_fusion.2
  219.3 25.9 %collective-permute-done.9 = f32[1,1024]{1,0:T(1,128)S(1)} collective-permute-done((f32[1,1024]{1,0:T(1,128)S(1)}, f32[1,1024]{1,0:T(1,128)S(1)}, u32[]{:S(2)}, u32[]{:S(2)}) %collective-permute-start.9) | collective-permute-done | bytes 4128 | tf_op jit(solution)/shard_map/ppermute | solution.py:578
  253.3 20.8 %collective-permute-done.15 = bf16[256,1024]{1,0:T(8,128)(2,1)S(1)} collective-permute-done((bf16[256,1024]{1,0:T(8,128)(2,1)S(1)}, bf16[256,1024]{1,0:T(8,128)(2,1)S(1)}, u32[]{:S(2)}, u32[]{:S(2)}) %collective-permute-start.15) | collective-permute-done | bytes 524320 | tf_op jit(solution)/shard_map/ppermute | solution.py:578
  300.7 6.1 fusion.147.gn_ref
  306.8 6.8 fusion.148
  313.5 30.8 %scan_backward.2 = (bf16[2320,1024]{1,0:T(8,128)(2,1)}, f32[1024,8]{1,0:T(8,128)}, f32[256,8]{1,0:T(8,128)}, f32[16,128]{1,0:T(8,128)}) custom-call(f32[2320,1024]{1,0:T(8,128)} %fusion.145.zx_ref.bc_ref.dt_ref.bc_before_ref, f32[1024,1024]{1,0:T(8,128)} %get-tuple-element.77.x_ref, f32[1024,1024]{1,0:T(8,128)} %get-tuple-element.78.slope_ref, ...), custom_call_target="tpu_custom_call" | custom-call | tf_op jit(solution)/shard_map/scan_backward/pallas_call | solution.py:400
  344.4 9.8 %convolution_add_fusion = f32[1024,2048]{1,0:T(8,128)S(1)} fusion(f32[1024,2048]{1,0:T(8,128)} %fusion.148, bf16[1024,1024]{1,0:T(8,128)(2,1)} %get-tuple-element.91, bf16[1024,2048]{1,0:T(8,128)(2,1)} %all-gather.11.cloned.1.call-done), kind=kOutput, calls=%fused_computation.19 | convolution fusion | flops 4297064448 | bytes 23068672 | tf_op jit(solution)/shard_map/dot_general | solution.py:718
  361.0 8.9 %convolution_convert_fusion.1 = bf16[1024,1024]{1,0:T(8,128)(2,1)S(1)} fusion(bf16[2320,1024]{1,0:T(8,128)(2,1)} %get-tuple-element.110.refs_2_.refs_1_, bf16[1024,2320]{0,1:T(8,128)(2,1)} %pad_maximum_fusion.1), kind=kOutput, calls=%fused_computation.67 | convolution fusion | flops 4866441216 | bytes 11599872 | tf_op jit(solution)/shard_map/dot_general | solution.py:718
  369.9 9.8 %convolution_convert_fusion = bf16[1024,1024]{1,0:T(8,128)(2,1)S(1)} fusion(bf16[2320,1024]{1,0:T(8,128)(2,1)} %get-tuple-element.110.refs_2_.refs_1_, bf16[1024,2320]{0,1:T(8,128)(2,1)} %collective-permute-done), kind=kOutput, calls=%fused_computation.66 | convolution fusion | flops 4866441216 | bytes 11599872 | tf_op jit(solution)/shard_map/dot_general | solution.py:718
  383.2 6.1 fusion.149.gn_ref
  389.2 31.0 %scan_backward.3 = (bf16[2320,1024]{1,0:T(8,128)(2,1)}, f32[1024,8]{1,0:T(8,128)}, f32[256,8]{1,0:T(8,128)}, f32[16,128]{1,0:T(8,128)}) custom-call(f32[2320,1024]{1,0:T(8,128)} %fusion.146.zx_ref.bc_ref.dt_ref.bc_before_ref, f32[1024,1024]{1,0:T(8,128)} %get-tuple-element.97.x_ref, f32[1024,1024]{1,0:T(8,128)} %get-tuple-element.98.slope_ref, ...), custom_call_target="tpu_custom_call" | custom-call | tf_op jit(solution)/shard_map/scan_backward/pallas_call | solution.py:400
  424.4 27.7 %late_products.1 = (bf16[1024,2048]{1,0:T(8,128)(2,1)}, bf16[1024,1024]{1,0:T(8,128)(2,1)}, bf16[1024,1024]{1,0:T(8,128)(2,1)}) custom-call(bf16[1024,2048]{1,0:T(8,128)(2,1)} %all-gather.5.cloned.1.call-done.refs_0_, bf16[1024,2048]{1,0:T(8,128)(2,1)} %all-gather.7.cloned.1.call-done.refs_1_.refs_2_, bf16[2320,1024]{1,0:T(8,128)(2,1)} %get-tuple-element.110.refs_2_.refs_1_, ...), custom_call_target="tpu_custom_call" | custom-call | tf_op jit(solution)/shard_map/late_products/pallas_call | solution.py:532
  464.7 15.0 %product_tt.1 = bf16[1024,2048]{1,0:T(8,128)(2,1)} custom-call(bf16[1024,2048]{1,0:T(8,128)(2,1)} %all-gather.5.cloned.1.call-done.refs_0_, bf16[2320,1024]{1,0:T(8,128)(2,1)} %get-tuple-element.110.refs_2_.refs_1_, bf16[1024,2048]{1,0:T(8,128)(2,1)} %all-gather.7.cloned.1.call-done.refs_1_.refs_2_, bf16[2320,1024]{1,0:T(8,128)(2,1)} %get-tuple-element.127.refs_3_.refs_4_, ...), custom_call_target="tpu_custom_call" | custom-call | tf_op jit(solution)/shard_map/product_tt/pallas_call | solution.py:482
  500.9 6.4 collective-permute-done.32
  522.4 11.0 %collective-permute-done.43 = f32[512,320]{0,1:T(8,128)} collective-permute-done((f32[512,320]{0,1:T(8,128)}, f32[512,320]{0,1:T(8,128)}, u32[]{:S(2)}, u32[]{:S(2)}) %collective-permute-start.43) | collective-permute-done | bytes 655392 | tf_op jit(solution)/shard_map/ppermute | solution.py:578
  536.9 7.3 %collective-permute-done.35 = f32[3073]{0:T(1024)S(1)} collective-permute-done((f32[3073]{0:T(1024)S(1)}, f32[3073]{0:T(1024)S(1)}, u32[]{:S(2)}, u32[]{:S(2)}) %collective-permute-start.35) | collective-permute-done | bytes 12324 | tf_op jit(solution)/shard_map/ppermute | solution.py:655
  547.5 25.6 %collective-permute-done.45 = f32[256,320]{0,1:T(8,128)S(1)} collective-permute-done((f32[256,320]{0,1:T(8,128)S(1)}, f32[256,320]{0,1:T(8,128)S(1)}, u32[]{:S(2)}, u32[]{:S(2)}) %collective-permute-start.45) | collective-permute-done | bytes 327712 | tf_op jit(solution)/shard_map/ppermute | solution.py:655
  580.4 12.4 %collective-permute-done.37 = f32[11297]{0:T(1024)S(1)} collective-permute-done((f32[11297]{0:T(1024)S(1)}, f32[11297]{0:T(1024)S(1)}, u32[]{:S(2)}, u32[]{:S(2)}) %collective-permute-start.37) | collective-permute-done | bytes 45220 | tf_op jit(solution)/shard_map/ppermute | solution.py:655
  609.1 12.2 %collective-permute-done.48 = f32[512,320]{0,1:T(8,128)S(1)} collective-permute-done((f32[512,320]{0,1:T(8,128)S(1)}, f32[512,320]{0,1:T(8,128)S(1)}, u32[]{:S(2)}, u32[]{:S(2)}) %collective-permute-start.48) | collective-permute-done | bytes 655392 | tf_op jit(solution)/shard_map/ppermute | solution.py:578
  622.6 38.9 %all-reduce.12.cloned.1.call-done = bf16[1024,2048]{1,0:T(8,128)(2,1)} async-done(((bf16[1024,2048]{1,0:T(8,128)(2,1)}), bf16[1024,2048]{1,0:T(8,128)(2,1)}) %all-reduce.12.cloned.1.call-update) | async-done | bytes 4194320 | tf_op jit(solution)/shard_map/psum | solution.py:883
  666.5 5.4 copy.70
  676.0 32.7 %collective-permute-done.40 = bf16[256,1024]{1,0:T(8,128)(2,1)S(1)} collective-permute-done((bf16[256,1024]{1,0:T(8,128)(2,1)S(1)}, bf16[256,1024]{1,0:T(8,128)(2,1)S(1)}, u32[]{:S(2)}, u32[]{:S(2)}) %collective-permute-start.40) | collective-permute-done | bytes 524320 | tf_op jit(solution)/shard_map/ppermute | solution.py:703
  (435 shorter events, 209.2 us)
Async XLA Ops:
  7.2 62.6 %all-gather.5.cloned.1.call-start = ((), (), s32[]{:S(2)}) async-start(), calls=%async_computation | async-start | bytes 5242880 | tf_op jit(solution)/shard_map/all_gather | solution.py:756
  14.3 115.3 %all-gather.7.cloned.1.call-start = ((), (), s32[]{:S(2)}) async-start(), calls=%async_computation.1 | async-start | bytes 5242880 | tf_op jit(solution)/shard_map/all_gather | solution.py:756
  25.2 48.5 %collective-permute-start = (bf16[1024,2320]{0,1:T(8,128)(2,1)}, bf16[1024,2320]{0,1:T(8,128)(2,1)}, u32[]{:S(2)}, u32[]{:S(2)}) collective-permute-start(bf16[1024,2320]{0,1:T(8,128)(2,1)} %pad_maximum_fusion.1), channel_id=1, source_target_pairs={{0,1},{1,0},{2,3},{3,2},{4,5},{5,4},{6,7},{7,6},{8,9},{9,8},{10,11... | collective-permute-start | bytes 14254088 | tf_op jit(solution)/shard_map/ppermute | solution.py:685
  69.8 212.6 %all-gather.9.cloned.1.call-start = ((), (), s32[]{:S(2)}) async-start(), calls=%async_computation.2 | async-start | bytes 5242880 | tf_op jit(solution)/shard_map/all_gather | solution.py:756
  70.4 51.8 %collective-permute-start.3 = (bf16[1024,1024]{1,0:T(8,128)(2,1)}, bf16[1024,1024]{1,0:T(8,128)(2,1)}, u32[]{:S(2)}, u32[]{:S(2)}) collective-permute-start(bf16[1024,1024]{1,0:T(8,128)(2,1)} %bitcast.341), channel_id=1, source_target_pairs={{0,1},{1,0},{2,3},{3,2},{4,5},{5,4},{6,7},{7,6},{8,9},{9,8},{10,11... | collective-permute-start | bytes 6291464 | tf_op jit(solution)/shard_map/ppermute | solution.py:685
  120.7 33.4 %collective-permute-start.4 = (bf16[2,272,1024]{2,1,0:T(8,128)(2,1)S(1)}, bf16[2,272,1024]{2,1,0:T(8,128)(2,1)}, u32[]{:S(2)}, u32[]{:S(2)}) collective-permute-start(bf16[2,272,1024]{2,1,0:T(8,128)(2,1)S(1)} %maximum_maximum_fusion), channel_id=1, source_target_pairs={{0,2},{2,0},{4,6},{6,4},{1,3},{3,1},{5,7},{7,5},{8,10},{10,8},{12,... | collective-permute-start | bytes 3342344 | tf_op jit(solution)/shard_map/ppermute | solution.py:578
  128.5 25.5 %collective-permute-start.5 = (bf16[2,256,1024]{2,1,0:T(8,128)(2,1)}, bf16[2,256,1024]{2,1,0:T(8,128)(2,1)}, u32[]{:S(2)}, u32[]{:S(2)}) collective-permute-start(bf16[2,256,1024]{2,1,0:T(8,128)(2,1)} %dynamic-slice_bitcast_fusion.6), channel_id=1, source_target_pairs={{0,4},{2,6},{4,0},{6,2},{1,5},{3,7},{5,1},{7,3},{8,12},{10,14},{12... | collective-permute-start | bytes 3145736 | tf_op jit(solution)/shard_map/ppermute | solution.py:578
  160.0 24.9 %collective-permute-start.7 = (bf16[256,1024]{1,0:T(8,128)(2,1)}, bf16[256,1024]{1,0:T(8,128)(2,1)}, u32[]{:S(2)}, u32[]{:S(2)}) collective-permute-start(bf16[256,1024]{1,0:T(8,128)(2,1)} %fusion.39), channel_id=1, source_target_pairs={{0,2},{2,0},{4,6},{6,4},{1,3},{3,1},{5,7},{7,5},{8,10},{10,8},{12,... | collective-permute-start | bytes 1572872 | tf_op jit(solution)/shard_map/ppermute | solution.py:578
  195.0 149.3 %all-gather.11.cloned.1.call-start = ((), (), s32[]{:S(2)}) async-start(), calls=%async_computation.3 | async-start | bytes 5242880 | tf_op jit(solution)/shard_map/all_gather | solution.py:756
  201.9 44.6 %collective-permute-start.12 = (bf16[2,272,1024]{2,1,0:T(8,128)(2,1)}, bf16[2,272,1024]{2,1,0:T(8,128)(2,1)}, u32[]{:S(2)}, u32[]{:S(2)}) collective-permute-start(bf16[2,272,1024]{2,1,0:T(8,128)(2,1)} %maximum_maximum_fusion.1), channel_id=1, source_target_pairs={{0,2},{2,0},{4,6},{6,4},{1,3},{3,1},{5,7},{7,5},{8,10},{10,8},{12,... | collective-permute-start | bytes 3342344 | tf_op jit(solution)/shard_map/ppermute | solution.py:578
  209.7 36.7 %collective-permute-start.13 = (bf16[2,256,1024]{2,1,0:T(8,128)(2,1)}, bf16[2,256,1024]{2,1,0:T(8,128)(2,1)}, u32[]{:S(2)}, u32[]{:S(2)}) collective-permute-start(bf16[2,256,1024]{2,1,0:T(8,128)(2,1)} %dynamic-slice_bitcast_fusion.4), channel_id=1, source_target_pairs={{0,4},{2,6},{4,0},{6,2},{1,5},{3,7},{5,1},{7,3},{8,12},{10,14},{12... | collective-permute-start | bytes 3145736 | tf_op jit(solution)/shard_map/ppermute | solution.py:578
  211.0 34.2 %collective-permute-start.9 = (f32[1,1024]{1,0:T(1,128)S(1)}, f32[1,1024]{1,0:T(1,128)S(1)}, u32[]{:S(2)}, u32[]{:S(2)}) collective-permute-start(f32[1,1024]{1,0:T(1,128)S(1)} %get-tuple-element.204), channel_id=1, source_target_pairs={{0,2},{2,0},{4,6},{6,4},{1,3},{3,1},{5,7},{7,5},{8,10},{10,8},{12,... | collective-permute-start | bytes 12296 | tf_op jit(solution)/shard_map/ppermute | solution.py:578
  212.0 33.2 %collective-permute-start.10 = (f32[1,1024]{1,0:T(1,128)S(1)}, f32[1,1024]{1,0:T(1,128)S(1)}, u32[]{:S(2)}, u32[]{:S(2)}) collective-permute-start(f32[1,1024]{1,0:T(1,128)S(1)} %get-tuple-element.204), channel_id=1, source_target_pairs={{0,4},{2,6},{4,0},{6,2},{1,5},{3,7},{5,1},{7,3},{8,12},{10,14},{12... | collective-permute-start | bytes 12296 | tf_op jit(solution)/shard_map/ppermute | solution.py:578
  213.1 32.8 %collective-permute-start.11 = (f32[1,1024]{1,0:T(1,128)S(1)}, f32[1,1024]{1,0:T(1,128)S(1)}, u32[]{:S(2)}, u32[]{:S(2)}) collective-permute-start(f32[1,1024]{1,0:T(1,128)S(1)} %get-tuple-element.204), channel_id=1, source_target_pairs={{0,6},{2,4},{4,2},{6,0},{1,7},{3,5},{5,3},{7,1},{8,14},{10,12},{12... | collective-permute-start | bytes 12296 | tf_op jit(solution)/shard_map/ppermute | solution.py:578
  249.1 25.6 %collective-permute-start.14 = (bf16[272,1024]{1,0:T(8,128)(2,1)S(1)}, bf16[272,1024]{1,0:T(8,128)(2,1)S(1)}, u32[]{:S(2)}, u32[]{:S(2)}) collective-permute-start(bf16[272,1024]{1,0:T(8,128)(2,1)S(1)} %pad_maximum_fusion.15), channel_id=1, source_target_pairs={{0,4},{2,6},{4,0},{6,2},{1,5},{3,7},{5,1},{7,3},{8,12},{10,14},{12... | collective-permute-start | bytes 1671176 | tf_op jit(solution)/shard_map/ppermute | solution.py:578
  282.4 169.8 %all-reduce.10.cloned.1.call-start = ((), (), s32[]{:S(2)}) async-start(), calls=%async_computation.4 | async-start | bytes 4194304 | tf_op jit(solution)/shard_map/psum | solution.py:856
  295.3 49.0 %collective-permute-start.17 = (bf16[256,1024]{1,0:T(8,128)(2,1)S(1)}, bf16[256,1024]{1,0:T(8,128)(2,1)}, u32[]{:S(2)}, u32[]{:S(2)}) collective-permute-start(bf16[256,1024]{1,0:T(8,128)(2,1)S(1)} %get-tuple-element.222), channel_id=1, source_target_pairs={{0,8},{8,16},{16,24},{24,0},{1,9},{9,17},{17,25},{25,1},{2,10},{10... | collective-permute-start | bytes 1572872 | tf_op jit(solution)/shard_map/ppermute | solution.py:703
  296.8 47.5 %collective-permute-start.18 = (bf16[256,1024]{1,0:T(8,128)(2,1)S(1)}, bf16[256,1024]{1,0:T(8,128)(2,1)}, u32[]{:S(2)}, u32[]{:S(2)}) collective-permute-start(bf16[256,1024]{1,0:T(8,128)(2,1)S(1)} %get-tuple-element.223), channel_id=1, source_target_pairs={{0,16},{8,24},{16,0},{24,8},{1,17},{9,25},{17,1},{25,9},{2,18},{10... | collective-permute-start | bytes 1572872 | tf_op jit(solution)/shard_map/ppermute | solution.py:703
  299.2 45.1 %collective-permute-start.19 = (bf16[256,1024]{1,0:T(8,128)(2,1)S(1)}, bf16[256,1024]{1,0:T(8,128)(2,1)}, u32[]{:S(2)}, u32[]{:S(2)}) collective-permute-start(bf16[256,1024]{1,0:T(8,128)(2,1)S(1)} %get-tuple-element.224), channel_id=1, source_target_pairs={{0,24},{8,0},{16,8},{24,16},{1,25},{9,1},{17,9},{25,17},{2,26},{10... | collective-permute-start | bytes 1572872 | tf_op jit(solution)/shard_map/ppermute | solution.py:703
  360.9 300.5 %all-reduce.12.cloned.1.call-start = ((), (), s32[]{:S(2)}) async-start(), calls=%async_computation.5 | async-start | bytes 8388608 | tf_op jit(solution)/shard_map/psum | solution.py:883
  379.8 40.4 %collective-permute-start.25 = (bf16[2,256,1024]{2,1,0:T(8,128)(2,1)S(1)}, bf16[2,256,1024]{2,1,0:T(8,128)(2,1)}, u32[]{:S(2)}, u32[]{:S(2)}) collective-permute-start(bf16[2,256,1024]{2,1,0:T(8,128)(2,1)S(1)} %dynamic-slice_bitcast_fusion.2), channel_id=1, source_target_pairs={{0,4},{2,6},{4,0},{6,2},{1,5},{3,7},{5,1},{7,3},{8,12},{10,14},{12... | collective-permute-start | bytes 3145736 | tf_op jit(solution)/shard_map/ppermute | solution.py:578
  382.4 37.9 %collective-permute-start.24 = (bf16[2,256,1024]{2,1,0:T(8,128)(2,1)}, bf16[2,256,1024]{2,1,0:T(8,128)(2,1)}, u32[]{:S(2)}, u32[]{:S(2)}) collective-permute-start(bf16[2,256,1024]{2,1,0:T(8,128)(2,1)} %dynamic-slice_bitcast_fusion.3), channel_id=1, source_target_pairs={{0,2},{2,0},{4,6},{6,4},{1,3},{3,1},{5,7},{7,5},{8,10},{10,8},{12,... | collective-permute-start | bytes 3145736 | tf_op jit(solution)/shard_map/ppermute | solution.py:578
  456.8 30.1 %collective-permute-start.30 = (bf16[2,256,1024]{2,1,0:T(8,128)(2,1)}, bf16[2,256,1024]{2,1,0:T(8,128)(2,1)}, u32[]{:S(2)}, u32[]{:S(2)}) collective-permute-start(bf16[2,256,1024]{2,1,0:T(8,128)(2,1)} %dynamic-slice_bitcast_fusion), channel_id=1, source_target_pairs={{0,4},{2,6},{4,0},{6,2},{1,5},{3,7},{5,1},{7,3},{8,12},{10,14},{12... | collective-permute-start | bytes 3145736 | tf_op jit(solution)/shard_map/ppermute | solution.py:578
  459.3 27.7 %collective-permute-start.29 = (bf16[2,256,1024]{2,1,0:T(8,128)(2,1)}, bf16[2,256,1024]{2,1,0:T(8,128)(2,1)}, u32[]{:S(2)}, u32[]{:S(2)}) collective-permute-start(bf16[2,256,1024]{2,1,0:T(8,128)(2,1)} %dynamic-slice_bitcast_fusion.1), channel_id=1, source_target_pairs={{0,2},{2,0},{4,6},{6,4},{1,3},{3,1},{5,7},{7,5},{8,10},{10,8},{12,... | collective-permute-start | bytes 3145736 | tf_op jit(solution)/shard_map/ppermute | solution.py:578
  461.6 35.2 %collective-permute-start.27 = (bf16[256,1024]{1,0:T(8,128)(2,1)}, bf16[256,1024]{1,0:T(8,128)(2,1)}, u32[]{:S(2)}, u32[]{:S(2)}) collective-permute-start(bf16[256,1024]{1,0:T(8,128)(2,1)} %fusion.30), channel_id=1, source_target_pairs={{0,2},{2,0},{4,6},{6,4},{1,3},{3,1},{5,7},{7,5},{8,10},{10,8},{12,... | collective-permute-start | bytes 1572872 | tf_op jit(solution)/shard_map/ppermute | solution.py:578
  462.9 33.9 %collective-permute-start.26 = (bf16[256,1024]{1,0:T(8,128)(2,1)}, bf16[256,1024]{1,0:T(8,128)(2,1)}, u32[]{:S(2)}, u32[]{:S(2)}) collective-permute-start(bf16[256,1024]{1,0:T(8,128)(2,1)} %fusion.31), channel_id=1, source_target_pairs={{0,4},{2,6},{4,0},{6,2},{1,5},{3,7},{5,1},{7,3},{8,12},{10,14},{12... | collective-permute-start | bytes 1572872 | tf_op jit(solution)/shard_map/ppermute | solution.py:578
  487.0 26.2 %collective-permute-start.42 = (f32[1024,272]{0,1:T(8,128)}, f32[1024,272]{0,1:T(8,128)S(1)}, u32[]{:S(2)}, u32[]{:S(2)}) collective-permute-start(f32[1024,272]{0,1:T(8,128)} %slice.272), channel_id=1, source_target_pairs={{0,1},{1,0},{2,3},{3,2},{4,5},{5,4},{6,7},{7,6},{8,9},{9,8},{10,11... | collective-permute-start | bytes 3342344 | tf_op jit(solution)/shard_map/ppermute | solution.py:685
  544.3 28.9 %collective-permute-start.45 = (f32[256,320]{0,1:T(8,128)S(1)}, f32[256,320]{0,1:T(8,128)S(1)}, u32[]{:S(2)}, u32[]{:S(2)}) collective-permute-start(f32[256,320]{0,1:T(8,128)S(1)} %dynamic-slice_add_fusion), channel_id=1, source_target_pairs={{0,8},{8,0},{16,24},{24,16},{1,9},{9,1},{17,25},{25,17},{2,10},{10... | collective-permute-start | bytes 983048 | tf_op jit(solution)/shard_map/ppermute | solution.py:655
  544.9 30.2 %collective-permute-start.36 = (f32[11297]{0:T(1024)S(1)}, f32[11297]{0:T(1024)S(1)}, u32[]{:S(2)}, u32[]{:S(2)}) collective-permute-start(f32[11297]{0:T(1024)S(1)} %pad_maximum_fusion.16), channel_id=1, source_target_pairs={{0,8},{8,0},{16,24},{24,16},{1,9},{9,1},{17,25},{25,17},{2,10},{10... | collective-permute-start | bytes 135572 | tf_op jit(solution)/shard_map/ppermute | solution.py:655
  547.5 61.3 %collective-permute-start.38 = (bf16[2,256,1024]{2,1,0:T(8,128)(2,1)}, bf16[2,256,1024]{2,1,0:T(8,128)(2,1)S(1)}, u32[]{:S(2)}, u32[]{:S(2)}) collective-permute-start(bf16[2,256,1024]{2,1,0:T(8,128)(2,1)} %pad_maximum_fusion.12), channel_id=1, source_target_pairs={{0,1},{1,0},{2,3},{3,2},{4,5},{5,4},{6,7},{7,6},{8,9},{9,8},{10,11... | collective-permute-start | bytes 3145736 | tf_op jit(solution)/shard_map/ppermute | solution.py:685
  662.9 45.9 %collective-permute-start.40 = (bf16[256,1024]{1,0:T(8,128)(2,1)S(1)}, bf16[256,1024]{1,0:T(8,128)(2,1)S(1)}, u32[]{:S(2)}, u32[]{:S(2)}) collective-permute-start(bf16[256,1024]{1,0:T(8,128)(2,1)S(1)} %get-tuple-element.218), channel_id=1, source_target_pairs={{0,16},{8,24},{16,0},{24,8},{1,17},{9,25},{17,1},{25,9},{2,18},{10... | collective-permute-start | bytes 1572872 | tf_op jit(solution)/shard_map/ppermute | solution.py:703
  663.2 45.6 %collective-permute-start.41 = (bf16[256,1024]{1,0:T(8,128)(2,1)S(1)}, bf16[256,1024]{1,0:T(8,128)(2,1)S(1)}, u32[]{:S(2)}, u32[]{:S(2)}) collective-permute-start(bf16[256,1024]{1,0:T(8,128)(2,1)S(1)} %get-tuple-element.217), channel_id=1, source_target_pairs={{0,8},{8,16},{16,24},{24,0},{1,9},{9,17},{17,25},{25,1},{2,10},{10... | collective-permute-start | bytes 1572872 | tf_op jit(solution)/shard_map/ppermute | solution.py:703
  (99 other events, 1345.8 us)
Sparse Core Ops, SparseCore 0:
  14.4 55.3 all-gather.4
  72.2 53.6 all-gather.6
  195.2 79.1 all-gather.8
  282.5 52.6 all-gather.10
  361.1 84.4 all-reduce.9
  497.0 164.4 all-reduce.11

commit v5 on v4

--- a/solution.py
+++ b/solution.py
@@ -578,6 +578,58 @@
     return lax.ppermute(v, "row", [(i, i ^ bit) for i in range(4)])
 
 
+class Gather:
+    def __init__(self, x, small=None):
+        self.count = lax.axis_size("row")
+        self.x, self.small, self.size = x, small, x.shape[0]
+        self.sent = x
+        if self.count == 4 and small is not None:
+            self.sent = jnp.concatenate([x, split(small, x.shape[1])], axis=0)
+
+    def first(self):
+        self.got = self.cross = (self.sent,)
+        if self.count == 4:
+            self.got = (flip(self.sent, 1), flip(self.sent, 2))
+
+    def second(self, *before):
+        self.cross = self.passing = self.got
+        if self.count == 4:
+            from_x, from_y = tie(self.got, *before)
+            self.passing = tie((from_y[: self.size // 2], from_x[self.size // 2 :]))
+            self.cross = (flip(self.passing[0], 1), flip(self.passing[1], 2))
+
+    def last(self, *before):
+        count, x, small, size = self.count, self.x, self.small, self.size
+        me = lax.axis_index("row")
+        if count != 4:
+            if small is not None:
+                placed = jnp.zeros((count * size,), F32)
+                placed = lax.dynamic_update_slice_in_dim(placed, small, me * size, 0)
+                small = butterfly(placed[None, :], "row")
+            return lax.all_gather(x, "row", axis=0, tiled=True), small
+        from_x, from_y = self.got
+        cross_a, cross_b = tie(self.cross, *before)
+        out = jnp.zeros((4 * size, x.shape[1]), x.dtype)
+        put = lambda o, v, bit, off: lax.dynamic_update_slice(o, v, ((me ^ bit) * size + off, 0))
+        out = put(out, x, 0, 0)
+        out = put(out, from_x[:size], 1, 0)
+        out = put(out, from_y[:size], 2, 0)
+        out = put(out, cross_a, 3, 0)
+        out = put(out, cross_b[: size // 2], 3, size // 2)
+        if small is not None:
+            whole = jnp.zeros((1, 4 * size), F32)
+            tails = (
+                small,
+                joined(from_x[size:], size),
+                joined(from_y[size:], size),
+                joined(cross_b[size // 2 :], size),
+            )
+            for bit, v in enumerate(tails):
+                whole = lax.dynamic_update_slice(whole, v[None, :], (0, (me ^ bit) * size))
+            small = whole
+        return out, small
+
+
 class Scatter:
     def __init__(self, left, right, small=None):
         self.count = lax.axis_size("row")
@@ -771,9 +823,6 @@
     )
     out_own = output_weight.reshape(inner, width_col)
     in_other, out_other = other_col(in_own), other_col(out_own)
-    in_weight = tie(jnp.concatenate([in_own, in_other], axis=0))
-
-    scaled[0] = tie(scaled[0], in_weight)
 
     column = lambda v: v.reshape(-1, 1)
     taps = jnp.concatenate(
@@ -792,7 +841,7 @@
     targets_own = widened(targets)
     positions = row_index * local_len + jnp.arange(local_len, dtype=jnp.int32)
 
-    zx, gated, entering, kept_rows, scatters = [], [], [], [], []
+    zx, gated, entering, kept_rows, scatters, gathers = [], [], [], [], [], []
     result, g_result, g_rows, coef = [], [], [], []
     loss_part = jnp.zeros((), F32)
 
@@ -812,30 +861,45 @@
         placed = lax.dynamic_update_slice_in_dim(
             jnp.zeros((local_len * row_count,), F32), share, row_index * local_len, 0
         )
+        sent = (grad * gate_inv).astype(BF)
+        if k < seq_col - 1:
+            gathers.append(Gather(sent, share))
+            gathers[-1].first()
+            return gathers[-1].sent
         coef.append(sum_over_row(placed[None, :]))
-        sent = (grad * gate_inv).astype(BF)
         g_rows.append(spread(tie(sent, *g_rows[-1:])))
         return sent
 
     for k in range(seq_col):
         source = scaled[k] if k == 0 else tie(scaled[k], *scatters[-1].sent)
-        projected = matmul(in_weight, source, 0, 1)
+        projected = matmul(in_own, source[:, :width_col], 0, 1) + matmul(
+            in_other, source[:, width_col:], 0, 1
+        )
         if k > 0:
             scatters[-1].second(projected)
             projected = tie(projected, *scatters[-1].passed)
+            projected = tie(projected, finish(k - 1, projected))
         zx.append(projected)
         g, square, e, *kept = scan_forward(projected, taps, bc_taps, dt_par, heads)
         kept_rows.append(kept)
         gated.append(g)
         entering.append(e)
-        if k > 0:
-            g = tie(g, finish(k - 1, g))
         left, right = (matmul(g, w, 0, 0).astype(BF) for w in (out_own, out_other))
         scatters.append(Scatter(left, right, square))
+        if k > 0:
+            gathers[-1].second(left, right)
+            scatters[-1].sent = tie(scatters[-1].sent, *gathers[-1].passing)
         scatters[-1].first()
     out_weight = tie(jnp.concatenate(tie((out_own, out_other), *scatters[-1].sent), axis=1))
-    scatters[-1].second(out_weight, *coef)
-    finish(seq_col - 1)
+    scatters[-1].second(out_weight)
+    for spread_k in gathers:
+        whole, c = spread_k.last()
+        g_rows.append(whole)
+        coef.append(c)
+    early = []
+    if seq_col > 1:
+        early = [matmul(out_weight, g_rows[0], 1, 1), matmul(gated[0], g_rows[0], 1, 0)]
+    finish(seq_col - 1, *early)
 
     to_rows = lambda g: Scatter(*(matmul(g, w, 0, 1).astype(BF) for w in (in_own, in_other)))
     g_in, scatters = [], []
@@ -844,8 +908,11 @@
     for k in range(seq_col):
         final = k == seq_col - 1
         whole = g_rows[k] if k == 0 else tie(g_rows[k], g_in[-1], coef[k])
-        w_out_part = w_out_part + matmul(gated[k], whole, 1, 0)
-        gn = matmul(out_weight, tie(whole, w_out_part) if final else whole, 1, 1)
+        if k == 0 and early:
+            gn, w_out_part = early
+        else:
+            w_out_part = w_out_part + matmul(gated[k], whole, 1, 0)
+            gn = matmul(out_weight, tie(whole, w_out_part) if final else whole, 1, 1)
         before = (w_out_part,)
         if k == 0:
             dealt_output = dealt_rows(result)
@@ -872,7 +939,9 @@
         g_in.append(g)
 
     there, left, right = late_products(scaled, g_in, in_own.T, in_other.T, wide)
-    there, left, right, g_in[-1] = tie((there, left, right, g_in[-1]), w_out_sum)
+    there, left, right, g_in[-1] = tie(
+        (there, left, right, g_in[-1]), w_out_sum, *(v for s in scatters for v in s.ended)
+    )
     scatters.append(Scatter(left, right))
     scatters[-1].first()
     g_late = g_in[:-1] + [tie(g_in[-1], *scatters[-1].sent)]

time: 725 us -> 697 us (0.961)
  waiting for transfers between devices: 269 us -> 251 us
  other arithmetic: 91.2 us -> 73.9 us
    ppermute x26 -> x27, waiting for transfers between devices: 95.5 us -> 66.1 us  [flip(): return lax.ppermute(v, 'row', [(i, i ^ bit) for i in range(4)])]
    dot_general x14 -> x16, matrix products: 100 us -> 106 us  [matmul(): lax.dot_general(a, b, (((over_a,), (over_b,)), ((), ())), preferred_eleme...]
    unnamed x154 -> x168, local copies, waits for them, and re-layouts: 26.1 us -> 21.1 us
    all_gather x4 -> x3, waiting for transfers between devices: 44.2 us -> 47.6 us  [per_device(): spread = lambda v: lax.all_gather(v, 'row', axis=0, tiled=True)]
    ppermute x26 -> x27, starting transfers between devices: 29.6 us -> 29.8 us  [flip(): return lax.ppermute(v, 'row', [(i, i ^ bit) for i in range(4)])]
  transfers between devices with their start and end apart: 55 -> 55, of which waited for: 23 -> 28; matrix products, arithmetic and copies ran while one was open for 28% -> 27% of each run, Pallas kernels for 19% -> 20%
where the time goes in v5:
time: 697 us; the launch traced here: 693 us
  waiting for transfers between devices  251 us (36%)
  Pallas kernels  138 us (20%)
  matrix products  106 us (15%)
  other arithmetic  73.9 us (11%)
  local copies, waits for them, and re-layouts  55.9 us (8%)
  starting transfers between devices  47.8 us (7%)
  between operations  19.9 us (3%)
    dot_general x16, matrix products, matmul(): lax.dot_general(a, b, (((over_a,), (over_b,)), ((), ())), preferred_eleme...  106 us
    ppermute x27, waiting for transfers between devices, flip(): return lax.ppermute(v, 'row', [(i, i ^ bit) for i in range(4)])  66.1 us
    pallas_call x2, Pallas kernels, scan_backward(): pl.pallas_call(body, grid=(count,), in_specs=[pl.BlockSpec((2 * inner, sp...  61.6 us
    ppermute x6, waiting for transfers between devices, butterfly(): v = v + lax.ppermute(v, axis, [(i, i ^ bit) for i in range(count)])  52.3 us
    all_gather x3, waiting for transfers between devices, per_device(): spread = lambda v: lax.all_gather(v, 'row', axis=0, tiled=True)  47.6 us
    psum x1, waiting for transfers between devices, per_device(): w_zx = lax.psum(in_low, 'dp')  41.9 us
    ppermute x6, waiting for transfers between devices, sent_back(): lax.ppermute(piece, 'dp', [(i, (i + hop) % groups) for i in range(groups)])  36.8 us
    pallas_call x2, Pallas kernels, scan_forward(): pl.pallas_call(body, grid=(length // span,), in_specs=[pl.BlockSpec((2 *...  33.8 us
  transfers between devices with their start and end apart: 55, of which 28 were waited for; matrix products, arithmetic and copies ran while one was open for 27% of the time, Pallas kernels for 20%

profile of v5, /device:TPU:0, one launch (start us, length us, event | category | flops | bytes accessed | tf_op | source)
XLA Modules:
  0.0 692.8 jit_solution(11046376428662971288)
XLA Ops:
  14.4 6.7 copy.58
  25.5 44.3 %all-gather.4.cloned.1.call-done.refs_0_ = bf16[1024,2048]{1,0:T(8,128)(2,1)} async-done(((bf16[256,2048]{1,0:T(8,128)(2,1)}), bf16[1024,2048]{1,0:T(8,128)(2,1)}) %all-gather.4.cloned.1.call-update) | async-done | bytes 4194320 | tf_op jit(solution)/shard_map/all_gather | solution.py:808
  78.0 8.3 %fusion.18 = f32[2320,1024]{1,0:T(8,128)S(1)} fusion(bf16[1024,2320]{0,1:T(8,128)(2,1)} %pad_maximum_fusion, bf16[1024,2048]{1,0:T(8,128)(2,1)} %all-gather.4.cloned.1.call-done.refs_0_), kind=kOutput, calls=%fused_computation.47 | convolution fusion | flops 4865392640 | bytes 16351232 | tf_op jit(solution)/shard_map/dot_general | solution.py:770
  86.3 9.9 %convolution_add_fusion.1.zx_ref.bc_ref.dt_ref.bc_before_ref = f32[2320,1024]{1,0:T(8,128)} fusion(f32[2320,1024]{1,0:T(8,128)S(1)} %fusion.18, bf16[1024,2320]{0,1:T(8,128)(2,1)} %collective-permute-done.2, bf16[1024,2048]{1,0:T(8,128)(2,1)S(1)} %copy-done.6), kind=kOutput, calls=%fused_computation.2 | convolution fusion | flops 4867768320 | bytes 25853952 | tf_op jit(solution)/shard_map/dot_general | solution.py:770
  96.2 17.2 %scan_forward.2 = (bf16[1024,1024]{1,0:T(8,128)(2,1)}, f32[1,1024]{1,0:T(1,128)}, bf16[8192,128]{1,0:T(8,128)(2,1)}, f32[1024,1024]{1,0:T(8,128)}, f32[1024,1024]{1,0:T(8,128)}, /*index=5*/f32[1024,1024]{1,0:T(8,128)}) custom-call(f32[2320,1024]{1,0:T(8,128)} %convolution_add_fusion.1.zx_ref.bc_ref.dt_ref.bc_before_ref, ...), custom_call_target="tpu_custom_call" | custom-call | tf_op jit(solution)/shard_map/scan_forward/pallas_call | solution.py:350
  115.3 4.6 convolution_convert_fusion.4
  129.5 7.8 %fusion.23 = f32[2320,1024]{1,0:T(8,128)S(1)} fusion(bf16[1024,2320]{0,1:T(8,128)(2,1)} %pad_maximum_fusion, bf16[1024,2048]{1,0:T(8,128)(2,1)} %all-gather.6.cloned.1.call-done.refs_1_.refs_2_), kind=kOutput, calls=%fused_computation.71 | convolution fusion | flops 4865392640 | bytes 16351232 | tf_op jit(solution)/shard_map/dot_general | solution.py:770
  137.4 10.6 %convolution_add_fusion.zx_ref.bc_ref.dt_ref.bc_before_ref = f32[2320,1024]{1,0:T(8,128)} fusion(f32[2320,1024]{1,0:T(8,128)S(1)} %fusion.23, bf16[1024,2320]{0,1:T(8,128)(2,1)} %collective-permute-done.2, bf16[1024,2048]{1,0:T(8,128)(2,1)S(1)} %copy-done.8), kind=kOutput, calls=%fused_computation.1 | convolution fusion | flops 4867768320 | bytes 25853952 | tf_op jit(solution)/shard_map/dot_general | solution.py:770
  148.1 6.8 collective-permute-done.4
  162.4 9.0 %collective-permute-done.7 = bf16[256,1024]{1,0:T(8,128)(2,1)S(1)} collective-permute-done((bf16[256,1024]{1,0:T(8,128)(2,1)S(1)}, bf16[256,1024]{1,0:T(8,128)(2,1)S(1)}, u32[]{:S(2)}, u32[]{:S(2)}) %collective-permute-start.7) | collective-permute-done | bytes 524320 | tf_op jit(solution)/shard_map/ppermute | solution.py:578
  183.4 16.6 %scan_forward.3 = (bf16[1024,1024]{1,0:T(8,128)(2,1)}, f32[1,1024]{1,0:T(1,128)}, bf16[8192,128]{1,0:T(8,128)(2,1)}, f32[1024,1024]{1,0:T(8,128)}, f32[1024,1024]{1,0:T(8,128)}, /*index=5*/f32[1024,1024]{1,0:T(8,128)}) custom-call(f32[2320,1024]{1,0:T(8,128)} %convolution_add_fusion.zx_ref.bc_ref.dt_ref.bc_before_ref, ...), custom_call_target="tpu_custom_call" | custom-call | tf_op jit(solution)/shard_map/scan_forward/pallas_call | solution.py:350
  201.4 4.6 convolution_convert_fusion.2
  231.0 6.1 fusion.161.gn_ref
  237.1 12.2 %collective-permute-done.14 = bf16[2,256,1024]{2,1,0:T(8,128)(2,1)S(1)} collective-permute-done((bf16[2,256,1024]{2,1,0:T(8,128)(2,1)S(1)}, bf16[2,256,1024]{2,1,0:T(8,128)(2,1)S(1)}, u32[]{:S(2)}, u32[]{:S(2)}) %collective-permute-start.14) | collective-permute-done | bytes 1048608 | tf_op jit(solution)/shard_map/ppermute | solution.py:578
  252.4 6.7 fusion.162
  282.0 30.8 %scan_backward.2 = (bf16[2320,1024]{1,0:T(8,128)(2,1)}, f32[1024,8]{1,0:T(8,128)}, f32[256,8]{1,0:T(8,128)}, f32[16,128]{1,0:T(8,128)}) custom-call(f32[2320,1024]{1,0:T(8,128)} %convolution_add_fusion.1.zx_ref.bc_ref.dt_ref.bc_before_ref, f32[1024,1024]{1,0:T(8,128)} %get-tuple-element.83.x_ref, f32[1024,1024]{1,0:T(8,128)} %get-tuple-element.84.slope_ref, ...), custom_call_target="tpu_custom_call" | custom-call | tf_op jit(solution)/shard_map/scan_backward/pallas_call | solution.py:400
  321.8 8.6 %convolution_add_fusion.2 = f32[1024,2048]{1,0:T(8,128)S(1)} fusion(f32[1024,2048]{1,0:T(8,128)} %fusion.162, bf16[1024,1024]{1,0:T(8,128)(2,1)S(1)} %copy-done.78, bf16[1024,2048]{1,0:T(8,128)(2,1)} %all-gather.8.cloned.1.call-done), kind=kOutput, calls=%fused_computation.20 | convolution fusion | flops 4297064448 | bytes 23068672 | tf_op jit(solution)/shard_map/dot_general | solution.py:770
  337.2 8.9 %convolution_convert_fusion.1 = bf16[1024,1024]{1,0:T(8,128)(2,1)S(1)} fusion(bf16[2320,1024]{1,0:T(8,128)(2,1)} %get-tuple-element.124.refs_2_.refs_1_, bf16[1024,2320]{0,1:T(8,128)(2,1)} %pad_maximum_fusion), kind=kOutput, calls=%fused_computation.74 | convolution fusion | flops 4866441216 | bytes 11599872 | tf_op jit(solution)/shard_map/dot_general | solution.py:770
  346.2 9.7 %convolution_convert_fusion = bf16[1024,1024]{1,0:T(8,128)(2,1)S(1)} fusion(bf16[2320,1024]{1,0:T(8,128)(2,1)} %get-tuple-element.124.refs_2_.refs_1_, bf16[1024,2320]{0,1:T(8,128)(2,1)} %collective-permute-done.2), kind=kOutput, calls=%fused_computation.73 | convolution fusion | flops 4866441216 | bytes 11599872 | tf_op jit(solution)/shard_map/dot_general | solution.py:770
  358.9 6.1 fusion.163.gn_ref
  364.9 30.8 %scan_backward.3 = (bf16[2320,1024]{1,0:T(8,128)(2,1)}, f32[1024,8]{1,0:T(8,128)}, f32[256,8]{1,0:T(8,128)}, f32[16,128]{1,0:T(8,128)}) custom-call(f32[2320,1024]{1,0:T(8,128)} %convolution_add_fusion.zx_ref.bc_ref.dt_ref.bc_before_ref, f32[1024,1024]{1,0:T(8,128)} %get-tuple-element.111.x_ref, f32[1024,1024]{1,0:T(8,128)} %get-tuple-element.112.slope_ref, ...), custom_call_target="tpu_custom_call" | custom-call | tf_op jit(solution)/shard_map/scan_backward/pallas_call | solution.py:400
  400.4 27.6 %late_products.1 = (bf16[1024,2048]{1,0:T(8,128)(2,1)}, bf16[1024,1024]{1,0:T(8,128)(2,1)}, bf16[1024,1024]{1,0:T(8,128)(2,1)}) custom-call(bf16[1024,2048]{1,0:T(8,128)(2,1)} %all-gather.4.cloned.1.call-done.refs_0_, bf16[1024,2048]{1,0:T(8,128)(2,1)} %all-gather.6.cloned.1.call-done.refs_1_.refs_2_, bf16[2320,1024]{1,0:T(8,128)(2,1)} %get-tuple-element.124.refs_2_.refs_1_, ...), custom_call_target="tpu_custom_call" | custom-call | tf_op jit(solution)/shard_map/late_products/pallas_call | solution.py:532
  439.1 15.1 %product_tt.1 = bf16[1024,2048]{1,0:T(8,128)(2,1)} custom-call(bf16[1024,2048]{1,0:T(8,128)(2,1)} %all-gather.4.cloned.1.call-done.refs_0_, bf16[2320,1024]{1,0:T(8,128)(2,1)} %get-tuple-element.124.refs_2_.refs_1_, bf16[1024,2048]{1,0:T(8,128)(2,1)} %all-gather.6.cloned.1.call-done.refs_1_.refs_2_, bf16[2320,1024]{1,0:T(8,128)(2,1)} %get-tuple-element.141.refs_3_.refs_4_, ...), custom_call_target="tpu_custom_call" | custom-call | tf_op jit(solution)/shard_map/product_tt/pallas_call | solution.py:482
  492.9 10.9 %collective-permute-done.44 = f32[512,320]{0,1:T(8,128)} collective-permute-done((f32[512,320]{0,1:T(8,128)}, f32[512,320]{0,1:T(8,128)}, u32[]{:S(2)}, u32[]{:S(2)}) %collective-permute-start.44) | collective-permute-done | bytes 655392 | tf_op jit(solution)/shard_map/ppermute | solution.py:578
  508.1 6.5 collective-permute-done.36
  520.0 26.4 %collective-permute-done.46 = f32[256,320]{0,1:T(8,128)S(1)} collective-permute-done((f32[256,320]{0,1:T(8,128)S(1)}, f32[256,320]{0,1:T(8,128)S(1)}, u32[]{:S(2)}, u32[]{:S(2)}) %collective-permute-start.46) | collective-permute-done | bytes 327712 | tf_op jit(solution)/shard_map/ppermute | solution.py:707
  552.0 17.7 %collective-permute-done.38 = f32[11297]{0:T(1024)S(1)} collective-permute-done((f32[11297]{0:T(1024)S(1)}, f32[11297]{0:T(1024)S(1)}, u32[]{:S(2)}, u32[]{:S(2)}) %collective-permute-start.38) | collective-permute-done | bytes 45220 | tf_op jit(solution)/shard_map/ppermute | solution.py:707
  583.9 7.1 %collective-permute-done.49 = f32[512,320]{0,1:T(8,128)S(1)} collective-permute-done((f32[512,320]{0,1:T(8,128)S(1)}, f32[512,320]{0,1:T(8,128)S(1)}, u32[]{:S(2)}, u32[]{:S(2)}) %collective-permute-start.49) | collective-permute-done | bytes 655392 | tf_op jit(solution)/shard_map/ppermute | solution.py:578
  592.3 41.9 %all-reduce.13.cloned.1.call-done = bf16[1024,2048]{1,0:T(8,128)(2,1)} async-done(((bf16[1024,2048]{1,0:T(8,128)(2,1)}), bf16[1024,2048]{1,0:T(8,128)(2,1)}) %all-reduce.13.cloned.1.call-update) | async-done | bytes 4194320 | tf_op jit(solution)/shard_map/psum | solution.py:952
  638.6 5.4 copy.70
  644.1 16.8 %collective-permute-done.40 = bf16[256,1024]{1,0:T(8,128)(2,1)S(1)} collective-permute-done((bf16[256,1024]{1,0:T(8,128)(2,1)S(1)}, bf16[256,1024]{1,0:T(8,128)(2,1)S(1)}, u32[]{:S(2)}, u32[]{:S(2)}) %collective-permute-start.40) | collective-permute-done | bytes 524320 | tf_op jit(solution)/shard_map/ppermute | solution.py:755
  660.8 20.0 %collective-permute-done.41 = bf16[256,1024]{1,0:T(8,128)(2,1)S(1)} collective-permute-done((bf16[256,1024]{1,0:T(8,128)(2,1)S(1)}, bf16[256,1024]{1,0:T(8,128)(2,1)S(1)}, u32[]{:S(2)}, u32[]{:S(2)}) %collective-permute-start.41) | collective-permute-done | bytes 524320 | tf_op jit(solution)/shard_map/ppermute | solution.py:755
  (463 shorter events, 211.1 us)
Async XLA Ops:
  7.2 62.6 %all-gather.4.cloned.1.call-start = ((), (), s32[]{:S(2)}) async-start(), calls=%async_computation | async-start | bytes 5242880 | tf_op jit(solution)/shard_map/all_gather | solution.py:808
  14.3 115.2 %all-gather.6.cloned.1.call-start = ((), (), s32[]{:S(2)}) async-start(), calls=%async_computation.1 | async-start | bytes 5242880 | tf_op jit(solution)/shard_map/all_gather | solution.py:808
  25.1 61.2 %collective-permute-start.2 = (bf16[1024,2320]{0,1:T(8,128)(2,1)}, bf16[1024,2320]{0,1:T(8,128)(2,1)}, u32[]{:S(2)}, u32[]{:S(2)}) collective-permute-start(bf16[1024,2320]{0,1:T(8,128)(2,1)} %pad_maximum_fusion), channel_id=1, source_target_pairs={{0,1},{1,0},{2,3},{3,2},{4,5},{5,4},{6,7},{7,6},{8,9},{9,8},{10,11... | collective-permute-start | bytes 14254088 | tf_op jit(solution)/shard_map/ppermute | solution.py:737
  69.9 251.9 %all-gather.8.cloned.1.call-start = ((), (), s32[]{:S(2)}) async-start(), calls=%async_computation.2 | async-start | bytes 5242880 | tf_op jit(solution)/shard_map/all_gather | solution.py:808
  72.9 102.0 %collective-permute-start.8 = (bf16[2,256,1024]{2,1,0:T(8,128)(2,1)}, bf16[2,256,1024]{2,1,0:T(8,128)(2,1)}, u32[]{:S(2)}, u32[]{:S(2)}) collective-permute-start(bf16[2,256,1024]{2,1,0:T(8,128)(2,1)} %get-tuple-element.244), channel_id=1, source_target_pairs={{0,1},{1,0},{2,3},{3,2},{4,5},{5,4},{6,7},{7,6},{8,9},{9,8},{10,11... | collective-permute-start | bytes 3145736 | tf_op jit(solution)/shard_map/ppermute | solution.py:737
  73.0 42.3 %collective-permute-start.3 = (bf16[1024,1024]{1,0:T(8,128)(2,1)}, bf16[1024,1024]{1,0:T(8,128)(2,1)}, u32[]{:S(2)}, u32[]{:S(2)}) collective-permute-start(bf16[1024,1024]{1,0:T(8,128)(2,1)} %bitcast.8), channel_id=1, source_target_pairs={{0,1},{1,0},{2,3},{3,2},{4,5},{5,4},{6,7},{7,6},{8,9},{9,8},{10,11... | collective-permute-start | bytes 6291464 | tf_op jit(solution)/shard_map/ppermute | solution.py:737
  120.9 27.1 %collective-permute-start.5 = (bf16[2,256,1024]{2,1,0:T(8,128)(2,1)}, bf16[2,256,1024]{2,1,0:T(8,128)(2,1)}, u32[]{:S(2)}, u32[]{:S(2)}) collective-permute-start(bf16[2,256,1024]{2,1,0:T(8,128)(2,1)} %dynamic-slice_bitcast_fusion.6), channel_id=1, source_target_pairs={{0,4},{2,6},{4,0},{6,2},{1,5},{3,7},{5,1},{7,3},{8,12},{10,14},{12... | collective-permute-start | bytes 3145736 | tf_op jit(solution)/shard_map/ppermute | solution.py:578
  128.3 26.6 %collective-permute-start.4 = (bf16[2,272,1024]{2,1,0:T(8,128)(2,1)}, bf16[2,272,1024]{2,1,0:T(8,128)(2,1)}, u32[]{:S(2)}, u32[]{:S(2)}) collective-permute-start(bf16[2,272,1024]{2,1,0:T(8,128)(2,1)} %maximum_maximum_fusion), channel_id=1, source_target_pairs={{0,2},{2,0},{4,6},{6,4},{1,3},{3,1},{5,7},{7,5},{8,10},{10,8},{12,... | collective-permute-start | bytes 3342344 | tf_op jit(solution)/shard_map/ppermute | solution.py:578
  181.3 30.4 %collective-permute-start.10 = (bf16[272,2048]{1,0:T(8,128)(2,1)}, bf16[272,2048]{1,0:T(8,128)(2,1)}, u32[]{:S(2)}, u32[]{:S(2)}) collective-permute-start(bf16[272,2048]{1,0:T(8,128)(2,1)} %pad_maximum_fusion.6), channel_id=1, source_target_pairs={{0,4},{2,6},{4,0},{6,2},{1,5},{3,7},{5,1},{7,3},{8,12},{10,14},{12... | collective-permute-start | bytes 3342344 | tf_op jit(solution)/shard_map/ppermute | solution.py:578
  181.7 30.1 %collective-permute-start.9 = (bf16[272,2048]{1,0:T(8,128)(2,1)}, bf16[272,2048]{1,0:T(8,128)(2,1)}, u32[]{:S(2)}, u32[]{:S(2)}) collective-permute-start(bf16[272,2048]{1,0:T(8,128)(2,1)} %pad_maximum_fusion.6), channel_id=1, source_target_pairs={{0,2},{2,0},{4,6},{6,4},{1,3},{3,1},{5,7},{7,5},{8,10},{10,8},{12,... | collective-permute-start | bytes 3342344 | tf_op jit(solution)/shard_map/ppermute | solution.py:578
  216.3 33.0 %collective-permute-start.14 = (bf16[2,256,1024]{2,1,0:T(8,128)(2,1)S(1)}, bf16[2,256,1024]{2,1,0:T(8,128)(2,1)S(1)}, u32[]{:S(2)}, u32[]{:S(2)}) collective-permute-start(bf16[2,256,1024]{2,1,0:T(8,128)(2,1)S(1)} %dynamic-slice_bitcast_fusion.4), channel_id=1, source_target_pairs={{0,4},{2,6},{4,0},{6,2},{1,5},{3,7},{5,1},{7,3},{8,12},{10,14},{12... | collective-permute-start | bytes 3145736 | tf_op jit(solution)/shard_map/ppermute | solution.py:578
  216.6 33.0 %collective-permute-start.13 = (bf16[2,272,1024]{2,1,0:T(8,128)(2,1)S(1)}, bf16[2,272,1024]{2,1,0:T(8,128)(2,1)S(1)}, u32[]{:S(2)}, u32[]{:S(2)}) collective-permute-start(bf16[2,272,1024]{2,1,0:T(8,128)(2,1)S(1)} %maximum_maximum_fusion.1), channel_id=1, source_target_pairs={{0,2},{2,0},{4,6},{6,4},{1,3},{3,1},{5,7},{7,5},{8,10},{10,8},{12,... | collective-permute-start | bytes 3342344 | tf_op jit(solution)/shard_map/ppermute | solution.py:578
  268.8 160.0 %all-reduce.11.cloned.1.call-start = ((), (), s32[]{:S(2)}) async-start(), calls=%async_computation.3 | async-start | bytes 4194304 | tf_op jit(solution)/shard_map/psum | solution.py:923
  273.3 40.9 %collective-permute-start.21 = (f32[1,1024]{1,0:T(1,128)S(1)}, f32[1,1024]{1,0:T(1,128)S(1)}, u32[]{:S(2)}, u32[]{:S(2)}) collective-permute-start(f32[1,1024]{1,0:T(1,128)S(1)} %get-tuple-element.213), channel_id=1, source_target_pairs={{0,2},{2,0},{4,6},{6,4},{1,3},{3,1},{5,7},{7,5},{8,10},{10,8},{12,... | collective-permute-start | bytes 12296 | tf_op jit(solution)/shard_map/ppermute | solution.py:578
  276.0 42.5 %collective-permute-start.18 = (bf16[256,1024]{1,0:T(8,128)(2,1)S(1)}, bf16[256,1024]{1,0:T(8,128)(2,1)}, u32[]{:S(2)}, u32[]{:S(2)}) collective-permute-start(bf16[256,1024]{1,0:T(8,128)(2,1)S(1)} %get-tuple-element.238), channel_id=1, source_target_pairs={{0,8},{8,16},{16,24},{24,0},{1,9},{9,17},{17,25},{25,1},{2,10},{10... | collective-permute-start | bytes 1572872 | tf_op jit(solution)/shard_map/ppermute | solution.py:755
  277.5 41.0 %collective-permute-start.19 = (bf16[256,1024]{1,0:T(8,128)(2,1)S(1)}, bf16[256,1024]{1,0:T(8,128)(2,1)}, u32[]{:S(2)}, u32[]{:S(2)}) collective-permute-start(bf16[256,1024]{1,0:T(8,128)(2,1)S(1)} %get-tuple-element.239), channel_id=1, source_target_pairs={{0,16},{8,24},{16,0},{24,8},{1,17},{9,25},{17,1},{25,9},{2,18},{10... | collective-permute-start | bytes 1572872 | tf_op jit(solution)/shard_map/ppermute | solution.py:755
  279.9 38.5 %collective-permute-start.20 = (bf16[256,1024]{1,0:T(8,128)(2,1)S(1)}, bf16[256,1024]{1,0:T(8,128)(2,1)}, u32[]{:S(2)}, u32[]{:S(2)}) collective-permute-start(bf16[256,1024]{1,0:T(8,128)(2,1)S(1)} %get-tuple-element.240), channel_id=1, source_target_pairs={{0,24},{8,0},{16,8},{24,16},{1,25},{9,1},{17,9},{25,17},{2,26},{10... | collective-permute-start | bytes 1572872 | tf_op jit(solution)/shard_map/ppermute | solution.py:755
  337.2 297.0 %all-reduce.13.cloned.1.call-start = ((), (), s32[]{:S(2)}) async-start(), calls=%async_computation.4 | async-start | bytes 8388608 | tf_op jit(solution)/shard_map/psum | solution.py:952
  356.0 39.8 %collective-permute-start.26 = (bf16[2,256,1024]{2,1,0:T(8,128)(2,1)S(1)}, bf16[2,256,1024]{2,1,0:T(8,128)(2,1)}, u32[]{:S(2)}, u32[]{:S(2)}) collective-permute-start(bf16[2,256,1024]{2,1,0:T(8,128)(2,1)S(1)} %dynamic-slice_bitcast_fusion.2), channel_id=1, source_target_pairs={{0,4},{2,6},{4,0},{6,2},{1,5},{3,7},{5,1},{7,3},{8,12},{10,14},{12... | collective-permute-start | bytes 3145736 | tf_op jit(solution)/shard_map/ppermute | solution.py:578
  357.5 38.3 %collective-permute-start.25 = (bf16[2,256,1024]{2,1,0:T(8,128)(2,1)S(1)}, bf16[2,256,1024]{2,1,0:T(8,128)(2,1)}, u32[]{:S(2)}, u32[]{:S(2)}) collective-permute-start(bf16[2,256,1024]{2,1,0:T(8,128)(2,1)S(1)} %dynamic-slice_bitcast_fusion.3), channel_id=1, source_target_pairs={{0,2},{2,0},{4,6},{6,4},{1,3},{3,1},{5,7},{7,5},{8,10},{10,8},{12,... | collective-permute-start | bytes 3145736 | tf_op jit(solution)/shard_map/ppermute | solution.py:578
  398.3 29.7 %collective-permute-start.28 = (bf16[256,1024]{1,0:T(8,128)(2,1)S(1)}, bf16[256,1024]{1,0:T(8,128)(2,1)S(1)}, u32[]{:S(2)}, u32[]{:S(2)}) collective-permute-start(bf16[256,1024]{1,0:T(8,128)(2,1)S(1)} %fusion.36), channel_id=1, source_target_pairs={{0,2},{2,0},{4,6},{6,4},{1,3},{3,1},{5,7},{7,5},{8,10},{10,8},{12,... | collective-permute-start | bytes 1572872 | tf_op jit(solution)/shard_map/ppermute | solution.py:578
  399.9 28.9 %collective-permute-start.27 = (bf16[256,1024]{1,0:T(8,128)(2,1)S(1)}, bf16[256,1024]{1,0:T(8,128)(2,1)}, u32[]{:S(2)}, u32[]{:S(2)}) collective-permute-start(bf16[256,1024]{1,0:T(8,128)(2,1)S(1)} %fusion.37), channel_id=1, source_target_pairs={{0,4},{2,6},{4,0},{6,2},{1,5},{3,7},{5,1},{7,3},{8,12},{10,14},{12... | collective-permute-start | bytes 1572872 | tf_op jit(solution)/shard_map/ppermute | solution.py:578
  432.2 25.8 %collective-permute-start.30 = (bf16[2,256,1024]{2,1,0:T(8,128)(2,1)}, bf16[2,256,1024]{2,1,0:T(8,128)(2,1)S(1)}, u32[]{:S(2)}, u32[]{:S(2)}) collective-permute-start(bf16[2,256,1024]{2,1,0:T(8,128)(2,1)} %dynamic-slice_bitcast_fusion.1), channel_id=1, source_target_pairs={{0,2},{2,0},{4,6},{6,4},{1,3},{3,1},{5,7},{7,5},{8,10},{10,8},{12,... | collective-permute-start | bytes 3145736 | tf_op jit(solution)/shard_map/ppermute | solution.py:578
  433.6 25.6 %collective-permute-start.31 = (bf16[2,256,1024]{2,1,0:T(8,128)(2,1)}, bf16[2,256,1024]{2,1,0:T(8,128)(2,1)}, u32[]{:S(2)}, u32[]{:S(2)}) collective-permute-start(bf16[2,256,1024]{2,1,0:T(8,128)(2,1)} %dynamic-slice_bitcast_fusion), channel_id=1, source_target_pairs={{0,4},{2,6},{4,0},{6,2},{1,5},{3,7},{5,1},{7,3},{8,12},{10,14},{12... | collective-permute-start | bytes 3145736 | tf_op jit(solution)/shard_map/ppermute | solution.py:578
  514.7 31.7 %collective-permute-start.46 = (f32[256,320]{0,1:T(8,128)S(1)}, f32[256,320]{0,1:T(8,128)S(1)}, u32[]{:S(2)}, u32[]{:S(2)}) collective-permute-start(f32[256,320]{0,1:T(8,128)S(1)} %dynamic-slice_add_fusion), channel_id=1, source_target_pairs={{0,8},{8,0},{16,24},{24,16},{1,9},{9,1},{17,25},{25,17},{2,10},{10... | collective-permute-start | bytes 983048 | tf_op jit(solution)/shard_map/ppermute | solution.py:707
  518.9 29.3 %collective-permute-start.37 = (f32[11297]{0:T(1024)S(1)}, f32[11297]{0:T(1024)S(1)}, u32[]{:S(2)}, u32[]{:S(2)}) collective-permute-start(f32[11297]{0:T(1024)S(1)} %pad_maximum_fusion.16), channel_id=1, source_target_pairs={{0,8},{8,0},{16,24},{24,16},{1,9},{9,1},{17,25},{25,17},{2,10},{10... | collective-permute-start | bytes 135572 | tf_op jit(solution)/shard_map/ppermute | solution.py:707
  520.0 62.4 %collective-permute-start.39 = (bf16[2,256,1024]{2,1,0:T(8,128)(2,1)}, bf16[2,256,1024]{2,1,0:T(8,128)(2,1)}, u32[]{:S(2)}, u32[]{:S(2)}) collective-permute-start(bf16[2,256,1024]{2,1,0:T(8,128)(2,1)} %pad_maximum_fusion.12), channel_id=1, source_target_pairs={{0,1},{1,0},{2,3},{3,2},{4,5},{5,4},{6,7},{7,6},{8,9},{9,8},{10,11... | collective-permute-start | bytes 3145736 | tf_op jit(solution)/shard_map/ppermute | solution.py:737
  546.4 25.5 %collective-permute-start.47 = (f32[256,320]{0,1:T(8,128)S(1)}, f32[256,320]{0,1:T(8,128)S(1)}, u32[]{:S(2)}, u32[]{:S(2)}) collective-permute-start(f32[256,320]{0,1:T(8,128)S(1)} %add.767), channel_id=1, source_target_pairs={{0,16},{8,24},{16,0},{24,8},{1,17},{9,25},{17,1},{25,9},{2,18},{10... | collective-permute-start | bytes 983048 | tf_op jit(solution)/shard_map/ppermute | solution.py:707
  548.3 21.5 %collective-permute-start.38 = (f32[11297]{0:T(1024)S(1)}, f32[11297]{0:T(1024)S(1)}, u32[]{:S(2)}, u32[]{:S(2)}) collective-permute-start(f32[11297]{0:T(1024)S(1)} %fusion.192), channel_id=1, source_target_pairs={{0,16},{8,24},{16,0},{24,8},{1,17},{9,25},{17,1},{25,9},{2,18},{10... | collective-permute-start | bytes 135572 | tf_op jit(solution)/shard_map/ppermute | solution.py:707
  634.4 26.4 %collective-permute-start.40 = (bf16[256,1024]{1,0:T(8,128)(2,1)S(1)}, bf16[256,1024]{1,0:T(8,128)(2,1)S(1)}, u32[]{:S(2)}, u32[]{:S(2)}) collective-permute-start(bf16[256,1024]{1,0:T(8,128)(2,1)S(1)} %get-tuple-element.231), channel_id=1, source_target_pairs={{0,24},{8,0},{16,8},{24,16},{1,25},{9,1},{17,9},{25,17},{2,26},{10... | collective-permute-start | bytes 1572872 | tf_op jit(solution)/shard_map/ppermute | solution.py:755
  635.8 25.0 %collective-permute-start.42 = (bf16[256,1024]{1,0:T(8,128)(2,1)S(1)}, bf16[256,1024]{1,0:T(8,128)(2,1)S(1)}, u32[]{:S(2)}, u32[]{:S(2)}) collective-permute-start(bf16[256,1024]{1,0:T(8,128)(2,1)S(1)} %get-tuple-element.233), channel_id=1, source_target_pairs={{0,8},{8,16},{16,24},{24,0},{1,9},{9,17},{17,25},{25,1},{2,10},{10... | collective-permute-start | bytes 1572872 | tf_op jit(solution)/shard_map/ppermute | solution.py:755
  636.7 44.1 %collective-permute-start.41 = (bf16[256,1024]{1,0:T(8,128)(2,1)S(1)}, bf16[256,1024]{1,0:T(8,128)(2,1)S(1)}, u32[]{:S(2)}, u32[]{:S(2)}) collective-permute-start(bf16[256,1024]{1,0:T(8,128)(2,1)S(1)} %get-tuple-element.234), channel_id=1, source_target_pairs={{0,16},{8,24},{16,0},{24,8},{1,17},{9,25},{17,1},{25,9},{2,18},{10... | collective-permute-start | bytes 1572872 | tf_op jit(solution)/shard_map/ppermute | solution.py:755
  (106 other events, 1065.8 us)
Sparse Core Ops, SparseCore 0:
  14.4 55.3 all-gather.3
  71.6 53.0 all-gather.5
  268.9 52.8 all-gather.7
  337.3 88.5 all-reduce.10
  465.8 168.3 all-reduce.12

commit v6 on v5

--- a/solution.py
+++ b/solution.py
@@ -822,8 +822,6 @@
         )
     )
     out_own = output_weight.reshape(inner, width_col)
-    in_other, out_other = other_col(in_own), other_col(out_own)
-
     column = lambda v: v.reshape(-1, 1)
     taps = jnp.concatenate(
         [
@@ -837,8 +835,19 @@
     )
     bc_taps = jnp.concatenate([conv_bc.T, column(conv_bc_bias), jnp.zeros((aux, 3), F32)], axis=1)
     dt_par = jnp.pad(jnp.stack([dt_bias, a_log], axis=1), ((0, steps - heads), (0, 6)))
-
-    targets_own = widened(targets)
+    targets_there = lax.dynamic_slice_in_dim(targets, (1 - col_index) * seq_col, seq_col, 0)
+    in_own, taps, bc_taps, dt_par, targets_there = tie(
+        (in_own, taps, bc_taps, dt_par, targets_there)
+    )
+    in_other, out_other = other_col(in_own), other_col(out_own)
+
+    targets_own = jnp.concatenate(
+        [
+            lax.dynamic_slice_in_dim(targets, col_index * seq_col, seq_col, 0),
+            other_col(targets_there),
+        ],
+        axis=2,
+    )
     positions = row_index * local_len + jnp.arange(local_len, dtype=jnp.int32)
 
     zx, gated, entering, kept_rows, scatters, gathers = [], [], [], [], [], []
@@ -948,11 +957,11 @@
     in_low = product(
         "tt", list(zip(scaled, g_late)), TILE, added=other_col(there), columns=width_col, wide=wide
     )
-    scatters[-1].second(in_low)
     w_zx = lax.psum(in_low, "dp")
     g_aux = [g[wide:] for g in g_in]
     g_aux[-1] = tie(g_aux[-1], in_low)
     aux_part = sum(matmul(scaled[i], g_aux[i], 0, 1) for i in range(seq_col))
+    scatters[-1].second(aux_part)
     aux_half = aux_part[:width_col] + other_col(aux_part[width_col:])
     aux_half = jnp.concatenate(
         [

time: 697 us -> 689 us (0.989)
    psum x1, waiting for transfers between devices: 41.9 us -> 29.3 us  [per_device(): w_zx = lax.psum(in_low, 'dp')]
    ppermute x6, waiting for transfers between devices: 52.3 us -> 61.3 us  [butterfly(): v = v + lax.ppermute(v, axis, [(i, i ^ bit) for i in range(count)])]
    unnamed x168 -> x172, local copies, waits for them, and re-layouts: 21.1 us -> 22.1 us
  transfers between devices with their start and end apart: 55 -> 55, of which waited for: 28 -> 27; matrix products, arithmetic and copies ran while one was open for 27% -> 28% of each run, Pallas kernels for 20% -> 20%
where the time goes in v6:
time: 689 us; the launch traced here: 685 us
  waiting for transfers between devices  249 us (36%)
  Pallas kernels  138 us (20%)
  matrix products  103 us (15%)
  other arithmetic  70.3 us (10%)
  local copies, waits for them, and re-layouts  57.9 us (8%)
  starting transfers between devices  47.1 us (7%)
  between operations  19.9 us (3%)
    dot_general x16, matrix products, matmul(): lax.dot_general(a, b, (((over_a,), (over_b,)), ((), ())), preferred_eleme...  103 us
    ppermute x27, waiting for transfers between devices, flip(): return lax.ppermute(v, 'row', [(i, i ^ bit) for i in range(4)])  65.5 us
    pallas_call x2, Pallas kernels, scan_backward(): pl.pallas_call(body, grid=(count,), in_specs=[pl.BlockSpec((2 * inner, sp...  61.5 us
    ppermute x6, waiting for transfers between devices, butterfly(): v = v + lax.ppermute(v, axis, [(i, i ^ bit) for i in range(count)])  61.3 us
    all_gather x3, waiting for transfers between devices, per_device(): spread = lambda v: lax.all_gather(v, 'row', axis=0, tiled=True)  49.8 us
    ppermute x6, waiting for transfers between devices, sent_back(): lax.ppermute(piece, 'dp', [(i, (i + hop) % groups) for i in range(groups)])  36.6 us
    pallas_call x2, Pallas kernels, scan_forward(): pl.pallas_call(body, grid=(length // span,), in_specs=[pl.BlockSpec((2 *...  33.3 us
    psum x1, waiting for transfers between devices, per_device(): w_zx = lax.psum(in_low, 'dp')  29.3 us
  transfers between devices with their start and end apart: 55, of which 27 were waited for; matrix products, arithmetic and copies ran while one was open for 28% of the time, Pallas kernels for 20%

profile of v6, /device:TPU:0, one launch (start us, length us, event | category | flops | bytes accessed | tf_op | source)
XLA Modules:
  0.0 684.7 jit_solution(15864769051111199537)
XLA Ops:
  15.0 6.7 copy.58
  29.7 40.1 %all-gather.4.cloned.1.call-done.refs_0_ = bf16[1024,2048]{1,0:T(8,128)(2,1)} async-done(((bf16[256,2048]{1,0:T(8,128)(2,1)}), bf16[1024,2048]{1,0:T(8,128)(2,1)}) %all-gather.4.cloned.1.call-update) | async-done | bytes 4194320 | tf_op jit(solution)/shard_map/all_gather | solution.py:808
  73.9 7.8 %fusion.18 = f32[2320,1024]{1,0:T(8,128)S(1)} fusion(bf16[1024,2320]{0,1:T(8,128)(2,1)} %pad_maximum_fusion, bf16[1024,2048]{1,0:T(8,128)(2,1)} %all-gather.4.cloned.1.call-done.refs_0_), kind=kOutput, calls=%fused_computation.47 | convolution fusion | flops 4865392640 | bytes 16351232 | tf_op jit(solution)/shard_map/dot_general | solution.py:770
  81.8 9.9 %convolution_add_fusion.1.zx_ref.bc_ref.dt_ref.bc_before_ref = f32[2320,1024]{1,0:T(8,128)} fusion(f32[2320,1024]{1,0:T(8,128)S(1)} %fusion.18, bf16[1024,2320]{0,1:T(8,128)(2,1)} %collective-permute-done.2, bf16[1024,2048]{1,0:T(8,128)(2,1)S(1)} %copy-done.6), kind=kOutput, calls=%fused_computation.2 | convolution fusion | flops 4867768320 | bytes 25853952 | tf_op jit(solution)/shard_map/dot_general | solution.py:770
  91.7 16.7 %scan_forward.2 = (bf16[1024,1024]{1,0:T(8,128)(2,1)}, f32[1,1024]{1,0:T(1,128)}, bf16[8192,128]{1,0:T(8,128)(2,1)}, f32[1024,1024]{1,0:T(8,128)}, f32[1024,1024]{1,0:T(8,128)}, /*index=5*/f32[1024,1024]{1,0:T(8,128)}) custom-call(f32[2320,1024]{1,0:T(8,128)} %convolution_add_fusion.1.zx_ref.bc_ref.dt_ref.bc_before_ref, ...), custom_call_target="tpu_custom_call" | custom-call | tf_op jit(solution)/shard_map/scan_forward/pallas_call | solution.py:350
  123.4 6.1 all-gather.6.cloned.1.call-done.refs_1_.refs_2_
  129.5 7.8 %fusion.23 = f32[2320,1024]{1,0:T(8,128)S(1)} fusion(bf16[1024,2320]{0,1:T(8,128)(2,1)} %pad_maximum_fusion, bf16[1024,2048]{1,0:T(8,128)(2,1)} %all-gather.6.cloned.1.call-done.refs_1_.refs_2_), kind=kOutput, calls=%fused_computation.71 | convolution fusion | flops 4865392640 | bytes 16351232 | tf_op jit(solution)/shard_map/dot_general | solution.py:770
  137.4 10.6 %convolution_add_fusion.zx_ref.bc_ref.dt_ref.bc_before_ref = f32[2320,1024]{1,0:T(8,128)} fusion(f32[2320,1024]{1,0:T(8,128)S(1)} %fusion.23, bf16[1024,2320]{0,1:T(8,128)(2,1)} %collective-permute-done.2, bf16[1024,2048]{1,0:T(8,128)(2,1)S(1)} %copy-done.8), kind=kOutput, calls=%fused_computation.1 | convolution fusion | flops 4867768320 | bytes 25853952 | tf_op jit(solution)/shard_map/dot_general | solution.py:770
  156.9 8.7 %collective-permute-done.7 = bf16[256,1024]{1,0:T(8,128)(2,1)S(1)} collective-permute-done((bf16[256,1024]{1,0:T(8,128)(2,1)S(1)}, bf16[256,1024]{1,0:T(8,128)(2,1)S(1)}, u32[]{:S(2)}, u32[]{:S(2)}) %collective-permute-start.7) | collective-permute-done | bytes 524320 | tf_op jit(solution)/shard_map/ppermute | solution.py:578
  177.7 16.6 %scan_forward.3 = (bf16[1024,1024]{1,0:T(8,128)(2,1)}, f32[1,1024]{1,0:T(1,128)}, bf16[8192,128]{1,0:T(8,128)(2,1)}, f32[1024,1024]{1,0:T(8,128)}, f32[1024,1024]{1,0:T(8,128)}, /*index=5*/f32[1024,1024]{1,0:T(8,128)}) custom-call(f32[2320,1024]{1,0:T(8,128)} %convolution_add_fusion.zx_ref.bc_ref.dt_ref.bc_before_ref, ...), custom_call_target="tpu_custom_call" | custom-call | tf_op jit(solution)/shard_map/scan_forward/pallas_call | solution.py:350
  216.9 5.2 collective-permute-done.11
  224.4 6.1 fusion.161.gn_ref
  230.6 12.4 %collective-permute-done.14 = bf16[2,256,1024]{2,1,0:T(8,128)(2,1)S(1)} collective-permute-done((bf16[2,256,1024]{2,1,0:T(8,128)(2,1)S(1)}, bf16[2,256,1024]{2,1,0:T(8,128)(2,1)S(1)}, u32[]{:S(2)}, u32[]{:S(2)}) %collective-permute-start.14) | collective-permute-done | bytes 1048608 | tf_op jit(solution)/shard_map/ppermute | solution.py:578
  245.5 6.7 fusion.162
  275.4 30.7 %scan_backward.2 = (bf16[2320,1024]{1,0:T(8,128)(2,1)}, f32[1024,8]{1,0:T(8,128)}, f32[256,8]{1,0:T(8,128)}, f32[16,128]{1,0:T(8,128)}) custom-call(f32[2320,1024]{1,0:T(8,128)} %convolution_add_fusion.1.zx_ref.bc_ref.dt_ref.bc_before_ref, f32[1024,1024]{1,0:T(8,128)} %get-tuple-element.92.x_ref, f32[1024,1024]{1,0:T(8,128)} %get-tuple-element.93.slope_ref, ...), custom_call_target="tpu_custom_call" | custom-call | tf_op jit(solution)/shard_map/scan_backward/pallas_call | solution.py:400
  315.2 8.6 %convolution_add_fusion.2 = f32[1024,2048]{1,0:T(8,128)S(1)} fusion(f32[1024,2048]{1,0:T(8,128)} %fusion.162, bf16[1024,1024]{1,0:T(8,128)(2,1)S(1)} %copy-done.80, bf16[1024,2048]{1,0:T(8,128)(2,1)} %all-gather.8.cloned.1.call-done), kind=kOutput, calls=%fused_computation.20 | convolution fusion | flops 4297064448 | bytes 23068672 | tf_op jit(solution)/shard_map/dot_general | solution.py:770
  330.6 8.9 %convolution_convert_fusion.1 = bf16[1024,1024]{1,0:T(8,128)(2,1)S(1)} fusion(bf16[2320,1024]{1,0:T(8,128)(2,1)} %get-tuple-element.134.refs_2_.refs_1_, bf16[1024,2320]{0,1:T(8,128)(2,1)} %pad_maximum_fusion), kind=kOutput, calls=%fused_computation.74 | convolution fusion | flops 4866441216 | bytes 11599872 | tf_op jit(solution)/shard_map/dot_general | solution.py:770
  339.6 9.7 %convolution_convert_fusion = bf16[1024,1024]{1,0:T(8,128)(2,1)S(1)} fusion(bf16[2320,1024]{1,0:T(8,128)(2,1)} %get-tuple-element.134.refs_2_.refs_1_, bf16[1024,2320]{0,1:T(8,128)(2,1)} %collective-permute-done.2), kind=kOutput, calls=%fused_computation.73 | convolution fusion | flops 4866441216 | bytes 11599872 | tf_op jit(solution)/shard_map/dot_general | solution.py:770
  352.3 6.1 fusion.163.gn_ref
  358.4 30.8 %scan_backward.3 = (bf16[2320,1024]{1,0:T(8,128)(2,1)}, f32[1024,8]{1,0:T(8,128)}, f32[256,8]{1,0:T(8,128)}, f32[16,128]{1,0:T(8,128)}) custom-call(f32[2320,1024]{1,0:T(8,128)} %convolution_add_fusion.zx_ref.bc_ref.dt_ref.bc_before_ref, f32[1024,1024]{1,0:T(8,128)} %get-tuple-element.121.x_ref, f32[1024,1024]{1,0:T(8,128)} %get-tuple-element.122.slope_ref, ...), custom_call_target="tpu_custom_call" | custom-call | tf_op jit(solution)/shard_map/scan_backward/pallas_call | solution.py:400
  393.8 27.7 %late_products.1 = (bf16[1024,2048]{1,0:T(8,128)(2,1)}, bf16[1024,1024]{1,0:T(8,128)(2,1)}, bf16[1024,1024]{1,0:T(8,128)(2,1)}) custom-call(bf16[1024,2048]{1,0:T(8,128)(2,1)} %all-gather.4.cloned.1.call-done.refs_0_, bf16[1024,2048]{1,0:T(8,128)(2,1)} %all-gather.6.cloned.1.call-done.refs_1_.refs_2_, bf16[2320,1024]{1,0:T(8,128)(2,1)} %get-tuple-element.134.refs_2_.refs_1_, ...), custom_call_target="tpu_custom_call" | custom-call | tf_op jit(solution)/shard_map/late_products/pallas_call | solution.py:532
  432.4 15.1 %product_tt.1 = bf16[1024,2048]{1,0:T(8,128)(2,1)} custom-call(bf16[1024,2048]{1,0:T(8,128)(2,1)} %all-gather.4.cloned.1.call-done.refs_0_, bf16[2320,1024]{1,0:T(8,128)(2,1)} %get-tuple-element.134.refs_2_.refs_1_, bf16[1024,2048]{1,0:T(8,128)(2,1)} %all-gather.6.cloned.1.call-done.refs_1_.refs_2_, bf16[2320,1024]{1,0:T(8,128)(2,1)} %get-tuple-element.151.refs_3_.refs_4_, ...), custom_call_target="tpu_custom_call" | custom-call | tf_op jit(solution)/shard_map/product_tt/pallas_call | solution.py:482
  465.0 7.8 %collective-permute-done.33 = bf16[256,1024]{1,0:T(8,128)(2,1)S(1)} collective-permute-done((bf16[256,1024]{1,0:T(8,128)(2,1)S(1)}, bf16[256,1024]{1,0:T(8,128)(2,1)S(1)}, u32[]{:S(2)}, u32[]{:S(2)}) %collective-permute-start.33) | collective-permute-done | bytes 524320 | tf_op jit(solution)/shard_map/ppermute | solution.py:578
  488.5 11.2 %collective-permute-done.44 = f32[512,320]{0,1:T(8,128)} collective-permute-done((f32[512,320]{0,1:T(8,128)}, f32[512,320]{0,1:T(8,128)}, u32[]{:S(2)}, u32[]{:S(2)}) %collective-permute-start.44) | collective-permute-done | bytes 655392 | tf_op jit(solution)/shard_map/ppermute | solution.py:578
  504.0 6.5 collective-permute-done.36
  515.9 24.2 %collective-permute-done.46 = f32[256,320]{0,1:T(8,128)S(1)} collective-permute-done((f32[256,320]{0,1:T(8,128)S(1)}, f32[256,320]{0,1:T(8,128)S(1)}, u32[]{:S(2)}, u32[]{:S(2)}) %collective-permute-start.46) | collective-permute-done | bytes 327712 | tf_op jit(solution)/shard_map/ppermute | solution.py:707
  545.7 29.8 %collective-permute-done.38 = f32[11297]{0:T(1024)S(1)} collective-permute-done((f32[11297]{0:T(1024)S(1)}, f32[11297]{0:T(1024)S(1)}, u32[]{:S(2)}, u32[]{:S(2)}) %collective-permute-start.38) | collective-permute-done | bytes 45220 | tf_op jit(solution)/shard_map/ppermute | solution.py:707
  589.1 6.7 collective-permute-done.49
  597.0 29.3 %all-reduce.13.cloned.1.call-done = bf16[1024,2048]{1,0:T(8,128)(2,1)} async-done(((bf16[1024,2048]{1,0:T(8,128)(2,1)}), bf16[1024,2048]{1,0:T(8,128)(2,1)}) %all-reduce.13.cloned.1.call-update) | async-done | bytes 4194320 | tf_op jit(solution)/shard_map/psum | solution.py:960
  630.8 5.4 copy.70
  636.2 17.4 %collective-permute-done.40 = bf16[256,1024]{1,0:T(8,128)(2,1)S(1)} collective-permute-done((bf16[256,1024]{1,0:T(8,128)(2,1)S(1)}, bf16[256,1024]{1,0:T(8,128)(2,1)S(1)}, u32[]{:S(2)}, u32[]{:S(2)}) %collective-permute-start.40) | collective-permute-done | bytes 524320 | tf_op jit(solution)/shard_map/ppermute | solution.py:755
  653.6 19.2 %collective-permute-done.41 = bf16[256,1024]{1,0:T(8,128)(2,1)S(1)} collective-permute-done((bf16[256,1024]{1,0:T(8,128)(2,1)S(1)}, bf16[256,1024]{1,0:T(8,128)(2,1)S(1)}, u32[]{:S(2)}, u32[]{:S(2)}) %collective-permute-start.41) | collective-permute-done | bytes 524320 | tf_op jit(solution)/shard_map/ppermute | solution.py:755
  (467 shorter events, 208.1 us)
Async XLA Ops:
  7.2 62.7 %all-gather.4.cloned.1.call-start = ((), (), s32[]{:S(2)}) async-start(), calls=%async_computation | async-start | bytes 5242880 | tf_op jit(solution)/shard_map/all_gather | solution.py:808
  14.4 115.1 %all-gather.6.cloned.1.call-start = ((), (), s32[]{:S(2)}) async-start(), calls=%async_computation.1 | async-start | bytes 5242880 | tf_op jit(solution)/shard_map/all_gather | solution.py:808
  29.3 52.4 %collective-permute-start.2 = (bf16[1024,2320]{0,1:T(8,128)(2,1)}, bf16[1024,2320]{0,1:T(8,128)(2,1)}, u32[]{:S(2)}, u32[]{:S(2)}) collective-permute-start(bf16[1024,2320]{0,1:T(8,128)(2,1)} %pad_maximum_fusion), channel_id=1, source_target_pairs={{0,1},{1,0},{2,3},{3,2},{4,5},{5,4},{6,7},{7,6},{8,9},{9,8},{10,11... | collective-permute-start | bytes 14254088 | tf_op jit(solution)/shard_map/ppermute | solution.py:737
  69.9 245.3 %all-gather.8.cloned.1.call-start = ((), (), s32[]{:S(2)}) async-start(), calls=%async_computation.2 | async-start | bytes 5242880 | tf_op jit(solution)/shard_map/all_gather | solution.py:808
  70.1 40.1 %collective-permute-start.3 = (bf16[1024,1024]{1,0:T(8,128)(2,1)}, bf16[1024,1024]{1,0:T(8,128)(2,1)}, u32[]{:S(2)}, u32[]{:S(2)}) collective-permute-start(bf16[1024,1024]{1,0:T(8,128)(2,1)} %bitcast.345), channel_id=1, source_target_pairs={{0,1},{1,0},{2,3},{3,2},{4,5},{5,4},{6,7},{7,6},{8,9},{9,8},{10,11... | collective-permute-start | bytes 6291464 | tf_op jit(solution)/shard_map/ppermute | solution.py:737
  70.2 99.0 %collective-permute-start.8 = (bf16[2,256,1024]{2,1,0:T(8,128)(2,1)}, bf16[2,256,1024]{2,1,0:T(8,128)(2,1)}, u32[]{:S(2)}, u32[]{:S(2)}) collective-permute-start(bf16[2,256,1024]{2,1,0:T(8,128)(2,1)} %get-tuple-element.105), channel_id=1, source_target_pairs={{0,1},{1,0},{2,3},{3,2},{4,5},{5,4},{6,7},{7,6},{8,9},{9,8},{10,11... | collective-permute-start | bytes 3145736 | tf_op jit(solution)/shard_map/ppermute | solution.py:737
  116.1 31.9 %collective-permute-start.5 = (bf16[2,256,1024]{2,1,0:T(8,128)(2,1)}, bf16[2,256,1024]{2,1,0:T(8,128)(2,1)}, u32[]{:S(2)}, u32[]{:S(2)}) collective-permute-start(bf16[2,256,1024]{2,1,0:T(8,128)(2,1)} %dynamic-slice_bitcast_fusion.6), channel_id=1, source_target_pairs={{0,4},{2,6},{4,0},{6,2},{1,5},{3,7},{5,1},{7,3},{8,12},{10,14},{12... | collective-permute-start | bytes 3145736 | tf_op jit(solution)/shard_map/ppermute | solution.py:578
  121.9 26.9 %collective-permute-start.4 = (bf16[2,272,1024]{2,1,0:T(8,128)(2,1)}, bf16[2,272,1024]{2,1,0:T(8,128)(2,1)}, u32[]{:S(2)}, u32[]{:S(2)}) collective-permute-start(bf16[2,272,1024]{2,1,0:T(8,128)(2,1)} %maximum_maximum_fusion), channel_id=1, source_target_pairs={{0,2},{2,0},{4,6},{6,4},{1,3},{3,1},{5,7},{7,5},{8,10},{10,8},{12,... | collective-permute-start | bytes 3342344 | tf_op jit(solution)/shard_map/ppermute | solution.py:578
  175.7 29.0 %collective-permute-start.10 = (bf16[272,2048]{1,0:T(8,128)(2,1)}, bf16[272,2048]{1,0:T(8,128)(2,1)}, u32[]{:S(2)}, u32[]{:S(2)}) collective-permute-start(bf16[272,2048]{1,0:T(8,128)(2,1)} %pad_maximum_fusion.6), channel_id=1, source_target_pairs={{0,4},{2,6},{4,0},{6,2},{1,5},{3,7},{5,1},{7,3},{8,12},{10,14},{12... | collective-permute-start | bytes 3342344 | tf_op jit(solution)/shard_map/ppermute | solution.py:578
  176.5 28.2 %collective-permute-start.9 = (bf16[272,2048]{1,0:T(8,128)(2,1)}, bf16[272,2048]{1,0:T(8,128)(2,1)}, u32[]{:S(2)}, u32[]{:S(2)}) collective-permute-start(bf16[272,2048]{1,0:T(8,128)(2,1)} %pad_maximum_fusion.6), channel_id=1, source_target_pairs={{0,2},{2,0},{4,6},{6,4},{1,3},{3,1},{5,7},{7,5},{8,10},{10,8},{12,... | collective-permute-start | bytes 3342344 | tf_op jit(solution)/shard_map/ppermute | solution.py:578
  209.2 33.8 %collective-permute-start.14 = (bf16[2,256,1024]{2,1,0:T(8,128)(2,1)S(1)}, bf16[2,256,1024]{2,1,0:T(8,128)(2,1)S(1)}, u32[]{:S(2)}, u32[]{:S(2)}) collective-permute-start(bf16[2,256,1024]{2,1,0:T(8,128)(2,1)S(1)} %dynamic-slice_bitcast_fusion.4), channel_id=1, source_target_pairs={{0,4},{2,6},{4,0},{6,2},{1,5},{3,7},{5,1},{7,3},{8,12},{10,14},{12... | collective-permute-start | bytes 3145736 | tf_op jit(solution)/shard_map/ppermute | solution.py:578
  210.1 32.9 %collective-permute-start.13 = (bf16[2,272,1024]{2,1,0:T(8,128)(2,1)S(1)}, bf16[2,272,1024]{2,1,0:T(8,128)(2,1)S(1)}, u32[]{:S(2)}, u32[]{:S(2)}) collective-permute-start(bf16[2,272,1024]{2,1,0:T(8,128)(2,1)S(1)} %maximum_maximum_fusion.1), channel_id=1, source_target_pairs={{0,2},{2,0},{4,6},{6,4},{1,3},{3,1},{5,7},{7,5},{8,10},{10,8},{12,... | collective-permute-start | bytes 3342344 | tf_op jit(solution)/shard_map/ppermute | solution.py:578
  262.2 160.2 %all-reduce.11.cloned.1.call-start = ((), (), s32[]{:S(2)}) async-start(), calls=%async_computation.3 | async-start | bytes 4194304 | tf_op jit(solution)/shard_map/psum | solution.py:932
  266.7 40.6 %collective-permute-start.21 = (f32[1,1024]{1,0:T(1,128)S(1)}, f32[1,1024]{1,0:T(1,128)S(1)}, u32[]{:S(2)}, u32[]{:S(2)}) collective-permute-start(f32[1,1024]{1,0:T(1,128)S(1)} %get-tuple-element.223), channel_id=1, source_target_pairs={{0,2},{2,0},{4,6},{6,4},{1,3},{3,1},{5,7},{7,5},{8,10},{10,8},{12,... | collective-permute-start | bytes 12296 | tf_op jit(solution)/shard_map/ppermute | solution.py:578
  269.4 42.2 %collective-permute-start.18 = (bf16[256,1024]{1,0:T(8,128)(2,1)S(1)}, bf16[256,1024]{1,0:T(8,128)(2,1)}, u32[]{:S(2)}, u32[]{:S(2)}) collective-permute-start(bf16[256,1024]{1,0:T(8,128)(2,1)S(1)} %get-tuple-element.248), channel_id=1, source_target_pairs={{0,8},{8,16},{16,24},{24,0},{1,9},{9,17},{17,25},{25,1},{2,10},{10... | collective-permute-start | bytes 1572872 | tf_op jit(solution)/shard_map/ppermute | solution.py:755
  271.0 40.6 %collective-permute-start.19 = (bf16[256,1024]{1,0:T(8,128)(2,1)S(1)}, bf16[256,1024]{1,0:T(8,128)(2,1)}, u32[]{:S(2)}, u32[]{:S(2)}) collective-permute-start(bf16[256,1024]{1,0:T(8,128)(2,1)S(1)} %get-tuple-element.249), channel_id=1, source_target_pairs={{0,16},{8,24},{16,0},{24,8},{1,17},{9,25},{17,1},{25,9},{2,18},{10... | collective-permute-start | bytes 1572872 | tf_op jit(solution)/shard_map/ppermute | solution.py:755
  273.3 38.3 %collective-permute-start.20 = (bf16[256,1024]{1,0:T(8,128)(2,1)S(1)}, bf16[256,1024]{1,0:T(8,128)(2,1)}, u32[]{:S(2)}, u32[]{:S(2)}) collective-permute-start(bf16[256,1024]{1,0:T(8,128)(2,1)S(1)} %get-tuple-element.250), channel_id=1, source_target_pairs={{0,24},{8,0},{16,8},{24,16},{1,25},{9,1},{17,9},{25,17},{2,26},{10... | collective-permute-start | bytes 1572872 | tf_op jit(solution)/shard_map/ppermute | solution.py:755
  330.6 295.8 %all-reduce.13.cloned.1.call-start = ((), (), s32[]{:S(2)}) async-start(), calls=%async_computation.4 | async-start | bytes 8388608 | tf_op jit(solution)/shard_map/psum | solution.py:960
  349.4 39.8 %collective-permute-start.26 = (bf16[2,256,1024]{2,1,0:T(8,128)(2,1)S(1)}, bf16[2,256,1024]{2,1,0:T(8,128)(2,1)}, u32[]{:S(2)}, u32[]{:S(2)}) collective-permute-start(bf16[2,256,1024]{2,1,0:T(8,128)(2,1)S(1)} %dynamic-slice_bitcast_fusion.2), channel_id=1, source_target_pairs={{0,4},{2,6},{4,0},{6,2},{1,5},{3,7},{5,1},{7,3},{8,12},{10,14},{12... | collective-permute-start | bytes 3145736 | tf_op jit(solution)/shard_map/ppermute | solution.py:578
  350.9 38.2 %collective-permute-start.25 = (bf16[2,256,1024]{2,1,0:T(8,128)(2,1)S(1)}, bf16[2,256,1024]{2,1,0:T(8,128)(2,1)}, u32[]{:S(2)}, u32[]{:S(2)}) collective-permute-start(bf16[2,256,1024]{2,1,0:T(8,128)(2,1)S(1)} %dynamic-slice_bitcast_fusion.3), channel_id=1, source_target_pairs={{0,2},{2,0},{4,6},{6,4},{1,3},{3,1},{5,7},{7,5},{8,10},{10,8},{12,... | collective-permute-start | bytes 3145736 | tf_op jit(solution)/shard_map/ppermute | solution.py:578
  391.7 29.9 %collective-permute-start.28 = (bf16[256,1024]{1,0:T(8,128)(2,1)S(1)}, bf16[256,1024]{1,0:T(8,128)(2,1)S(1)}, u32[]{:S(2)}, u32[]{:S(2)}) collective-permute-start(bf16[256,1024]{1,0:T(8,128)(2,1)S(1)} %fusion.36), channel_id=1, source_target_pairs={{0,2},{2,0},{4,6},{6,4},{1,3},{3,1},{5,7},{7,5},{8,10},{10,8},{12,... | collective-permute-start | bytes 1572872 | tf_op jit(solution)/shard_map/ppermute | solution.py:578
  393.2 29.2 %collective-permute-start.27 = (bf16[256,1024]{1,0:T(8,128)(2,1)S(1)}, bf16[256,1024]{1,0:T(8,128)(2,1)}, u32[]{:S(2)}, u32[]{:S(2)}) collective-permute-start(bf16[256,1024]{1,0:T(8,128)(2,1)S(1)} %fusion.37), channel_id=1, source_target_pairs={{0,4},{2,6},{4,0},{6,2},{1,5},{3,7},{5,1},{7,3},{8,12},{10,14},{12... | collective-permute-start | bytes 1572872 | tf_op jit(solution)/shard_map/ppermute | solution.py:578
  427.3 28.9 %collective-permute-start.30 = (bf16[2,256,1024]{2,1,0:T(8,128)(2,1)}, bf16[2,256,1024]{2,1,0:T(8,128)(2,1)}, u32[]{:S(2)}, u32[]{:S(2)}) collective-permute-start(bf16[2,256,1024]{2,1,0:T(8,128)(2,1)} %dynamic-slice_bitcast_fusion.1), channel_id=1, source_target_pairs={{0,2},{2,0},{4,6},{6,4},{1,3},{3,1},{5,7},{7,5},{8,10},{10,8},{12,... | collective-permute-start | bytes 3145736 | tf_op jit(solution)/shard_map/ppermute | solution.py:578
  429.7 26.5 %collective-permute-start.31 = (bf16[2,256,1024]{2,1,0:T(8,128)(2,1)}, bf16[2,256,1024]{2,1,0:T(8,128)(2,1)}, u32[]{:S(2)}, u32[]{:S(2)}) collective-permute-start(bf16[2,256,1024]{2,1,0:T(8,128)(2,1)} %dynamic-slice_bitcast_fusion), channel_id=1, source_target_pairs={{0,4},{2,6},{4,0},{6,2},{1,5},{3,7},{5,1},{7,3},{8,12},{10,14},{12... | collective-permute-start | bytes 3145736 | tf_op jit(solution)/shard_map/ppermute | solution.py:578
  510.6 29.5 %collective-permute-start.46 = (f32[256,320]{0,1:T(8,128)S(1)}, f32[256,320]{0,1:T(8,128)S(1)}, u32[]{:S(2)}, u32[]{:S(2)}) collective-permute-start(f32[256,320]{0,1:T(8,128)S(1)} %dynamic-slice_add_fusion), channel_id=1, source_target_pairs={{0,8},{8,0},{16,24},{24,16},{1,9},{9,1},{17,25},{25,17},{2,10},{10... | collective-permute-start | bytes 983048 | tf_op jit(solution)/shard_map/ppermute | solution.py:707
  514.8 26.2 %collective-permute-start.37 = (f32[11297]{0:T(1024)S(1)}, f32[11297]{0:T(1024)S(1)}, u32[]{:S(2)}, u32[]{:S(2)}) collective-permute-start(f32[11297]{0:T(1024)S(1)} %pad_maximum_fusion.16), channel_id=1, source_target_pairs={{0,8},{8,0},{16,24},{24,16},{1,9},{9,1},{17,25},{25,17},{2,10},{10... | collective-permute-start | bytes 135572 | tf_op jit(solution)/shard_map/ppermute | solution.py:707
  515.9 71.5 %collective-permute-start.39 = (bf16[2,256,1024]{2,1,0:T(8,128)(2,1)}, bf16[2,256,1024]{2,1,0:T(8,128)(2,1)}, u32[]{:S(2)}, u32[]{:S(2)}) collective-permute-start(bf16[2,256,1024]{2,1,0:T(8,128)(2,1)} %pad_maximum_fusion.12), channel_id=1, source_target_pairs={{0,1},{1,0},{2,3},{3,2},{4,5},{5,4},{6,7},{7,6},{8,9},{9,8},{10,11... | collective-permute-start | bytes 3145736 | tf_op jit(solution)/shard_map/ppermute | solution.py:737
  540.2 37.6 %collective-permute-start.47 = (f32[256,320]{0,1:T(8,128)S(1)}, f32[256,320]{0,1:T(8,128)S(1)}, u32[]{:S(2)}, u32[]{:S(2)}) collective-permute-start(f32[256,320]{0,1:T(8,128)S(1)} %add.767), channel_id=1, source_target_pairs={{0,16},{8,24},{16,0},{24,8},{1,17},{9,25},{17,1},{25,9},{2,18},{10... | collective-permute-start | bytes 983048 | tf_op jit(solution)/shard_map/ppermute | solution.py:707
  541.2 34.4 %collective-permute-start.38 = (f32[11297]{0:T(1024)S(1)}, f32[11297]{0:T(1024)S(1)}, u32[]{:S(2)}, u32[]{:S(2)}) collective-permute-start(f32[11297]{0:T(1024)S(1)} %fusion.192), channel_id=1, source_target_pairs={{0,16},{8,24},{16,0},{24,8},{1,17},{9,25},{17,1},{25,9},{2,18},{10... | collective-permute-start | bytes 135572 | tf_op jit(solution)/shard_map/ppermute | solution.py:707
  626.6 27.0 %collective-permute-start.40 = (bf16[256,1024]{1,0:T(8,128)(2,1)S(1)}, bf16[256,1024]{1,0:T(8,128)(2,1)S(1)}, u32[]{:S(2)}, u32[]{:S(2)}) collective-permute-start(bf16[256,1024]{1,0:T(8,128)(2,1)S(1)} %get-tuple-element.241), channel_id=1, source_target_pairs={{0,24},{8,0},{16,8},{24,16},{1,25},{9,1},{17,9},{25,17},{2,26},{10... | collective-permute-start | bytes 1572872 | tf_op jit(solution)/shard_map/ppermute | solution.py:755
  628.7 24.9 %collective-permute-start.42 = (bf16[256,1024]{1,0:T(8,128)(2,1)S(1)}, bf16[256,1024]{1,0:T(8,128)(2,1)S(1)}, u32[]{:S(2)}, u32[]{:S(2)}) collective-permute-start(bf16[256,1024]{1,0:T(8,128)(2,1)S(1)} %get-tuple-element.243), channel_id=1, source_target_pairs={{0,8},{8,16},{16,24},{24,0},{1,9},{9,17},{17,25},{25,1},{2,10},{10... | collective-permute-start | bytes 1572872 | tf_op jit(solution)/shard_map/ppermute | solution.py:755
  629.0 43.7 %collective-permute-start.41 = (bf16[256,1024]{1,0:T(8,128)(2,1)S(1)}, bf16[256,1024]{1,0:T(8,128)(2,1)S(1)}, u32[]{:S(2)}, u32[]{:S(2)}) collective-permute-start(bf16[256,1024]{1,0:T(8,128)(2,1)S(1)} %get-tuple-element.244), channel_id=1, source_target_pairs={{0,16},{8,24},{16,0},{24,8},{1,17},{9,25},{17,1},{25,9},{2,18},{10... | collective-permute-start | bytes 1572872 | tf_op jit(solution)/shard_map/ppermute | solution.py:755
  (108 other events, 1250.1 us)
Sparse Core Ops, SparseCore 0:
  14.5 55.3 all-gather.3
  71.7 57.7 all-gather.5
  262.3 52.8 all-gather.7
  330.7 88.2 all-reduce.10
  456.4 169.9 all-reduce.12

commit v7 on v6

--- a/solution.py
+++ b/solution.py
@@ -907,7 +907,7 @@
         coef.append(c)
     early = []
     if seq_col > 1:
-        early = [matmul(out_weight, g_rows[0], 1, 1), matmul(gated[0], g_rows[0], 1, 0)]
+        early = [matmul(out_weight, g_rows[0], 1, 1).astype(BF), matmul(gated[0], g_rows[0], 1, 0)]
     finish(seq_col - 1, *early)
 
     to_rows = lambda g: Scatter(*(matmul(g, w, 0, 1).astype(BF) for w in (in_own, in_other)))
@@ -921,7 +921,7 @@
             gn, w_out_part = early
         else:
             w_out_part = w_out_part + matmul(gated[k], whole, 1, 0)
-            gn = matmul(out_weight, tie(whole, w_out_part) if final else whole, 1, 1)
+            gn = matmul(out_weight, tie(whole, w_out_part) if final else whole, 1, 1).astype(BF)
         before = (w_out_part,)
         if k == 0:
             dealt_output = dealt_rows(result)

time: 689 us -> 688 us (level)
  no operation moved by 1% of the time
where the time goes in v7:
time: 688 us; the launch traced here: 684 us
  waiting for transfers between devices  249 us (36%)
  Pallas kernels  138 us (20%)
  matrix products  102 us (15%)
  other arithmetic  70.4 us (10%)
  local copies, waits for them, and re-layouts  57.7 us (8%)
  starting transfers between devices  47.1 us (7%)
  between operations  20 us (3%)
    dot_general x16, matrix products, matmul(): lax.dot_general(a, b, (((over_a,), (over_b,)), ((), ())), preferred_eleme...  102 us
    ppermute x27, waiting for transfers between devices, flip(): return lax.ppermute(v, 'row', [(i, i ^ bit) for i in range(4)])  65.9 us
    pallas_call x2, Pallas kernels, scan_backward(): pl.pallas_call(body, grid=(count,), in_specs=[pl.BlockSpec((2 * inner, sp...  61.4 us
    ppermute x6, waiting for transfers between devices, butterfly(): v = v + lax.ppermute(v, axis, [(i, i ^ bit) for i in range(count)])  61.3 us
    all_gather x3, waiting for transfers between devices, per_device(): spread = lambda v: lax.all_gather(v, 'row', axis=0, tiled=True)  49.7 us
    ppermute x6, waiting for transfers between devices, sent_back(): lax.ppermute(piece, 'dp', [(i, (i + hop) % groups) for i in range(groups)])  36.6 us
    pallas_call x2, Pallas kernels, scan_forward(): pl.pallas_call(body, grid=(length // span,), in_specs=[pl.BlockSpec((2 *...  33.3 us
    psum x1, waiting for transfers between devices, per_device(): w_zx = lax.psum(in_low, 'dp')  29.3 us
  transfers between devices with their start and end apart: 55, of which 27 were waited for; matrix products, arithmetic and copies ran while one was open for 28% of the time, Pallas kernels for 20%

profile of v7, /device:TPU:0, one launch (start us, length us, event | category | flops | bytes accessed | tf_op | source)
XLA Modules:
  0.0 683.7 jit_solution(12897923483736684174)
XLA Ops:
  14.9 6.7 copy.58
  29.7 40.2 %all-gather.4.cloned.1.call-done.refs_0_ = bf16[1024,2048]{1,0:T(8,128)(2,1)} async-done(((bf16[256,2048]{1,0:T(8,128)(2,1)}), bf16[1024,2048]{1,0:T(8,128)(2,1)}) %all-gather.4.cloned.1.call-update) | async-done | bytes 4194320 | tf_op jit(solution)/shard_map/all_gather | solution.py:808
  73.9 7.8 %fusion.18 = f32[2320,1024]{1,0:T(8,128)S(1)} fusion(bf16[1024,2320]{0,1:T(8,128)(2,1)} %pad_maximum_fusion, bf16[1024,2048]{1,0:T(8,128)(2,1)} %all-gather.4.cloned.1.call-done.refs_0_), kind=kOutput, calls=%fused_computation.47 | convolution fusion | flops 4865392640 | bytes 16351232 | tf_op jit(solution)/shard_map/dot_general | solution.py:770
  81.8 9.9 %convolution_add_fusion.1.zx_ref.bc_ref.dt_ref.bc_before_ref = f32[2320,1024]{1,0:T(8,128)} fusion(f32[2320,1024]{1,0:T(8,128)S(1)} %fusion.18, bf16[1024,2320]{0,1:T(8,128)(2,1)} %collective-permute-done.2, bf16[1024,2048]{1,0:T(8,128)(2,1)S(1)} %copy-done.6), kind=kOutput, calls=%fused_computation.2 | convolution fusion | flops 4867768320 | bytes 25853952 | tf_op jit(solution)/shard_map/dot_general | solution.py:770
  91.7 16.7 %scan_forward.2 = (bf16[1024,1024]{1,0:T(8,128)(2,1)}, f32[1,1024]{1,0:T(1,128)}, bf16[8192,128]{1,0:T(8,128)(2,1)}, f32[1024,1024]{1,0:T(8,128)}, f32[1024,1024]{1,0:T(8,128)}, /*index=5*/f32[1024,1024]{1,0:T(8,128)}) custom-call(f32[2320,1024]{1,0:T(8,128)} %convolution_add_fusion.1.zx_ref.bc_ref.dt_ref.bc_before_ref, ...), custom_call_target="tpu_custom_call" | custom-call | tf_op jit(solution)/shard_map/scan_forward/pallas_call | solution.py:350
  123.4 6.0 all-gather.6.cloned.1.call-done.refs_1_.refs_2_
  129.4 7.8 %fusion.23 = f32[2320,1024]{1,0:T(8,128)S(1)} fusion(bf16[1024,2320]{0,1:T(8,128)(2,1)} %pad_maximum_fusion, bf16[1024,2048]{1,0:T(8,128)(2,1)} %all-gather.6.cloned.1.call-done.refs_1_.refs_2_), kind=kOutput, calls=%fused_computation.71 | convolution fusion | flops 4865392640 | bytes 16351232 | tf_op jit(solution)/shard_map/dot_general | solution.py:770
  137.2 10.6 %convolution_add_fusion.zx_ref.bc_ref.dt_ref.bc_before_ref = f32[2320,1024]{1,0:T(8,128)} fusion(f32[2320,1024]{1,0:T(8,128)S(1)} %fusion.23, bf16[1024,2320]{0,1:T(8,128)(2,1)} %collective-permute-done.2, bf16[1024,2048]{1,0:T(8,128)(2,1)S(1)} %copy-done.8), kind=kOutput, calls=%fused_computation.1 | convolution fusion | flops 4867768320 | bytes 25853952 | tf_op jit(solution)/shard_map/dot_general | solution.py:770
  156.8 8.7 %collective-permute-done.7 = bf16[256,1024]{1,0:T(8,128)(2,1)S(1)} collective-permute-done((bf16[256,1024]{1,0:T(8,128)(2,1)S(1)}, bf16[256,1024]{1,0:T(8,128)(2,1)S(1)}, u32[]{:S(2)}, u32[]{:S(2)}) %collective-permute-start.7) | collective-permute-done | bytes 524320 | tf_op jit(solution)/shard_map/ppermute | solution.py:578
  177.7 16.6 %scan_forward.3 = (bf16[1024,1024]{1,0:T(8,128)(2,1)}, f32[1,1024]{1,0:T(1,128)}, bf16[8192,128]{1,0:T(8,128)(2,1)}, f32[1024,1024]{1,0:T(8,128)}, f32[1024,1024]{1,0:T(8,128)}, /*index=5*/f32[1024,1024]{1,0:T(8,128)}) custom-call(f32[2320,1024]{1,0:T(8,128)} %convolution_add_fusion.zx_ref.bc_ref.dt_ref.bc_before_ref, ...), custom_call_target="tpu_custom_call" | custom-call | tf_op jit(solution)/shard_map/scan_forward/pallas_call | solution.py:350
  216.9 5.2 collective-permute-done.11
  224.5 5.8 convolution_convert_fusion.3.gn_ref
  230.3 12.8 %collective-permute-done.14 = bf16[2,256,1024]{2,1,0:T(8,128)(2,1)S(1)} collective-permute-done((bf16[2,256,1024]{2,1,0:T(8,128)(2,1)S(1)}, bf16[2,256,1024]{2,1,0:T(8,128)(2,1)S(1)}, u32[]{:S(2)}, u32[]{:S(2)}) %collective-permute-start.14) | collective-permute-done | bytes 1048608 | tf_op jit(solution)/shard_map/ppermute | solution.py:578
  245.5 6.7 fusion.161
  275.4 30.8 %scan_backward.2 = (bf16[2320,1024]{1,0:T(8,128)(2,1)}, f32[1024,8]{1,0:T(8,128)}, f32[256,8]{1,0:T(8,128)}, f32[16,128]{1,0:T(8,128)}) custom-call(f32[2320,1024]{1,0:T(8,128)} %convolution_add_fusion.1.zx_ref.bc_ref.dt_ref.bc_before_ref, f32[1024,1024]{1,0:T(8,128)} %get-tuple-element.92.x_ref, f32[1024,1024]{1,0:T(8,128)} %get-tuple-element.93.slope_ref, ...), custom_call_target="tpu_custom_call" | custom-call | tf_op jit(solution)/shard_map/scan_backward/pallas_call | solution.py:400
  315.1 8.2 %convolution_add_fusion.2 = f32[1024,2048]{1,0:T(8,128)S(1)} fusion(f32[1024,2048]{1,0:T(8,128)} %fusion.161, bf16[1024,1024]{1,0:T(8,128)(2,1)S(1)} %copy-done.80, bf16[1024,2048]{1,0:T(8,128)(2,1)} %all-gather.8.cloned.1.call-done), kind=kOutput, calls=%fused_computation.20 | convolution fusion | flops 4297064448 | bytes 23068672 | tf_op jit(solution)/shard_map/dot_general | solution.py:770
  330.1 8.9 %convolution_convert_fusion.1 = bf16[1024,1024]{1,0:T(8,128)(2,1)S(1)} fusion(bf16[2320,1024]{1,0:T(8,128)(2,1)} %get-tuple-element.134.refs_2_.refs_1_, bf16[1024,2320]{0,1:T(8,128)(2,1)} %pad_maximum_fusion), kind=kOutput, calls=%fused_computation.74 | convolution fusion | flops 4866441216 | bytes 11599872 | tf_op jit(solution)/shard_map/dot_general | solution.py:770
  339.1 9.7 %convolution_convert_fusion = bf16[1024,1024]{1,0:T(8,128)(2,1)S(1)} fusion(bf16[2320,1024]{1,0:T(8,128)(2,1)} %get-tuple-element.134.refs_2_.refs_1_, bf16[1024,2320]{0,1:T(8,128)(2,1)} %collective-permute-done.2), kind=kOutput, calls=%fused_computation.73 | convolution fusion | flops 4866441216 | bytes 11599872 | tf_op jit(solution)/shard_map/dot_general | solution.py:770
  351.8 5.7 convolution_convert_fusion.2.gn_ref
  357.5 30.6 %scan_backward.3 = (bf16[2320,1024]{1,0:T(8,128)(2,1)}, f32[1024,8]{1,0:T(8,128)}, f32[256,8]{1,0:T(8,128)}, f32[16,128]{1,0:T(8,128)}) custom-call(f32[2320,1024]{1,0:T(8,128)} %convolution_add_fusion.zx_ref.bc_ref.dt_ref.bc_before_ref, f32[1024,1024]{1,0:T(8,128)} %get-tuple-element.121.x_ref, f32[1024,1024]{1,0:T(8,128)} %get-tuple-element.122.slope_ref, ...), custom_call_target="tpu_custom_call" | custom-call | tf_op jit(solution)/shard_map/scan_backward/pallas_call | solution.py:400
  392.8 27.7 %late_products.1 = (bf16[1024,2048]{1,0:T(8,128)(2,1)}, bf16[1024,1024]{1,0:T(8,128)(2,1)}, bf16[1024,1024]{1,0:T(8,128)(2,1)}) custom-call(bf16[1024,2048]{1,0:T(8,128)(2,1)} %all-gather.4.cloned.1.call-done.refs_0_, bf16[1024,2048]{1,0:T(8,128)(2,1)} %all-gather.6.cloned.1.call-done.refs_1_.refs_2_, bf16[2320,1024]{1,0:T(8,128)(2,1)} %get-tuple-element.134.refs_2_.refs_1_, ...), custom_call_target="tpu_custom_call" | custom-call | tf_op jit(solution)/shard_map/late_products/pallas_call | solution.py:532
  431.4 15.1 %product_tt.1 = bf16[1024,2048]{1,0:T(8,128)(2,1)} custom-call(bf16[1024,2048]{1,0:T(8,128)(2,1)} %all-gather.4.cloned.1.call-done.refs_0_, bf16[2320,1024]{1,0:T(8,128)(2,1)} %get-tuple-element.134.refs_2_.refs_1_, bf16[1024,2048]{1,0:T(8,128)(2,1)} %all-gather.6.cloned.1.call-done.refs_1_.refs_2_, bf16[2320,1024]{1,0:T(8,128)(2,1)} %get-tuple-element.151.refs_3_.refs_4_, ...), custom_call_target="tpu_custom_call" | custom-call | tf_op jit(solution)/shard_map/product_tt/pallas_call | solution.py:482
  463.9 7.8 %collective-permute-done.33 = bf16[256,1024]{1,0:T(8,128)(2,1)S(1)} collective-permute-done((bf16[256,1024]{1,0:T(8,128)(2,1)S(1)}, bf16[256,1024]{1,0:T(8,128)(2,1)S(1)}, u32[]{:S(2)}, u32[]{:S(2)}) %collective-permute-start.33) | collective-permute-done | bytes 524320 | tf_op jit(solution)/shard_map/ppermute | solution.py:578
  487.5 11.2 %collective-permute-done.44 = f32[512,320]{0,1:T(8,128)} collective-permute-done((f32[512,320]{0,1:T(8,128)}, f32[512,320]{0,1:T(8,128)}, u32[]{:S(2)}, u32[]{:S(2)}) %collective-permute-start.44) | collective-permute-done | bytes 655392 | tf_op jit(solution)/shard_map/ppermute | solution.py:578
  503.0 6.5 collective-permute-done.36
  515.0 24.2 %collective-permute-done.46 = f32[256,320]{0,1:T(8,128)S(1)} collective-permute-done((f32[256,320]{0,1:T(8,128)S(1)}, f32[256,320]{0,1:T(8,128)S(1)}, u32[]{:S(2)}, u32[]{:S(2)}) %collective-permute-start.46) | collective-permute-done | bytes 327712 | tf_op jit(solution)/shard_map/ppermute | solution.py:707
  544.8 29.9 %collective-permute-done.38 = f32[11297]{0:T(1024)S(1)} collective-permute-done((f32[11297]{0:T(1024)S(1)}, f32[11297]{0:T(1024)S(1)}, u32[]{:S(2)}, u32[]{:S(2)}) %collective-permute-start.38) | collective-permute-done | bytes 45220 | tf_op jit(solution)/shard_map/ppermute | solution.py:707
  588.2 6.6 collective-permute-done.49
  596.1 29.3 %all-reduce.13.cloned.1.call-done = bf16[1024,2048]{1,0:T(8,128)(2,1)} async-done(((bf16[1024,2048]{1,0:T(8,128)(2,1)}), bf16[1024,2048]{1,0:T(8,128)(2,1)}) %all-reduce.13.cloned.1.call-update) | async-done | bytes 4194320 | tf_op jit(solution)/shard_map/psum | solution.py:960
  629.8 5.4 copy.70
  635.2 17.5 %collective-permute-done.40 = bf16[256,1024]{1,0:T(8,128)(2,1)S(1)} collective-permute-done((bf16[256,1024]{1,0:T(8,128)(2,1)S(1)}, bf16[256,1024]{1,0:T(8,128)(2,1)S(1)}, u32[]{:S(2)}, u32[]{:S(2)}) %collective-permute-start.40) | collective-permute-done | bytes 524320 | tf_op jit(solution)/shard_map/ppermute | solution.py:755
  652.7 19.1 %collective-permute-done.41 = bf16[256,1024]{1,0:T(8,128)(2,1)S(1)} collective-permute-done((bf16[256,1024]{1,0:T(8,128)(2,1)S(1)}, bf16[256,1024]{1,0:T(8,128)(2,1)S(1)}, u32[]{:S(2)}, u32[]{:S(2)}) %collective-permute-start.41) | collective-permute-done | bytes 524320 | tf_op jit(solution)/shard_map/ppermute | solution.py:755
  (467 shorter events, 208.1 us)
Async XLA Ops:
  7.2 62.7 %all-gather.4.cloned.1.call-start = ((), (), s32[]{:S(2)}) async-start(), calls=%async_computation | async-start | bytes 5242880 | tf_op jit(solution)/shard_map/all_gather | solution.py:808
  14.4 115.0 %all-gather.6.cloned.1.call-start = ((), (), s32[]{:S(2)}) async-start(), calls=%async_computation.1 | async-start | bytes 5242880 | tf_op jit(solution)/shard_map/all_gather | solution.py:808
  29.3 52.5 %collective-permute-start.2 = (bf16[1024,2320]{0,1:T(8,128)(2,1)}, bf16[1024,2320]{0,1:T(8,128)(2,1)}, u32[]{:S(2)}, u32[]{:S(2)}) collective-permute-start(bf16[1024,2320]{0,1:T(8,128)(2,1)} %pad_maximum_fusion), channel_id=1, source_target_pairs={{0,1},{1,0},{2,3},{3,2},{4,5},{5,4},{6,7},{7,6},{8,9},{9,8},{10,11... | collective-permute-start | bytes 14254088 | tf_op jit(solution)/shard_map/ppermute | solution.py:737
  69.9 245.3 %all-gather.8.cloned.1.call-start = ((), (), s32[]{:S(2)}) async-start(), calls=%async_computation.2 | async-start | bytes 5242880 | tf_op jit(solution)/shard_map/all_gather | solution.py:808
  70.1 40.1 %collective-permute-start.3 = (bf16[1024,1024]{1,0:T(8,128)(2,1)}, bf16[1024,1024]{1,0:T(8,128)(2,1)}, u32[]{:S(2)}, u32[]{:S(2)}) collective-permute-start(bf16[1024,1024]{1,0:T(8,128)(2,1)} %bitcast.345), channel_id=1, source_target_pairs={{0,1},{1,0},{2,3},{3,2},{4,5},{5,4},{6,7},{7,6},{8,9},{9,8},{10,11... | collective-permute-start | bytes 6291464 | tf_op jit(solution)/shard_map/ppermute | solution.py:737
  70.2 99.0 %collective-permute-start.8 = (bf16[2,256,1024]{2,1,0:T(8,128)(2,1)}, bf16[2,256,1024]{2,1,0:T(8,128)(2,1)}, u32[]{:S(2)}, u32[]{:S(2)}) collective-permute-start(bf16[2,256,1024]{2,1,0:T(8,128)(2,1)} %get-tuple-element.105), channel_id=1, source_target_pairs={{0,1},{1,0},{2,3},{3,2},{4,5},{5,4},{6,7},{7,6},{8,9},{9,8},{10,11... | collective-permute-start | bytes 3145736 | tf_op jit(solution)/shard_map/ppermute | solution.py:737
  116.2 31.7 %collective-permute-start.5 = (bf16[2,256,1024]{2,1,0:T(8,128)(2,1)}, bf16[2,256,1024]{2,1,0:T(8,128)(2,1)}, u32[]{:S(2)}, u32[]{:S(2)}) collective-permute-start(bf16[2,256,1024]{2,1,0:T(8,128)(2,1)} %dynamic-slice_bitcast_fusion.6), channel_id=1, source_target_pairs={{0,4},{2,6},{4,0},{6,2},{1,5},{3,7},{5,1},{7,3},{8,12},{10,14},{12... | collective-permute-start | bytes 3145736 | tf_op jit(solution)/shard_map/ppermute | solution.py:578
  121.9 26.9 %collective-permute-start.4 = (bf16[2,272,1024]{2,1,0:T(8,128)(2,1)}, bf16[2,272,1024]{2,1,0:T(8,128)(2,1)}, u32[]{:S(2)}, u32[]{:S(2)}) collective-permute-start(bf16[2,272,1024]{2,1,0:T(8,128)(2,1)} %maximum_maximum_fusion), channel_id=1, source_target_pairs={{0,2},{2,0},{4,6},{6,4},{1,3},{3,1},{5,7},{7,5},{8,10},{10,8},{12,... | collective-permute-start | bytes 3342344 | tf_op jit(solution)/shard_map/ppermute | solution.py:578
  175.7 29.1 %collective-permute-start.10 = (bf16[272,2048]{1,0:T(8,128)(2,1)}, bf16[272,2048]{1,0:T(8,128)(2,1)}, u32[]{:S(2)}, u32[]{:S(2)}) collective-permute-start(bf16[272,2048]{1,0:T(8,128)(2,1)} %pad_maximum_fusion.6), channel_id=1, source_target_pairs={{0,4},{2,6},{4,0},{6,2},{1,5},{3,7},{5,1},{7,3},{8,12},{10,14},{12... | collective-permute-start | bytes 3342344 | tf_op jit(solution)/shard_map/ppermute | solution.py:578
  176.5 28.2 %collective-permute-start.9 = (bf16[272,2048]{1,0:T(8,128)(2,1)}, bf16[272,2048]{1,0:T(8,128)(2,1)}, u32[]{:S(2)}, u32[]{:S(2)}) collective-permute-start(bf16[272,2048]{1,0:T(8,128)(2,1)} %pad_maximum_fusion.6), channel_id=1, source_target_pairs={{0,2},{2,0},{4,6},{6,4},{1,3},{3,1},{5,7},{7,5},{8,10},{10,8},{12,... | collective-permute-start | bytes 3342344 | tf_op jit(solution)/shard_map/ppermute | solution.py:578
  209.3 33.8 %collective-permute-start.14 = (bf16[2,256,1024]{2,1,0:T(8,128)(2,1)S(1)}, bf16[2,256,1024]{2,1,0:T(8,128)(2,1)S(1)}, u32[]{:S(2)}, u32[]{:S(2)}) collective-permute-start(bf16[2,256,1024]{2,1,0:T(8,128)(2,1)S(1)} %dynamic-slice_bitcast_fusion.4), channel_id=1, source_target_pairs={{0,4},{2,6},{4,0},{6,2},{1,5},{3,7},{5,1},{7,3},{8,12},{10,14},{12... | collective-permute-start | bytes 3145736 | tf_op jit(solution)/shard_map/ppermute | solution.py:578
  210.1 32.9 %collective-permute-start.13 = (bf16[2,272,1024]{2,1,0:T(8,128)(2,1)S(1)}, bf16[2,272,1024]{2,1,0:T(8,128)(2,1)S(1)}, u32[]{:S(2)}, u32[]{:S(2)}) collective-permute-start(bf16[2,272,1024]{2,1,0:T(8,128)(2,1)S(1)} %maximum_maximum_fusion.1), channel_id=1, source_target_pairs={{0,2},{2,0},{4,6},{6,4},{1,3},{3,1},{5,7},{7,5},{8,10},{10,8},{12,... | collective-permute-start | bytes 3342344 | tf_op jit(solution)/shard_map/ppermute | solution.py:578
  262.1 159.2 %all-reduce.11.cloned.1.call-start = ((), (), s32[]{:S(2)}) async-start(), calls=%async_computation.3 | async-start | bytes 4194304 | tf_op jit(solution)/shard_map/psum | solution.py:932
  266.7 40.7 %collective-permute-start.21 = (f32[1,1024]{1,0:T(1,128)S(1)}, f32[1,1024]{1,0:T(1,128)S(1)}, u32[]{:S(2)}, u32[]{:S(2)}) collective-permute-start(f32[1,1024]{1,0:T(1,128)S(1)} %get-tuple-element.223), channel_id=1, source_target_pairs={{0,2},{2,0},{4,6},{6,4},{1,3},{3,1},{5,7},{7,5},{8,10},{10,8},{12,... | collective-permute-start | bytes 12296 | tf_op jit(solution)/shard_map/ppermute | solution.py:578
  269.4 42.2 %collective-permute-start.18 = (bf16[256,1024]{1,0:T(8,128)(2,1)S(1)}, bf16[256,1024]{1,0:T(8,128)(2,1)}, u32[]{:S(2)}, u32[]{:S(2)}) collective-permute-start(bf16[256,1024]{1,0:T(8,128)(2,1)S(1)} %get-tuple-element.248), channel_id=1, source_target_pairs={{0,8},{8,16},{16,24},{24,0},{1,9},{9,17},{17,25},{25,1},{2,10},{10... | collective-permute-start | bytes 1572872 | tf_op jit(solution)/shard_map/ppermute | solution.py:755
  270.9 40.7 %collective-permute-start.19 = (bf16[256,1024]{1,0:T(8,128)(2,1)S(1)}, bf16[256,1024]{1,0:T(8,128)(2,1)}, u32[]{:S(2)}, u32[]{:S(2)}) collective-permute-start(bf16[256,1024]{1,0:T(8,128)(2,1)S(1)} %get-tuple-element.249), channel_id=1, source_target_pairs={{0,16},{8,24},{16,0},{24,8},{1,17},{9,25},{17,1},{25,9},{2,18},{10... | collective-permute-start | bytes 1572872 | tf_op jit(solution)/shard_map/ppermute | solution.py:755
  273.3 38.3 %collective-permute-start.20 = (bf16[256,1024]{1,0:T(8,128)(2,1)S(1)}, bf16[256,1024]{1,0:T(8,128)(2,1)}, u32[]{:S(2)}, u32[]{:S(2)}) collective-permute-start(bf16[256,1024]{1,0:T(8,128)(2,1)S(1)} %get-tuple-element.250), channel_id=1, source_target_pairs={{0,24},{8,0},{16,8},{24,16},{1,25},{9,1},{17,9},{25,17},{2,26},{10... | collective-permute-start | bytes 1572872 | tf_op jit(solution)/shard_map/ppermute | solution.py:755
  330.1 295.4 %all-reduce.13.cloned.1.call-start = ((), (), s32[]{:S(2)}) async-start(), calls=%async_computation.4 | async-start | bytes 8388608 | tf_op jit(solution)/shard_map/psum | solution.py:960
  348.9 39.2 %collective-permute-start.26 = (bf16[2,256,1024]{2,1,0:T(8,128)(2,1)S(1)}, bf16[2,256,1024]{2,1,0:T(8,128)(2,1)}, u32[]{:S(2)}, u32[]{:S(2)}) collective-permute-start(bf16[2,256,1024]{2,1,0:T(8,128)(2,1)S(1)} %dynamic-slice_bitcast_fusion.2), channel_id=1, source_target_pairs={{0,4},{2,6},{4,0},{6,2},{1,5},{3,7},{5,1},{7,3},{8,12},{10,14},{12... | collective-permute-start | bytes 3145736 | tf_op jit(solution)/shard_map/ppermute | solution.py:578
  350.4 37.7 %collective-permute-start.25 = (bf16[2,256,1024]{2,1,0:T(8,128)(2,1)S(1)}, bf16[2,256,1024]{2,1,0:T(8,128)(2,1)}, u32[]{:S(2)}, u32[]{:S(2)}) collective-permute-start(bf16[2,256,1024]{2,1,0:T(8,128)(2,1)S(1)} %dynamic-slice_bitcast_fusion.3), channel_id=1, source_target_pairs={{0,2},{2,0},{4,6},{6,4},{1,3},{3,1},{5,7},{7,5},{8,10},{10,8},{12,... | collective-permute-start | bytes 3145736 | tf_op jit(solution)/shard_map/ppermute | solution.py:578
  390.7 29.8 %collective-permute-start.28 = (bf16[256,1024]{1,0:T(8,128)(2,1)S(1)}, bf16[256,1024]{1,0:T(8,128)(2,1)S(1)}, u32[]{:S(2)}, u32[]{:S(2)}) collective-permute-start(bf16[256,1024]{1,0:T(8,128)(2,1)S(1)} %fusion.36), channel_id=1, source_target_pairs={{0,2},{2,0},{4,6},{6,4},{1,3},{3,1},{5,7},{7,5},{8,10},{10,8},{12,... | collective-permute-start | bytes 1572872 | tf_op jit(solution)/shard_map/ppermute | solution.py:578
  392.2 29.1 %collective-permute-start.27 = (bf16[256,1024]{1,0:T(8,128)(2,1)S(1)}, bf16[256,1024]{1,0:T(8,128)(2,1)}, u32[]{:S(2)}, u32[]{:S(2)}) collective-permute-start(bf16[256,1024]{1,0:T(8,128)(2,1)S(1)} %fusion.37), channel_id=1, source_target_pairs={{0,4},{2,6},{4,0},{6,2},{1,5},{3,7},{5,1},{7,3},{8,12},{10,14},{12... | collective-permute-start | bytes 1572872 | tf_op jit(solution)/shard_map/ppermute | solution.py:578
  426.2 29.0 %collective-permute-start.30 = (bf16[2,256,1024]{2,1,0:T(8,128)(2,1)}, bf16[2,256,1024]{2,1,0:T(8,128)(2,1)}, u32[]{:S(2)}, u32[]{:S(2)}) collective-permute-start(bf16[2,256,1024]{2,1,0:T(8,128)(2,1)} %dynamic-slice_bitcast_fusion.1), channel_id=1, source_target_pairs={{0,2},{2,0},{4,6},{6,4},{1,3},{3,1},{5,7},{7,5},{8,10},{10,8},{12,... | collective-permute-start | bytes 3145736 | tf_op jit(solution)/shard_map/ppermute | solution.py:578
  428.7 26.5 %collective-permute-start.31 = (bf16[2,256,1024]{2,1,0:T(8,128)(2,1)}, bf16[2,256,1024]{2,1,0:T(8,128)(2,1)}, u32[]{:S(2)}, u32[]{:S(2)}) collective-permute-start(bf16[2,256,1024]{2,1,0:T(8,128)(2,1)} %dynamic-slice_bitcast_fusion), channel_id=1, source_target_pairs={{0,4},{2,6},{4,0},{6,2},{1,5},{3,7},{5,1},{7,3},{8,12},{10,14},{12... | collective-permute-start | bytes 3145736 | tf_op jit(solution)/shard_map/ppermute | solution.py:578
  509.6 29.6 %collective-permute-start.46 = (f32[256,320]{0,1:T(8,128)S(1)}, f32[256,320]{0,1:T(8,128)S(1)}, u32[]{:S(2)}, u32[]{:S(2)}) collective-permute-start(f32[256,320]{0,1:T(8,128)S(1)} %dynamic-slice_add_fusion), channel_id=1, source_target_pairs={{0,8},{8,0},{16,24},{24,16},{1,9},{9,1},{17,25},{25,17},{2,10},{10... | collective-permute-start | bytes 983048 | tf_op jit(solution)/shard_map/ppermute | solution.py:707
  513.9 26.2 %collective-permute-start.37 = (f32[11297]{0:T(1024)S(1)}, f32[11297]{0:T(1024)S(1)}, u32[]{:S(2)}, u32[]{:S(2)}) collective-permute-start(f32[11297]{0:T(1024)S(1)} %pad_maximum_fusion.16), channel_id=1, source_target_pairs={{0,8},{8,0},{16,24},{24,16},{1,9},{9,1},{17,25},{25,17},{2,10},{10... | collective-permute-start | bytes 135572 | tf_op jit(solution)/shard_map/ppermute | solution.py:707
  515.0 71.6 %collective-permute-start.39 = (bf16[2,256,1024]{2,1,0:T(8,128)(2,1)}, bf16[2,256,1024]{2,1,0:T(8,128)(2,1)}, u32[]{:S(2)}, u32[]{:S(2)}) collective-permute-start(bf16[2,256,1024]{2,1,0:T(8,128)(2,1)} %pad_maximum_fusion.12), channel_id=1, source_target_pairs={{0,1},{1,0},{2,3},{3,2},{4,5},{5,4},{6,7},{7,6},{8,9},{9,8},{10,11... | collective-permute-start | bytes 3145736 | tf_op jit(solution)/shard_map/ppermute | solution.py:737
  539.2 37.7 %collective-permute-start.47 = (f32[256,320]{0,1:T(8,128)S(1)}, f32[256,320]{0,1:T(8,128)S(1)}, u32[]{:S(2)}, u32[]{:S(2)}) collective-permute-start(f32[256,320]{0,1:T(8,128)S(1)} %add.767), channel_id=1, source_target_pairs={{0,16},{8,24},{16,0},{24,8},{1,17},{9,25},{17,1},{25,9},{2,18},{10... | collective-permute-start | bytes 983048 | tf_op jit(solution)/shard_map/ppermute | solution.py:707
  540.2 34.5 %collective-permute-start.38 = (f32[11297]{0:T(1024)S(1)}, f32[11297]{0:T(1024)S(1)}, u32[]{:S(2)}, u32[]{:S(2)}) collective-permute-start(f32[11297]{0:T(1024)S(1)} %fusion.190), channel_id=1, source_target_pairs={{0,16},{8,24},{16,0},{24,8},{1,17},{9,25},{17,1},{25,9},{2,18},{10... | collective-permute-start | bytes 135572 | tf_op jit(solution)/shard_map/ppermute | solution.py:707
  625.7 27.0 %collective-permute-start.40 = (bf16[256,1024]{1,0:T(8,128)(2,1)S(1)}, bf16[256,1024]{1,0:T(8,128)(2,1)S(1)}, u32[]{:S(2)}, u32[]{:S(2)}) collective-permute-start(bf16[256,1024]{1,0:T(8,128)(2,1)S(1)} %get-tuple-element.241), channel_id=1, source_target_pairs={{0,24},{8,0},{16,8},{24,16},{1,25},{9,1},{17,9},{25,17},{2,26},{10... | collective-permute-start | bytes 1572872 | tf_op jit(solution)/shard_map/ppermute | solution.py:755
  627.8 24.9 %collective-permute-start.42 = (bf16[256,1024]{1,0:T(8,128)(2,1)S(1)}, bf16[256,1024]{1,0:T(8,128)(2,1)S(1)}, u32[]{:S(2)}, u32[]{:S(2)}) collective-permute-start(bf16[256,1024]{1,0:T(8,128)(2,1)S(1)} %get-tuple-element.243), channel_id=1, source_target_pairs={{0,8},{8,16},{16,24},{24,0},{1,9},{9,17},{17,25},{25,1},{2,10},{10... | collective-permute-start | bytes 1572872 | tf_op jit(solution)/shard_map/ppermute | solution.py:755
  628.1 43.7 %collective-permute-start.41 = (bf16[256,1024]{1,0:T(8,128)(2,1)S(1)}, bf16[256,1024]{1,0:T(8,128)(2,1)S(1)}, u32[]{:S(2)}, u32[]{:S(2)}) collective-permute-start(bf16[256,1024]{1,0:T(8,128)(2,1)S(1)} %get-tuple-element.244), channel_id=1, source_target_pairs={{0,16},{8,24},{16,0},{24,8},{1,17},{9,25},{17,1},{25,9},{2,18},{10... | collective-permute-start | bytes 1572872 | tf_op jit(solution)/shard_map/ppermute | solution.py:755
  (108 other events, 1249.7 us)
Sparse Core Ops, SparseCore 0:
  14.5 55.3 all-gather.3
  71.7 57.6 all-gather.5
  262.3 52.8 all-gather.7
  330.2 88.2 all-reduce.10
  455.4 170.0 all-reduce.12
